TPU v7x, 32 devices: a whole 2x2x4 slice. The times are simulated.
32 devices in a mesh: groups: 2 (over y), blk: 4 (over z), win: 4 (over x, core).
Axes of the slice: x: 2, y: 2, z: 4, core: 2. Of those that a mesh axis runs over, the one named last changes fastest.
Arguments:
- spectra: bfloat16 [2, 24, 1024, 201], P(None, 'win', ('groups', 'blk')), parts along dimension 2
- channel_slot: int32 [1024], P(('groups', 'blk')), parts along dimension 0, may hold values from 0 to 511, as said below
- partners: int32 [2, 4], replicated, may hold values from 0 to 3, as said below
Outputs:
- correlations: bfloat16 [2, 1024, 101, 128], P(None, ('groups', 'blk', 'win')), parts along dimension 1
There are 2 independent parts, one for each index of `groups`. A program takes and returns all parts, laid end to end along the dimension named above; an argument that names none is the same for every part. Nothing has to cross between parts.
Inputs may be any that keep to these rules, and one draw needn't show every extreme that they name: channel_slot is a permutation of 0 to 511. For every acquisition shard s (channels s * 128 to s * 128 + 127) and every block b, exactly 32 of the shard's channels go to block b, and they take the slots b * 128 + s * 32 + q for q from 0 to 31. In round r, partners[r, i] = i XOR m_r for one value m_r of 1 to 3 per round; the rounds' values differ.
All inputs are finite; a program needn't handle non-finite values.
Results may differ from a plain program's by a relative error of at most 0.0057.
Values may be sent and summed in bfloat16 or wider, within the bound.
No kernel may reach another device: no remote copies, remote signals or barrier semaphores. Data moves between devices by JAX's collectives and lax.ppermute only.
A program may use at most 128 MiB of HBM per device.

v0:
```python
import math

import jax
import jax.numpy as jnp
import numpy as np
from jax import lax
from jax.experimental import pallas as pl
from jax.experimental.pallas import tpu as pltpu
from jax.sharding import PartitionSpec as P

L = 101
ROUNDS = 2

eps_power = 1e-06
half_band = 2
tile_rows = 8
LANES = 128
K8 = 8
K16 = 16
VMEM_BYTES = 56 * 1024 * 1024


def shortened(value):

    def short(part):
        return part.astype(jnp.bfloat16) if part.dtype == jnp.float32 else part

    return jax.tree.map(short, value)


def partner(value, axis, distance):
    mask = 2**distance
    pairs = [(source, source ^ mask) for source in range(lax.axis_size(axis))]
    return lax.ppermute(value, axis, pairs)


def band_mean(power, windows):
    nbins = power.shape[1]
    padded = jnp.pad(power, ((0, 0), (half_band, half_band)))
    ones = jnp.pad(jnp.ones((nbins,), jnp.float32), (half_band, half_band))
    total = padded[:, 0:nbins]
    count = ones[0:nbins]
    for offset in range(1, 2 * half_band + 1):
        total = total + padded[:, offset : offset + nbins]
        count = count + ones[offset : offset + nbins]
    return total / (count * windows)


def power_of(parts):
    value_array = parts.astype(jnp.float32)
    return jnp.sum(value_array * value_array, axis=(0, 1))


def whiten(parts, power, windows):
    scale = lax.rsqrt(band_mean(power, windows) + eps_power)
    return (parts.astype(jnp.float32) * scale).astype(jnp.bfloat16)


def lag_table(nbins, nlags, windows):
    samples = 2 * (nbins - 1)
    freq = jnp.arange(nbins, dtype=jnp.int32)
    lags = jnp.arange(nlags, dtype=jnp.int32) - (nlags - 1) // 2
    phase_index = freq[:, None] * lags[None, :] % samples
    angle = 2.0 * math.pi / samples * phase_index.astype(jnp.float32)
    weight = jnp.where((freq == 0) | (freq == nbins - 1), 1.0, 2.0).astype(jnp.float32)
    norm = 1.0 / math.sqrt(windows * samples)
    cos_part = weight[:, None] * jnp.cos(angle) * norm
    sin_part = -weight[:, None] * jnp.sin(angle) * norm
    return jnp.concatenate([cos_part, sin_part], axis=0)


def correlate(sources, receivers, table):
    left = jnp.concatenate([sources[0], sources[1]], axis=0)
    turned = jnp.concatenate([sources[1], -sources[0]], axis=0)
    right = jnp.concatenate([receivers[0], receivers[1]], axis=0)
    count = left.shape[1] // tile_rows

    def one_tile(index):
        start = index * tile_rows
        part_left = lax.dynamic_slice_in_dim(left, start, tile_rows, 1)
        part_turned = lax.dynamic_slice_in_dim(turned, start, tile_rows, 1)
        real = jnp.einsum("wak,wbk->kab", part_left, right, preferred_element_type=jnp.float32)
        imag = jnp.einsum("wak,wbk->kab", part_turned, right, preferred_element_type=jnp.float32)
        stacked = jnp.concatenate([real, imag], axis=0)
        return jnp.einsum("kab,kl->alb", stacked, table, precision=lax.Precision.HIGHEST)

    result = lax.map(one_tile, jnp.arange(count, dtype=jnp.int32))
    return result.reshape(count * tile_rows, table.shape[1], right.shape[1]).astype(jnp.bfloat16)


def make_walker(mask_bits, depth):

    def walker(moving):
        for bit in range(depth):
            if mask_bits >> bit & 1:
                moving = jax.tree.map(
                    lambda part, own: part.astype(own.dtype),
                    partner(shortened(moving), "blk", bit),
                    moving,
                )
        return moving

    return walker


def walking_body(spectra, channel_slot, partners):
    n_blk = lax.axis_size("blk")
    n_win = lax.axis_size("win")
    chans = spectra.shape[2]
    nbins = spectra.shape[3]
    per_peer = chans // n_blk
    here = lax.axis_index("blk")
    target = channel_slot // chans * per_peer + channel_slot % chans - here * per_peer
    selector = (jnp.arange(chans, dtype=jnp.int32)[:, None] == target[None, :]).astype(jnp.bfloat16)
    ordered = jnp.einsum(
        "pc,rwcf->rwpf", selector, spectra, preferred_element_type=jnp.float32
    ).astype(jnp.bfloat16)
    blocked = lax.all_to_all(ordered, "blk", split_axis=2, concat_axis=2, tiled=True)
    windows = spectra.shape[1] * n_win
    power = lax.psum(power_of(blocked), "win")
    outgoing = whiten(blocked, power, windows)
    own_all = lax.all_gather(outgoing, "win", axis=1, tiled=True)
    share = chans // n_win
    sources = lax.dynamic_slice_in_dim(own_all, lax.axis_index("win") * share, share, 2)
    table = lag_table(nbins, L, windows)
    masks = jnp.bitwise_xor(partners[:, here], here)
    bits = n_blk.bit_length() - 1
    results = []
    walkers = [make_walker(mask_bits, bits) for mask_bits in range(1, n_blk)]
    for round_index in range(ROUNDS):
        moving = lax.switch(masks[round_index] - 1, walkers, outgoing)
        partner_all = jax.tree.map(
            lambda part, own: part.astype(own.dtype),
            lax.all_gather(shortened(moving), "win", axis=1, tiled=True),
            moving,
        )
        results.append(correlate(sources, partner_all, table))
    return jnp.stack(results, axis=0)


def iota(shape, dim):
    return lax.broadcasted_iota(jnp.int32, shape, dim)


def bins_of(nbins):
    return -(-nbins // K16)


def lag_matrix(nbins, windows):
    samples = 2 * (nbins - 1)
    groups = 2 * bins_of(nbins)
    rows = -(-L // K8) * K8
    freq = np.arange(nbins)
    lags = np.arange(L) - (L - 1) // 2
    angle = 2.0 * np.pi / samples * (freq[:, None] * lags[None, :] % samples)
    weight = np.where((freq == 0) | (freq == nbins - 1), 1.0, 2.0)[:, None] / math.sqrt(windows * samples)
    full = np.zeros((rows, 2, groups * K8))
    full[:L, 0, :nbins] = (weight * np.cos(angle)).T
    full[:L, 1, :nbins] = -(weight * np.sin(angle)).T
    full = full.reshape(rows, 2, groups, K8).transpose(0, 2, 1, 3).reshape(rows, groups * 2 * K8)
    high = full.astype(jnp.bfloat16)
    low = (full - high.astype(np.float64)).astype(jnp.bfloat16)
    return np.concatenate([high, low], axis=0)


def pack_kernel(layout, nbins, here_ref, part_ref, slot_ref, x_ref, *rest):
    outs, (wide_ref, blocks_ref) = rest[: len(layout)], rest[len(layout) :]
    n_blk, n_grp, n_row, lanes = blocks_ref.shape
    per_peer = lanes // 4
    chans = slot_ref.shape[1]
    pairs = n_row // K16
    here = here_ref[0]
    slot = slot_ref[...]
    target = slot // chans * per_peer + slot % chans - here * per_peer
    target = jnp.concatenate([target] * 4, axis=1)
    wide_ref[...] = jnp.zeros(wide_ref.shape, jnp.float32)
    shape = (lanes, 4 * chans)
    row, col = iota(shape, 0), iota(shape, 1)
    same = row // per_peer == col // chans
    for block in range(n_blk):
        pick = jnp.where(same & (target == block * per_peer + row % per_peer), 1.0, 0.0).astype(jnp.bfloat16)
        for pair in range(pairs):
            part = jnp.concatenate([x_ref[p, pl.ds(pair * 2 * chans, 2 * chans), :] for p in range(2)], axis=0)
            wide_ref[:, pl.ds(0, nbins)] = jnp.dot(pick, part, preferred_element_type=jnp.float32)
            turned = wide_ref[...].T[: n_grp * K16].astype(jnp.bfloat16)
            blocks_ref[block, :, pl.ds(pair * K16, K16), :] = turned.reshape(n_grp, K16, lanes)
    masks = [part_ref[r, here] ^ here for r in range(ROUNDS)]
    masks.append(masks[0] ^ masks[1])
    for out, message in zip(outs, layout):
        for place, (step, name) in enumerate(message):
            mask = 0 if name is None else masks[name]
            out[place] = blocks_ref[here ^ step ^ mask]


def scale_of(power_ref, nbins, windows):
    rows = power_ref.shape[0] - 2 * K8
    total = power_ref[pl.ds(K8 - half_band, rows), :]
    for offset in range(1, 2 * half_band + 1):
        total = total + power_ref[pl.ds(K8 - half_band + offset, rows), :]
    bin_ = iota(total.shape, 0)
    count = jnp.minimum(bin_ + half_band, nbins - 1) - jnp.maximum(bin_ - half_band, 0) + 1
    count = jnp.maximum(count, 1).astype(jnp.float32)
    return lax.rsqrt(total / (count * windows) + eps_power)


def source_kernel(nbins, windows, *refs):
    src, (out_ref, power_ref, scale_ref) = refs[:4], refs[4:]
    n_grp, n_row, lanes = src[0].shape[1:]
    pairs = n_row // K16
    share = lanes // 4
    step = pl.program_id(0)

    @pl.when(step == 0)
    def _():
        total = jnp.zeros((n_grp, K16, lanes), jnp.float32)
        for ref in src:
            for pair in range(pairs):
                value = ref[0, :, pl.ds(pair * K16, K16), :].astype(jnp.float32)
                total = total + value * value
        total = total.reshape(n_grp * K16, lanes)
        total = total + pltpu.roll(total, 2 * share, 1)
        total = total + pltpu.roll(total, share, 1)
        power_ref[...] = jnp.zeros(power_ref.shape, jnp.float32)
        power_ref[pl.ds(K8, n_grp * K16), :] = total
        scale_ref[...] = scale_of(power_ref, nbins, windows).reshape(scale_ref.shape)

    scale = scale_ref[step]
    white = [
        [
            (ref[0, step, pl.ds(pair * K16, K16), :].astype(jnp.float32) * scale).astype(jnp.bfloat16).astype(jnp.float32)
            for ref in src
        ]
        for pair in range(pairs)
    ]
    lane_group = iota((share, lanes), 1) // (4 * K8)
    keep = iota((share, K8, lanes), 1) == iota((share, K8, lanes), 2) % K8
    for half in range(2):
        rows = [white[pair][e][half * K8 : (half + 1) * K8] for pair in range(pairs) for e in range(4)]
        rows = rows + [jnp.zeros((lanes - len(rows) * K8, lanes), jnp.float32)]
        turned = jnp.concatenate(rows, axis=0).T
        by_group = [turned[g * share : (g + 1) * share] for g in range(4)]
        crossed = [by_group[2], by_group[3], -by_group[0], -by_group[1]]
        for pair in range(pairs):
            spread = []
            for values in (by_group, crossed):
                line = jnp.zeros((share, lanes), jnp.float32)
                for g in range(4):
                    moved = values[g]
                    shift = (g - pair) * 4 * K8 % lanes
                    if shift:
                        moved = pltpu.roll(moved, shift, 1)
                    line = jnp.where(lane_group == g, moved, line)
                line = jnp.broadcast_to(line.reshape(share, 1, lanes), (share, K8, lanes))
                spread.append(jnp.where(keep, line, 0.0))
            both = jnp.concatenate(spread, axis=1).astype(jnp.bfloat16)
            out_ref[half, :, pl.ds(pair * lanes, lanes)] = both.reshape(share * 2 * K8, lanes)


def correlate_kernel(places, nbins, windows, here_ref, left_hbm, lag_ref, *rest):
    count = 1 + max(index for by_d in places for by_e in by_d for index, _ in by_e)
    pieces, rest = rest[:count], rest[count:]
    out_ref, left_ref, right_ref, cross_ref, power_ref, scale_ref, sem = rest
    copy = pltpu.make_async_copy(left_hbm, left_ref, sem)
    copy.start()
    n_grp, n_row, lanes = pieces[0].shape[1:]
    pairs = n_row // K16
    share = lanes // 4
    here = here_ref[0]
    shape = (4 * lanes, 4 * lanes)
    row, col = iota(shape, 0), iota(shape, 1)
    shard = (row // lanes) ^ here
    spot = row % lanes // share * lanes + shard * share + row % share
    order = jnp.where(col == spot, 1.0, 0.0).astype(jnp.bfloat16)
    power_ref[...] = jnp.zeros(power_ref.shape, jnp.float32)
    for r in range(ROUNDS):
        side = pl.ds(r * lanes, lanes)
        total = jnp.zeros((n_grp, 2, K8, lanes), jnp.float32)
        for e in range(4):
            parts = [pieces[places[r][d][e][0]][places[r][d][e][1]].reshape(n_grp * n_row, lanes) for d in range(4)]
            moved = jnp.dot(jnp.concatenate(parts, axis=1), order, preferred_element_type=jnp.float32)
            moved = moved.reshape(n_grp, pairs, 2, K8, 4 * lanes)
            for pair in range(pairs):
                for g in range(4):
                    value = moved[:, pair, :, :, g * lanes : (g + 1) * lanes]
                    right_ref[:, :, (pair * 4 + g) * 4 + e, :, side] = value
                    total = total + value * value
        power_ref[pl.ds(K8, n_grp * K16), side] = total.reshape(n_grp * K16, lanes)
    scale_ref[...] = scale_of(power_ref, nbins, windows).reshape(scale_ref.shape)
    copy.wait()

    def one_group(index, carry):
        for half in range(2):
            white = (right_ref[index, half] * scale_ref[index, half]).astype(jnp.bfloat16)
            white = white.reshape(-1, white.shape[-1])
            cross = jnp.dot(left_ref[2 * index + half], white, preferred_element_type=jnp.float32)
            place = pl.multiple_of((2 * index + half) * 2 * K8, 2 * K8)
            cross_ref[:, pl.ds(place, 2 * K8), :] = cross.astype(jnp.bfloat16).reshape(-1, 2 * K8, cross.shape[-1])
        return carry

    lax.fori_loop(0, n_grp, one_group, 0)

    def one_source(index, carry):
        both = jnp.dot(lag_ref[...], cross_ref[index], preferred_element_type=jnp.float32)
        rows = both.shape[0] // 2
        lagged = (both[:rows] + both[rows:])[:L].astype(jnp.bfloat16)
        for r in range(ROUNDS):
            out_ref[r, index] = lagged[:, r * lanes : (r + 1) * lanes]
        return carry

    lax.fori_loop(0, share, one_source, 0)


def swap(value, axis, mask):
    return lax.ppermute(value, axis, [(i, i ^ mask) for i in range(lax.axis_size(axis))])


def call(kernel, outs, operands, scratch, name, specs=None, **grid):
    return pl.pallas_call(
        kernel,
        out_shape=outs,
        in_specs=specs,
        scratch_shapes=scratch,
        compiler_params=pltpu.CompilerParams(vmem_limit_bytes=VMEM_BYTES),
        name=name,
        **grid,
    )(*operands)


def make_branch(case):
    near, far = (case, 1 - case) if case < 2 else (None, None)

    def branch(spectra, channel_slot, partners, here):
        chans, nbins = spectra.shape[2:]
        windows = spectra.shape[1] * lax.axis_size("win")
        n_grp = bins_of(nbins)
        pairs = spectra.shape[1] // 2
        share = chans // 4
        piece = (n_grp, pairs * K16, chans)
        win = lax.axis_index("win")
        if case < 2:
            far_first = [[(2, near)], [(2, None)], [(2, 2)], [(2, far)]]
        else:
            far_first = [[(2, 0), (2, 1)], [(3, None)], [(2, None)]]
        layout = far_first + [[(1, 0), (1, 1)], [(1, None)], [(0, 0), (0, 1)], [(0, None)]]
        vmem, smem = pl.BlockSpec(memory_space=pltpu.VMEM), pl.BlockSpec(memory_space=pltpu.SMEM)
        messages = call(
            lambda *refs: pack_kernel(layout, nbins, *refs),
            [jax.ShapeDtypeStruct((len(m),) + piece, jnp.bfloat16) for m in layout],
            (here, partners, channel_slot.reshape(1, chans), spectra.reshape(2, -1, nbins)),
            [pltpu.VMEM((chans, 2 * LANES), jnp.float32), pltpu.VMEM((4,) + piece, jnp.bfloat16)],
            "pack",
            [smem, smem, vmem, vmem],
        )
        far_sent, (near_sent, near_src, own, own_src) = messages[:-4], messages[-4:]
        far_got = [swap(m, "blk", 2) for m in far_sent]
        near_got = swap(near_sent, "blk", 1)
        near_src_got = swap(near_src, "blk", 1)
        if case < 2:
            relayed = [swap(far_got[i], "blk", 1) for i in (1, 0, 2)]
            src = [own_src, near_src_got, far_got[1], relayed[1]]
            held = {(far, 2): (far_got[3], 0), (near, 2): (far_got[0], 0)}
            held |= {(far, 3): (relayed[2], 0), (near, 3): (relayed[0], 0)}
        else:
            relayed = [swap(far_got[i], "blk", 1) for i in (0, 1)]
            src = [own_src, near_src_got, far_got[2], relayed[1]]
            held = {(r, 2): (far_got[0], r) for r in range(2)} | {(r, 3): (relayed[0], 1 - r) for r in range(2)}
        held |= {(r, 0): (own, r) for r in range(2)} | {(r, 1): (near_got, r) for r in range(2)}
        z = here[0]
        mine = (z >> 1) == (win >> 1)
        low = [jnp.where(mine, src[d], src[d + 2]) for d in range(2)]
        high = [jnp.where(mine, src[d + 2], src[d]) for d in range(2)]
        odd = ((win ^ z) & 1) == 1
        across = swap(jnp.concatenate(high, axis=0), "win", 2)
        first, second = low, [across[0:1], across[1:2]]
        sources = []
        for two in (first, second):
            sources.append(jnp.where(odd, two[1], two[0]))
            sources.append(swap(jnp.where(odd, two[0], two[1]), "win", 1))
        left = call(
            lambda *refs: source_kernel(nbins, windows, *refs),
            jax.ShapeDtypeStruct((2 * n_grp, share * 2 * K8, pairs * chans), jnp.bfloat16),
            sources,
            [
                pltpu.VMEM((n_grp * K16 + 2 * K8, chans), jnp.float32),
                pltpu.VMEM((n_grp, K16, chans), jnp.float32),
            ],
            "sources",
            [vmem] * 4,
            grid=(n_grp,),
            out_specs=pl.BlockSpec((2, share * 2 * K8, pairs * chans), lambda i: (i, 0, 0)),
        )
        pieces, places = [], [[[None] * 4 for _ in range(4)] for _ in range(ROUNDS)]
        gathered = {}
        for r in range(ROUNDS):
            for d in range(4):
                array, index = held[r, d]
                if id(array) not in gathered:
                    over = swap(array, "win", 2)
                    gathered[id(array)] = (len(pieces), array)
                    pieces += [array, swap(array, "win", 1), over, swap(over, "win", 1)]
                for e in range(4):
                    places[r][d][e] = (gathered[id(array)][0] + e, index)
        lag = jnp.asarray(lag_matrix(nbins, windows))
        return call(
            lambda *refs: correlate_kernel(places, nbins, windows, *refs),
            jax.ShapeDtypeStruct((ROUNDS, share, L, chans), jnp.bfloat16),
            (here, left, lag, *pieces),
            [
                pltpu.VMEM(left.shape, jnp.bfloat16),
                pltpu.VMEM((n_grp, 2, pairs * 16, K8, ROUNDS * chans), jnp.float32),
                pltpu.VMEM((share, n_grp * 4 * K8, ROUNDS * chans), jnp.bfloat16),
                pltpu.VMEM((n_grp * K16 + 2 * K8, ROUNDS * chans), jnp.float32),
                pltpu.VMEM((n_grp, 2, K8, ROUNDS * chans), jnp.float32),
                pltpu.SemaphoreType.DMA,
            ],
            "correlate",
            [smem, pl.BlockSpec(memory_space=pl.ANY)] + [vmem] * (1 + len(pieces)),
        )

    return branch


def gathering_body(spectra, channel_slot, partners):
    here = lax.axis_index("blk")
    masks = partners[:, here] ^ here
    case = jnp.where(masks[0] == 1, 0, jnp.where(masks[1] == 1, 1, 2))
    branches = [make_branch(i) for i in range(3)]
    return lax.switch(case, branches, spectra, channel_slot, partners, here.reshape(1))


def solution(mesh):
    in_specs = (P(None, "win", ("groups", "blk"), None), P(("groups", "blk")), P())
    out_specs = P(None, ("groups", "blk", "win"), None, None)

    def body(spectra, channel_slot, partners):
        small = all((mesh.shape[axis] - 1).bit_length() == 2 for axis in ("blk", "win"))
        small = small and spectra.shape[2] == LANES and spectra.shape[1] % 2 == 0 and spectra.shape[3] <= 2 * LANES
        return (gathering_body if small else walking_body)(spectra, channel_slot, partners)

    return jax.shard_map(body, mesh=mesh, in_specs=in_specs, out_specs=out_specs, check_vma=False)
```

profile of v0, /device:TPU:0, one launch (start us, length us, event | category | flops | bytes accessed | tf_op | source)
XLA Modules:
  0.0 114.9 jit_solution(12874584345507747911)
XLA Ops:
  0.0 0.8 dynamic-slice_xor_fusion
  0.8 0.5 fusion
  2.5 111.2 %conditional.1 = (bf16[2,32,101,128]{3,1,2,0:T(8,128)(2,1)S(1)}) conditional(s32[]{:T(128)} %bitcast.9, (s32[]{:T(128)}, s32[128]{0:T(128)}, bf16[2,6,128,201]{2,0,3,1:T(2,128)(2,1)}, s32[]{:T(128)}, s32[2,4]{1,0:T(2,128)}, /*index=5*/()) %tuple.14, (s32[]{:T(128)}, s32[128]{0:T(128)}, bf16[2,6,128,201]{2,0,3,1:T(2,128)(2,1)}, ...), branch_computations={%region_0.1_spmd, %region_1.2_spmd, %region_2.3_spmd} | conditional | flops 798728 | bytes 51830732 | solution.py:428
  2.7 3.0 %copy.20 = bf16[2,6,128,201]{3,2,1,0:T(8,128)(2,1)} copy(bf16[2,6,128,201]{2,0,3,1:T(2,128)(2,1)} %get-tuple-element.116) | data formatting | bytes 1234944 | tf_op jit(solution)/shard_map
  5.7 3.1 %pack.4 = (bf16[1,13,48,128]{3,2,1,0:T(8,128)(2,1)}, bf16[1,13,48,128]{3,2,1,0:T(8,128)(2,1)}, bf16[1,13,48,128]{3,2,1,0:T(8,128)(2,1)}, bf16[1,13,48,128]{3,2,1...) custom-call(s32[1]{0:T(128)} %bitcast.3.refs_0_, ...), custom_call_target="tpu_custom_call" | custom-call | tf_op jit(solution)/shard_map/cond/branch_1_fun/pack/pallas_call | solution.py:318
  8.8 4.0 %collective-permute-start.31 = (bf16[1,13,48,128]{3,2,1,0:T(8,128)(2,1)}, bf16[1,13,48,128]{3,2,1,0:T(8,128)(2,1)S(1)}, u32[]{:S(2)}, u32[]{:S(2)}) collective-permute-start(bf16[1,13,48,128]{3,2,1,0:T(8,128)(2,1)} %get-tuple-element.65), channel_id=1, source_target_pairs={{0,8},{4,12},{8,0},{12,4},{1,9},{5,13},{9,1},{13,5},{2,10},{6,14},... | collective-permute-start | bytes 479240 | tf_op jit(solution)/shard_map/cond/branch_1_fun/ppermute | solution.py:314
  12.8 1.6 %collective-permute-start.30 = (bf16[1,13,48,128]{3,2,1,0:T(8,128)(2,1)}, bf16[1,13,48,128]{3,2,1,0:T(8,128)(2,1)S(1)}, u32[]{:S(2)}, u32[]{:S(2)}) collective-permute-start(bf16[1,13,48,128]{3,2,1,0:T(8,128)(2,1)} %get-tuple-element.64), channel_id=1, source_target_pairs={{0,4},{4,0},{8,12},{12,8},{1,5},{5,1},{9,13},{13,9},{2,6},{6,2},{1... | collective-permute-start | bytes 479240 | tf_op jit(solution)/shard_map/cond/branch_1_fun/ppermute | solution.py:314
  14.4 0.3 collective-permute-start.33
  14.7 2.6 %collective-permute-start.44 = (bf16[1,13,48,128]{3,2,1,0:T(8,128)(2,1)}, bf16[1,13,48,128]{3,2,1,0:T(8,128)(2,1)S(1)}, u32[]{:S(2)}, u32[]{:S(2)}) collective-permute-start(bf16[1,13,48,128]{3,2,1,0:T(8,128)(2,1)} %get-tuple-element.71), channel_id=1, source_target_pairs={{0,8},{4,12},{8,0},{12,4},{1,9},{5,13},{9,1},{13,5},{2,10},{6,14},... | collective-permute-start | bytes 479240 | tf_op jit(solution)/shard_map/cond/branch_1_fun/ppermute | solution.py:314
  17.3 0.3 collective-permute-start.48
  17.7 4.6 %collective-permute-done.31.refs_19_ = bf16[1,13,48,128]{3,2,1,0:T(8,128)(2,1)S(1)} collective-permute-done((bf16[1,13,48,128]{3,2,1,0:T(8,128)(2,1)}, bf16[1,13,48,128]{3,2,1,0:T(8,128)(2,1)S(1)}, u32[]{:S(2)}, u32[]{:S(2)}) %collective-permute-start.31) | collective-permute-done | bytes 159776 | tf_op jit(solution)/shard_map/cond/branch_1_fun/ppermute | solution.py:314
  22.3 10.2 %collective-permute-start.54 = (bf16[1,13,48,128]{3,2,1,0:T(8,128)(2,1)S(1)}, bf16[1,13,48,128]{3,2,1,0:T(8,128)(2,1)S(1)}, u32[]{:S(2)}, u32[]{:S(2)}) collective-permute-start(bf16[1,13,48,128]{3,2,1,0:T(8,128)(2,1)S(1)} %collective-permute-done.31.refs_19_), channel_id=1, source_target_pairs={{0,2},{1,3},{2,0},{3,1},{4,6},{5,7},{6,4},{7,5},{8,10},{9,11},{10,... | collective-permute-start | bytes 479240 | tf_op jit(solution)/shard_map/cond/branch_1_fun/ppermute | solution.py:314
  32.5 0.0 collective-permute-done.30
  32.5 2.6 %collective-permute-done.33 = bf16[1,13,48,128]{3,2,1,0:T(8,128)(2,1)S(1)} collective-permute-done((bf16[1,13,48,128]{3,2,1,0:T(8,128)(2,1)}, bf16[1,13,48,128]{3,2,1,0:T(8,128)(2,1)S(1)}, u32[]{:S(2)}, u32[]{:S(2)}) %collective-permute-start.33) | collective-permute-done | bytes 159776 | tf_op jit(solution)/shard_map/cond/branch_1_fun/ppermute | solution.py:314
  35.1 0.0 collective-permute-start.40
  35.2 3.5 %collective-permute-done.44.refs_11_ = bf16[1,13,48,128]{3,2,1,0:T(8,128)(2,1)S(1)} collective-permute-done((bf16[1,13,48,128]{3,2,1,0:T(8,128)(2,1)}, bf16[1,13,48,128]{3,2,1,0:T(8,128)(2,1)S(1)}, u32[]{:S(2)}, u32[]{:S(2)}) %collective-permute-start.44) | collective-permute-done | bytes 159776 | tf_op jit(solution)/shard_map/cond/branch_1_fun/ppermute | solution.py:314
  38.7 2.6 %collective-permute-done.48 = bf16[1,13,48,128]{3,2,1,0:T(8,128)(2,1)S(1)} collective-permute-done((bf16[1,13,48,128]{3,2,1,0:T(8,128)(2,1)}, bf16[1,13,48,128]{3,2,1,0:T(8,128)(2,1)S(1)}, u32[]{:S(2)}, u32[]{:S(2)}) %collective-permute-start.48) | collective-permute-done | bytes 159776 | tf_op jit(solution)/shard_map/cond/branch_1_fun/ppermute | solution.py:314
  41.3 1.5 %collective-permute-start.46 = (bf16[1,13,48,128]{3,2,1,0:T(8,128)(2,1)S(1)}, bf16[1,13,48,128]{3,2,1,0:T(8,128)(2,1)S(1)}, u32[]{:S(2)}, u32[]{:S(2)}) collective-permute-start(bf16[1,13,48,128]{3,2,1,0:T(8,128)(2,1)S(1)} %collective-permute-done.44.refs_11_), channel_id=1, source_target_pairs={{0,2},{1,3},{2,0},{3,1},{4,6},{5,7},{6,4},{7,5},{8,10},{9,11},{10,... | collective-permute-start | bytes 479240 | tf_op jit(solution)/shard_map/cond/branch_1_fun/ppermute | solution.py:314
  42.8 0.0 collective-permute-start.45
  42.8 1.7 %collective-permute-done.32 = bf16[1,13,48,128]{3,2,1,0:T(8,128)(2,1)S(1)} collective-permute-done((bf16[1,13,48,128]{3,2,1,0:T(8,128)(2,1)S(1)}, bf16[1,13,48,128]{3,2,1,0:T(8,128)(2,1)S(1)}, u32[]{:S(2)}, u32[]{:S(2)}) %collective-permute-start.32) | collective-permute-done | bytes 159776 | tf_op jit(solution)/shard_map/cond/branch_1_fun/ppermute | solution.py:314
  44.6 1.6 %broadcast_select_fusion.14 = (bf16[1,13,48,128]{3,2,1,0:T(8,128)(2,1)S(1)}, bf16[1,13,48,128]{3,2,1,0:T(8,128)(2,1)}, bf16[1,13,48,128]{3,2,1,0:T(8,128)(2,1)S(1)}, bf16[1,13,48,128]{3,2,1,0:T(8,128)(2,1)S(1)}) fusion(pred[]{:T(512)S(6)} %eq.22, bf16[1,13,48,128]{3,2,1,0:T(8,128)(2,1)S(1)} %collective-permute-done.30, ...), kind=kLoop, calls=%fused_computation.16 | loop fusion | flops 479232 | bytes 1277954 | tf_op jit(solution)/shard_map/cond/branch_1_fun/jit(_where)/select_n | solution.py:378
  46.2 1.5 %collective-permute-start.38 = (bf16[2,13,48,128]{3,2,1,0:T(8,128)(2,1)}, bf16[2,13,48,128]{3,2,1,0:T(8,128)(2,1)S(1)}, u32[]{:S(2)}, u32[]{:S(2)}) collective-permute-start(bf16[2,13,48,128]{3,2,1,0:T(8,128)(2,1)} %get-tuple-element.69.refs_3_), channel_id=1, source_target_pairs={{0,2},{1,3},{2,0},{3,1},{4,6},{5,7},{6,4},{7,5},{8,10},{9,11},{10,... | collective-permute-start | bytes 958472 | tf_op jit(solution)/shard_map/cond/branch_1_fun/ppermute | solution.py:314
  47.6 5.5 %collective-permute-done.56.refs_23_ = bf16[1,13,48,128]{3,2,1,0:T(8,128)(2,1)S(1)} collective-permute-done((bf16[1,13,48,128]{3,2,1,0:T(8,128)(2,1)S(1)}, bf16[1,13,48,128]{3,2,1,0:T(8,128)(2,1)S(1)}, u32[]{:S(2)}, u32[]{:S(2)}) %collective-permute-start.56) | collective-permute-done | bytes 159776 | tf_op jit(solution)/shard_map/cond/branch_1_fun/ppermute | solution.py:314
  53.1 0.0 collective-permute-start.37
  53.1 0.0 collective-permute-done.46.refs_13_
  53.2 0.1 collective-permute-start.49
  53.3 0.0 collective-permute-done.45.refs_12_
  53.3 1.6 %collective-permute-start.35 = (bf16[2,13,48,128]{3,2,1,0:T(8,128)(2,1)S(1)}, bf16[2,13,48,128]{3,2,1,0:T(8,128)(2,1)S(1)}, u32[]{:S(2)}, u32[]{:S(2)}) collective-permute-start(bf16[2,13,48,128]{3,2,1,0:T(8,128)(2,1)S(1)} %pad_maximum_fusion.1), channel_id=1, source_target_pairs={{0,2},{1,3},{2,0},{3,1},{4,6},{5,7},{6,4},{7,5},{8,10},{9,11},{10,... | collective-permute-start | bytes 958472 | tf_op jit(solution)/shard_map/cond/branch_1_fun/ppermute | solution.py:314
  54.9 4.8 %collective-permute-done.49.refs_15_ = bf16[1,13,48,128]{3,2,1,0:T(8,128)(2,1)S(1)} collective-permute-done((bf16[1,13,48,128]{3,2,1,0:T(8,128)(2,1)S(1)}, bf16[1,13,48,128]{3,2,1,0:T(8,128)(2,1)S(1)}, u32[]{:S(2)}, u32[]{:S(2)}) %collective-permute-start.49) | collective-permute-done | bytes 159776 | tf_op jit(solution)/shard_map/cond/branch_1_fun/ppermute | solution.py:314
  59.7 0.0 collective-permute-start.55
  59.7 0.0 collective-permute-done.40.refs_7_
  59.7 0.5 collective-permute-start.34
  60.2 1.5 %collective-permute-start.42 = (bf16[2,13,48,128]{3,2,1,0:T(8,128)(2,1)S(1)}, bf16[2,13,48,128]{3,2,1,0:T(8,128)(2,1)S(1)}, u32[]{:S(2)}, u32[]{:S(2)}) collective-permute-start(bf16[2,13,48,128]{3,2,1,0:T(8,128)(2,1)S(1)} %collective-permute-done.40.refs_7_), channel_id=1, source_target_pairs={{0,2},{1,3},{2,0},{3,1},{4,6},{5,7},{6,4},{7,5},{8,10},{9,11},{10,... | collective-permute-start | bytes 958472 | tf_op jit(solution)/shard_map/cond/branch_1_fun/ppermute | solution.py:314
  61.8 0.5 collective-permute-start.58
  62.3 0.0 collective-permute-done.34.refs_1_
  62.3 0.5 collective-permute-start.47
  62.8 0.8 collective-permute-done.35
  63.5 1.5 %collective-permute-start.51 = (bf16[1,13,48,128]{3,2,1,0:T(8,128)(2,1)S(1)}, bf16[1,13,48,128]{3,2,1,0:T(8,128)(2,1)S(1)}, u32[]{:S(2)}, u32[]{:S(2)}) collective-permute-start(bf16[1,13,48,128]{3,2,1,0:T(8,128)(2,1)S(1)} %collective-permute-done.49.refs_15_), channel_id=1, source_target_pairs={{0,2},{1,3},{2,0},{3,1},{4,6},{5,7},{6,4},{7,5},{8,10},{9,11},{10,... | collective-permute-start | bytes 479240 | tf_op jit(solution)/shard_map/cond/branch_1_fun/ppermute | solution.py:314
  65.1 0.7 broadcast_select_fusion.12
  65.7 8.3 %collective-permute-done.58.refs_25_ = bf16[1,13,48,128]{3,2,1,0:T(8,128)(2,1)S(1)} collective-permute-done((bf16[1,13,48,128]{3,2,1,0:T(8,128)(2,1)S(1)}, bf16[1,13,48,128]{3,2,1,0:T(8,128)(2,1)S(1)}, u32[]{:S(2)}, u32[]{:S(2)}) %collective-permute-start.58) | collective-permute-done | bytes 159776 | tf_op jit(solution)/shard_map/cond/branch_1_fun/ppermute | solution.py:314
  74.0 0.0 collective-permute-start.50
  74.0 0.0 collective-permute-done.57.refs_24_
  74.0 0.5 collective-permute-start.41
  74.5 0.0 collective-permute-done.47.refs_14_
  74.6 0.1 collective-permute-start.36
  74.6 2.3 %collective-permute-done.51.refs_17_ = bf16[1,13,48,128]{3,2,1,0:T(8,128)(2,1)S(1)} collective-permute-done((bf16[1,13,48,128]{3,2,1,0:T(8,128)(2,1)S(1)}, bf16[1,13,48,128]{3,2,1,0:T(8,128)(2,1)S(1)}, u32[]{:S(2)}, u32[]{:S(2)}) %collective-permute-start.51) | collective-permute-done | bytes 159776 | tf_op jit(solution)/shard_map/cond/branch_1_fun/ppermute | solution.py:314
  77.0 0.5 collective-permute-start.43
  77.5 0.0 collective-permute-done.50.refs_16_
  77.5 0.1 collective-permute-start.59
  77.6 0.4 collective-permute-start.52
  78.0 0.2 copy-done.35
  78.2 10.8 %sources.4.refs_1_ = bf16[26,512,384]{2,1,0:T(8,128)(2,1)} custom-call(bf16[1,13,48,128]{3,2,1,0:T(8,128)(2,1)} %get-tuple-element.134.refs_0_, bf16[1,13,48,128]{3,2,1,0:T(8,128)(2,1)} %copy-done.31, bf16[1,13,48,128]{3,2,1,0:T(8,128)(2,1)} %get-tuple-element.136.refs_2_, bf16[1,13,48,128]{3,2,1,0:T(8,128)(2,1)} %copy-done.35), custom_call_target="tpu_custom_call" | custom-call | tf_op jit(solution)/shard_map/cond/branch_1_fun/sources/pallas_call | solution.py:318
  89.2 0.0 collective-permute-done.59.refs_26_
  89.3 0.0 collective-permute-done.41.refs_8_
  89.3 0.0 collective-permute-done.39.refs_6_
  89.3 0.6 copy-done.65
  89.9 0.1 copy-done.67
  90.0 0.2 copy-done.20
  90.1 0.1 copy-done.22
  90.2 0.7 copy-done.25
  90.9 20.6 %correlate.4 = bf16[2,32,101,128]{3,2,1,0:T(8,128)(2,1)} custom-call(s32[1]{0:T(128)} %bitcast.3.refs_0_, bf16[26,512,384]{2,1,0:T(8,128)(2,1)} %sources.4.refs_1_, bf16[208,416]{1,0:T(8,128)(2,1)} %constant.44.clone.2.refs_2_, bf16[2,13,48,128]{3,2,1,0:T(8,128)(2,1)} %get-tuple-element.69.refs_3_, bf16[2,13,48,128]{3,2,1,0:T(8,128)(2,1)} %copy-done.8, ...), custom_call_target="tpu_custom_call" | custom-call | tf_op jit(solution)/shard_map/cond/branch_1_fun/correlate/pallas_call | solution.py:318
  111.6 1.7 %copy.24 = bf16[2,32,101,128]{3,1,2,0:T(8,128)(2,1)S(1)} copy(bf16[2,32,101,128]{3,2,1,0:T(8,128)(2,1)} %correlate.4) | data formatting | bytes 3309568 | tf_op jit(solution)/shard_map/cond
  113.7 0.0 copy-start
  113.8 1.2 %copy-done = bf16[2,32,101,128]{3,1,2,0:T(8,128)(2,1)} copy-done((bf16[2,32,101,128]{3,1,2,0:T(8,128)(2,1)}, bf16[2,32,101,128]{3,1,2,0:T(8,128)(2,1)S(1)}, u32[]{:S(2)}) %copy-start) | copy-done | bytes 1654808
  (59 shorter events, 0.2 us)
Async XLA Ops:
  8.8 13.5 %collective-permute-start.31 = (bf16[1,13,48,128]{3,2,1,0:T(8,128)(2,1)}, bf16[1,13,48,128]{3,2,1,0:T(8,128)(2,1)S(1)}, u32[]{:S(2)}, u32[]{:S(2)}) collective-permute-start(bf16[1,13,48,128]{3,2,1,0:T(8,128)(2,1)} %get-tuple-element.65), channel_id=1, source_target_pairs={{0,8},{4,12},{8,0},{12,4},{1,9},{5,13},{9,1},{13,5},{2,10},{6,14},... | collective-permute-start | bytes 479240 | tf_op jit(solution)/shard_map/cond/branch_1_fun/ppermute | solution.py:314
  12.8 19.7 %collective-permute-start.30 = (bf16[1,13,48,128]{3,2,1,0:T(8,128)(2,1)}, bf16[1,13,48,128]{3,2,1,0:T(8,128)(2,1)S(1)}, u32[]{:S(2)}, u32[]{:S(2)}) collective-permute-start(bf16[1,13,48,128]{3,2,1,0:T(8,128)(2,1)} %get-tuple-element.64), channel_id=1, source_target_pairs={{0,4},{4,0},{8,12},{12,8},{1,5},{5,1},{9,13},{13,9},{2,6},{6,2},{1... | collective-permute-start | bytes 479240 | tf_op jit(solution)/shard_map/cond/branch_1_fun/ppermute | solution.py:314
  14.4 20.7 %collective-permute-start.33 = (bf16[1,13,48,128]{3,2,1,0:T(8,128)(2,1)}, bf16[1,13,48,128]{3,2,1,0:T(8,128)(2,1)S(1)}, u32[]{:S(2)}, u32[]{:S(2)}) collective-permute-start(bf16[1,13,48,128]{3,2,1,0:T(8,128)(2,1)} %get-tuple-element.67), channel_id=1, source_target_pairs={{0,8},{4,12},{8,0},{12,4},{1,9},{5,13},{9,1},{13,5},{2,10},{6,14},... | collective-permute-start | bytes 479240 | tf_op jit(solution)/shard_map/cond/branch_1_fun/ppermute | solution.py:314
  14.7 23.9 %collective-permute-start.44 = (bf16[1,13,48,128]{3,2,1,0:T(8,128)(2,1)}, bf16[1,13,48,128]{3,2,1,0:T(8,128)(2,1)S(1)}, u32[]{:S(2)}, u32[]{:S(2)}) collective-permute-start(bf16[1,13,48,128]{3,2,1,0:T(8,128)(2,1)} %get-tuple-element.71), channel_id=1, source_target_pairs={{0,8},{4,12},{8,0},{12,4},{1,9},{5,13},{9,1},{13,5},{2,10},{6,14},... | collective-permute-start | bytes 479240 | tf_op jit(solution)/shard_map/cond/branch_1_fun/ppermute | solution.py:314
  17.3 23.9 %collective-permute-start.48 = (bf16[1,13,48,128]{3,2,1,0:T(8,128)(2,1)}, bf16[1,13,48,128]{3,2,1,0:T(8,128)(2,1)S(1)}, u32[]{:S(2)}, u32[]{:S(2)}) collective-permute-start(bf16[1,13,48,128]{3,2,1,0:T(8,128)(2,1)} %get-tuple-element.72), channel_id=1, source_target_pairs={{0,8},{4,12},{8,0},{12,4},{1,9},{5,13},{9,1},{13,5},{2,10},{6,14},... | collective-permute-start | bytes 479240 | tf_op jit(solution)/shard_map/cond/branch_1_fun/ppermute | solution.py:314
  22.3 66.7 %copy-start.37 = (bf16[1,13,48,128]{3,2,1,0:T(8,128)(2,1)}, bf16[1,13,48,128]{3,2,1,0:T(8,128)(2,1)S(1)}, u32[]{:S(2)}) copy-start(bf16[1,13,48,128]{3,2,1,0:T(8,128)(2,1)S(1)} %collective-permute-done.31.refs_19_) | copy-start | bytes 479236 | tf_op jit(solution)/shard_map/cond
  22.3 20.5 %collective-permute-start.54 = (bf16[1,13,48,128]{3,2,1,0:T(8,128)(2,1)S(1)}, bf16[1,13,48,128]{3,2,1,0:T(8,128)(2,1)S(1)}, u32[]{:S(2)}, u32[]{:S(2)}) collective-permute-start(bf16[1,13,48,128]{3,2,1,0:T(8,128)(2,1)S(1)} %collective-permute-done.31.refs_19_), channel_id=1, source_target_pairs={{0,2},{1,3},{2,0},{3,1},{4,6},{5,7},{6,4},{7,5},{8,10},{9,11},{10,... | collective-permute-start | bytes 479240 | tf_op jit(solution)/shard_map/cond/branch_1_fun/ppermute | solution.py:314
  32.5 12.0 %collective-permute-start.32 = (bf16[1,13,48,128]{3,2,1,0:T(8,128)(2,1)S(1)}, bf16[1,13,48,128]{3,2,1,0:T(8,128)(2,1)S(1)}, u32[]{:S(2)}, u32[]{:S(2)}) collective-permute-start(bf16[1,13,48,128]{3,2,1,0:T(8,128)(2,1)S(1)} %collective-permute-done.31.refs_19_), channel_id=1, source_target_pairs={{0,4},{4,0},{8,12},{12,8},{1,5},{5,1},{9,13},{13,9},{2,6},{6,2},{1... | collective-permute-start | bytes 479240 | tf_op jit(solution)/shard_map/cond/branch_1_fun/ppermute | solution.py:314
  35.1 24.6 %collective-permute-start.40 = (bf16[2,13,48,128]{3,2,1,0:T(8,128)(2,1)}, bf16[2,13,48,128]{3,2,1,0:T(8,128)(2,1)S(1)}, u32[]{:S(2)}, u32[]{:S(2)}) collective-permute-start(bf16[2,13,48,128]{3,2,1,0:T(8,128)(2,1)} %get-tuple-element.70), channel_id=1, source_target_pairs={{0,4},{4,0},{8,12},{12,8},{1,5},{5,1},{9,13},{13,9},{2,6},{6,2},{1... | collective-permute-start | bytes 958472 | tf_op jit(solution)/shard_map/cond/branch_1_fun/ppermute | solution.py:314
  38.7 50.4 %copy-start.39 = (bf16[1,13,48,128]{3,2,1,0:T(8,128)(2,1)}, bf16[1,13,48,128]{3,2,1,0:T(8,128)(2,1)S(1)}, u32[]{:S(2)}) copy-start(bf16[1,13,48,128]{3,2,1,0:T(8,128)(2,1)S(1)} %collective-permute-done.44.refs_11_) | copy-start | bytes 479236 | tf_op jit(solution)/shard_map/cond
  38.7 7.5 %collective-permute-start.53 = (bf16[1,13,48,128]{3,2,1,0:T(8,128)(2,1)S(1)}, bf16[1,13,48,128]{3,2,1,0:T(8,128)(2,1)S(1)}, u32[]{:S(2)}, u32[]{:S(2)}) collective-permute-start(bf16[1,13,48,128]{3,2,1,0:T(8,128)(2,1)S(1)} %collective-permute-done.31.refs_19_), channel_id=1, source_target_pairs={{0,1},{1,0},{2,3},{3,2},{4,5},{5,4},{6,7},{7,6},{8,9},{9,8},{10,11... | collective-permute-start | bytes 479240 | tf_op jit(solution)/shard_map/cond/branch_1_fun/ppermute | solution.py:314
  41.3 11.9 %collective-permute-start.46 = (bf16[1,13,48,128]{3,2,1,0:T(8,128)(2,1)S(1)}, bf16[1,13,48,128]{3,2,1,0:T(8,128)(2,1)S(1)}, u32[]{:S(2)}, u32[]{:S(2)}) collective-permute-start(bf16[1,13,48,128]{3,2,1,0:T(8,128)(2,1)S(1)} %collective-permute-done.44.refs_11_), channel_id=1, source_target_pairs={{0,2},{1,3},{2,0},{3,1},{4,6},{5,7},{6,4},{7,5},{8,10},{9,11},{10,... | collective-permute-start | bytes 479240 | tf_op jit(solution)/shard_map/cond/branch_1_fun/ppermute | solution.py:314
  42.8 46.3 %copy-start.41 = (bf16[1,13,48,128]{3,2,1,0:T(8,128)(2,1)}, bf16[1,13,48,128]{3,2,1,0:T(8,128)(2,1)S(1)}, u32[]{:S(2)}) copy-start(bf16[1,13,48,128]{3,2,1,0:T(8,128)(2,1)S(1)} %collective-permute-done.54.refs_21_) | copy-start | bytes 479236 | tf_op jit(solution)/shard_map/cond
  42.8 10.5 %collective-permute-start.45 = (bf16[1,13,48,128]{3,2,1,0:T(8,128)(2,1)S(1)}, bf16[1,13,48,128]{3,2,1,0:T(8,128)(2,1)S(1)}, u32[]{:S(2)}, u32[]{:S(2)}) collective-permute-start(bf16[1,13,48,128]{3,2,1,0:T(8,128)(2,1)S(1)} %collective-permute-done.44.refs_11_), channel_id=1, source_target_pairs={{0,1},{1,0},{2,3},{3,2},{4,5},{5,4},{6,7},{7,6},{8,9},{9,8},{10,11... | collective-permute-start | bytes 479240 | tf_op jit(solution)/shard_map/cond/branch_1_fun/ppermute | solution.py:314
  44.6 8.6 %collective-permute-start.56 = (bf16[1,13,48,128]{3,2,1,0:T(8,128)(2,1)S(1)}, bf16[1,13,48,128]{3,2,1,0:T(8,128)(2,1)S(1)}, u32[]{:S(2)}, u32[]{:S(2)}) collective-permute-start(bf16[1,13,48,128]{3,2,1,0:T(8,128)(2,1)S(1)} %collective-permute-done.33), channel_id=1, source_target_pairs={{0,4},{4,0},{8,12},{12,8},{1,5},{5,1},{9,13},{13,9},{2,6},{6,2},{1... | collective-permute-start | bytes 479240 | tf_op jit(solution)/shard_map/cond/branch_1_fun/ppermute | solution.py:314
  46.2 42.9 %copy-start.43 = (bf16[1,13,48,128]{3,2,1,0:T(8,128)(2,1)}, bf16[1,13,48,128]{3,2,1,0:T(8,128)(2,1)S(1)}, u32[]{:S(2)}) copy-start(bf16[1,13,48,128]{3,2,1,0:T(8,128)(2,1)S(1)} %collective-permute-done.53.refs_20_) | copy-start | bytes 479236 | tf_op jit(solution)/shard_map/cond
  46.2 14.0 %collective-permute-start.38 = (bf16[2,13,48,128]{3,2,1,0:T(8,128)(2,1)}, bf16[2,13,48,128]{3,2,1,0:T(8,128)(2,1)S(1)}, u32[]{:S(2)}, u32[]{:S(2)}) collective-permute-start(bf16[2,13,48,128]{3,2,1,0:T(8,128)(2,1)} %get-tuple-element.69.refs_3_), channel_id=1, source_target_pairs={{0,2},{1,3},{2,0},{3,1},{4,6},{5,7},{6,4},{7,5},{8,10},{9,11},{10,... | collective-permute-start | bytes 958472 | tf_op jit(solution)/shard_map/cond/branch_1_fun/ppermute | solution.py:314
  53.1 35.9 %copy-start.49 = (bf16[1,13,48,128]{3,2,1,0:T(8,128)(2,1)}, bf16[1,13,48,128]{3,2,1,0:T(8,128)(2,1)S(1)}, u32[]{:S(2)}) copy-start(bf16[1,13,48,128]{3,2,1,0:T(8,128)(2,1)S(1)} %collective-permute-done.56.refs_23_) | copy-start | bytes 479236 | tf_op jit(solution)/shard_map/cond
  53.1 8.6 %collective-permute-start.37 = (bf16[2,13,48,128]{3,2,1,0:T(8,128)(2,1)}, bf16[2,13,48,128]{3,2,1,0:T(8,128)(2,1)S(1)}, u32[]{:S(2)}, u32[]{:S(2)}) collective-permute-start(bf16[2,13,48,128]{3,2,1,0:T(8,128)(2,1)} %get-tuple-element.69.refs_3_), channel_id=1, source_target_pairs={{0,1},{1,0},{2,3},{3,2},{4,5},{5,4},{6,7},{7,6},{8,9},{9,8},{10,11... | collective-permute-start | bytes 958472 | tf_op jit(solution)/shard_map/cond/branch_1_fun/ppermute | solution.py:314
  53.1 35.9 %copy-start.45 = (bf16[1,13,48,128]{3,2,1,0:T(8,128)(2,1)}, bf16[1,13,48,128]{3,2,1,0:T(8,128)(2,1)S(1)}, u32[]{:S(2)}) copy-start(bf16[1,13,48,128]{3,2,1,0:T(8,128)(2,1)S(1)} %collective-permute-done.46.refs_13_) | copy-start | bytes 479236 | tf_op jit(solution)/shard_map/cond
  53.2 6.5 %collective-permute-start.49 = (bf16[1,13,48,128]{3,2,1,0:T(8,128)(2,1)S(1)}, bf16[1,13,48,128]{3,2,1,0:T(8,128)(2,1)S(1)}, u32[]{:S(2)}, u32[]{:S(2)}) collective-permute-start(bf16[1,13,48,128]{3,2,1,0:T(8,128)(2,1)S(1)} %collective-permute-done.48), channel_id=1, source_target_pairs={{0,4},{4,0},{8,12},{12,8},{1,5},{5,1},{9,13},{13,9},{2,6},{6,2},{1... | collective-permute-start | bytes 479240 | tf_op jit(solution)/shard_map/cond/branch_1_fun/ppermute | solution.py:314
  53.3 35.8 %copy-start.47 = (bf16[1,13,48,128]{3,2,1,0:T(8,128)(2,1)}, bf16[1,13,48,128]{3,2,1,0:T(8,128)(2,1)S(1)}, u32[]{:S(2)}) copy-start(bf16[1,13,48,128]{3,2,1,0:T(8,128)(2,1)S(1)} %collective-permute-done.45.refs_12_) | copy-start | bytes 479236 | tf_op jit(solution)/shard_map/cond
  53.3 10.2 %collective-permute-start.35 = (bf16[2,13,48,128]{3,2,1,0:T(8,128)(2,1)S(1)}, bf16[2,13,48,128]{3,2,1,0:T(8,128)(2,1)S(1)}, u32[]{:S(2)}, u32[]{:S(2)}) collective-permute-start(bf16[2,13,48,128]{3,2,1,0:T(8,128)(2,1)S(1)} %pad_maximum_fusion.1), channel_id=1, source_target_pairs={{0,2},{1,3},{2,0},{3,1},{4,6},{5,7},{6,4},{7,5},{8,10},{9,11},{10,... | collective-permute-start | bytes 958472 | tf_op jit(solution)/shard_map/cond/branch_1_fun/ppermute | solution.py:314
  59.7 29.4 %copy-start.51 = (bf16[1,13,48,128]{3,2,1,0:T(8,128)(2,1)}, bf16[1,13,48,128]{3,2,1,0:T(8,128)(2,1)S(1)}, u32[]{:S(2)}) copy-start(bf16[1,13,48,128]{3,2,1,0:T(8,128)(2,1)S(1)} %collective-permute-done.49.refs_15_) | copy-start | bytes 479236 | tf_op jit(solution)/shard_map/cond
  59.7 2.6 %collective-permute-start.55 = (bf16[1,13,48,128]{3,2,1,0:T(8,128)(2,1)S(1)}, bf16[1,13,48,128]{3,2,1,0:T(8,128)(2,1)S(1)}, u32[]{:S(2)}, u32[]{:S(2)}) collective-permute-start(bf16[1,13,48,128]{3,2,1,0:T(8,128)(2,1)S(1)} %collective-permute-done.54.refs_21_), channel_id=1, source_target_pairs={{0,1},{1,0},{2,3},{3,2},{4,5},{5,4},{6,7},{7,6},{8,9},{9,8},{10,11... | collective-permute-start | bytes 479240 | tf_op jit(solution)/shard_map/cond/branch_1_fun/ppermute | solution.py:314
  59.7 29.4 %copy-start.2 = (bf16[2,13,48,128]{3,2,1,0:T(8,128)(2,1)}, bf16[2,13,48,128]{3,2,1,0:T(8,128)(2,1)S(1)}, u32[]{:S(2)}) copy-start(bf16[2,13,48,128]{3,2,1,0:T(8,128)(2,1)S(1)} %collective-permute-done.40.refs_7_) | copy-start | bytes 958468 | tf_op jit(solution)/shard_map/cond
  59.7 2.5 %collective-permute-start.34 = (bf16[1,13,48,128]{3,2,1,0:T(8,128)(2,1)S(1)}, bf16[1,13,48,128]{3,2,1,0:T(8,128)(2,1)S(1)}, u32[]{:S(2)}, u32[]{:S(2)}) collective-permute-start(bf16[1,13,48,128]{3,2,1,0:T(8,128)(2,1)S(1)} %get-tuple-element.133), channel_id=1, source_target_pairs={{0,1},{1,0},{2,3},{3,2},{4,5},{5,4},{6,7},{7,6},{8,9},{9,8},{10,11... | collective-permute-start | bytes 479240 | tf_op jit(solution)/shard_map/cond/branch_1_fun/ppermute | solution.py:314
  60.2 28.9 %copy-start.6 = (bf16[2,13,48,128]{3,2,1,0:T(8,128)(2,1)}, bf16[2,13,48,128]{3,2,1,0:T(8,128)(2,1)S(1)}, u32[]{:S(2)}) copy-start(bf16[2,13,48,128]{3,2,1,0:T(8,128)(2,1)S(1)} %collective-permute-done.38.refs_5_) | copy-start | bytes 958468 | tf_op jit(solution)/shard_map/cond
  60.2 16.7 %collective-permute-start.42 = (bf16[2,13,48,128]{3,2,1,0:T(8,128)(2,1)S(1)}, bf16[2,13,48,128]{3,2,1,0:T(8,128)(2,1)S(1)}, u32[]{:S(2)}, u32[]{:S(2)}) collective-permute-start(bf16[2,13,48,128]{3,2,1,0:T(8,128)(2,1)S(1)} %collective-permute-done.40.refs_7_), channel_id=1, source_target_pairs={{0,2},{1,3},{2,0},{3,1},{4,6},{5,7},{6,4},{7,5},{8,10},{9,11},{10,... | collective-permute-start | bytes 958472 | tf_op jit(solution)/shard_map/cond/branch_1_fun/ppermute | solution.py:314
  61.8 27.4 %copy-start.8 = (bf16[2,13,48,128]{3,2,1,0:T(8,128)(2,1)}, bf16[2,13,48,128]{3,2,1,0:T(8,128)(2,1)S(1)}, u32[]{:S(2)}) copy-start(bf16[2,13,48,128]{3,2,1,0:T(8,128)(2,1)S(1)} %collective-permute-done.37.refs_4_) | copy-start | bytes 958468 | tf_op jit(solution)/shard_map/cond
  61.8 12.3 %collective-permute-start.58 = (bf16[1,13,48,128]{3,2,1,0:T(8,128)(2,1)S(1)}, bf16[1,13,48,128]{3,2,1,0:T(8,128)(2,1)S(1)}, u32[]{:S(2)}, u32[]{:S(2)}) collective-permute-start(bf16[1,13,48,128]{3,2,1,0:T(8,128)(2,1)S(1)} %collective-permute-done.56.refs_23_), channel_id=1, source_target_pairs={{0,2},{1,3},{2,0},{3,1},{4,6},{5,7},{6,4},{7,5},{8,10},{9,11},{10,... | collective-permute-start | bytes 479240 | tf_op jit(solution)/shard_map/cond/branch_1_fun/ppermute | solution.py:314
  62.2 26.9 %copy-start.53 = (bf16[1,13,48,128]{3,2,1,0:T(8,128)(2,1)}, bf16[1,13,48,128]{3,2,1,0:T(8,128)(2,1)S(1)}, u32[]{:S(2)}) copy-start(bf16[1,13,48,128]{3,2,1,0:T(8,128)(2,1)S(1)} %collective-permute-done.55.refs_22_) | copy-start | bytes 479236 | tf_op jit(solution)/shard_map/cond
  62.3 11.8 %collective-permute-start.57 = (bf16[1,13,48,128]{3,2,1,0:T(8,128)(2,1)S(1)}, bf16[1,13,48,128]{3,2,1,0:T(8,128)(2,1)S(1)}, u32[]{:S(2)}, u32[]{:S(2)}) collective-permute-start(bf16[1,13,48,128]{3,2,1,0:T(8,128)(2,1)S(1)} %collective-permute-done.56.refs_23_), channel_id=1, source_target_pairs={{0,1},{1,0},{2,3},{3,2},{4,5},{5,4},{6,7},{7,6},{8,9},{9,8},{10,11... | collective-permute-start | bytes 479240 | tf_op jit(solution)/shard_map/cond/branch_1_fun/ppermute | solution.py:314
  62.3 15.7 %copy-start.31 = (bf16[1,13,48,128]{3,2,1,0:T(8,128)(2,1)}, bf16[1,13,48,128]{3,2,1,0:T(8,128)(2,1)S(1)}, u32[]{:S(2)}) copy-start(bf16[1,13,48,128]{3,2,1,0:T(8,128)(2,1)S(1)} %collective-permute-done.34.refs_1_) | copy-start | bytes 479236 | tf_op jit(solution)/shard_map/cond
  62.3 12.3 %collective-permute-start.47 = (bf16[1,13,48,128]{3,2,1,0:T(8,128)(2,1)S(1)}, bf16[1,13,48,128]{3,2,1,0:T(8,128)(2,1)S(1)}, u32[]{:S(2)}, u32[]{:S(2)}) collective-permute-start(bf16[1,13,48,128]{3,2,1,0:T(8,128)(2,1)S(1)} %collective-permute-done.46.refs_13_), channel_id=1, source_target_pairs={{0,1},{1,0},{2,3},{3,2},{4,5},{5,4},{6,7},{7,6},{8,9},{9,8},{10,11... | collective-permute-start | bytes 479240 | tf_op jit(solution)/shard_map/cond/branch_1_fun/ppermute | solution.py:314
  63.5 13.4 %collective-permute-start.51 = (bf16[1,13,48,128]{3,2,1,0:T(8,128)(2,1)S(1)}, bf16[1,13,48,128]{3,2,1,0:T(8,128)(2,1)S(1)}, u32[]{:S(2)}, u32[]{:S(2)}) collective-permute-start(bf16[1,13,48,128]{3,2,1,0:T(8,128)(2,1)S(1)} %collective-permute-done.49.refs_15_), channel_id=1, source_target_pairs={{0,2},{1,3},{2,0},{3,1},{4,6},{5,7},{6,4},{7,5},{8,10},{9,11},{10,... | collective-permute-start | bytes 479240 | tf_op jit(solution)/shard_map/cond/branch_1_fun/ppermute | solution.py:314
  74.0 15.1 %copy-start.55 = (bf16[1,13,48,128]{3,2,1,0:T(8,128)(2,1)}, bf16[1,13,48,128]{3,2,1,0:T(8,128)(2,1)S(1)}, u32[]{:S(2)}) copy-start(bf16[1,13,48,128]{3,2,1,0:T(8,128)(2,1)S(1)} %collective-permute-done.58.refs_25_) | copy-start | bytes 479236 | tf_op jit(solution)/shard_map/cond
  74.0 3.4 %collective-permute-start.50 = (bf16[1,13,48,128]{3,2,1,0:T(8,128)(2,1)S(1)}, bf16[1,13,48,128]{3,2,1,0:T(8,128)(2,1)S(1)}, u32[]{:S(2)}, u32[]{:S(2)}) collective-permute-start(bf16[1,13,48,128]{3,2,1,0:T(8,128)(2,1)S(1)} %collective-permute-done.49.refs_15_), channel_id=1, source_target_pairs={{0,1},{1,0},{2,3},{3,2},{4,5},{5,4},{6,7},{7,6},{8,9},{9,8},{10,11... | collective-permute-start | bytes 479240 | tf_op jit(solution)/shard_map/cond/branch_1_fun/ppermute | solution.py:314
  74.0 15.1 %copy-start.57 = (bf16[1,13,48,128]{3,2,1,0:T(8,128)(2,1)}, bf16[1,13,48,128]{3,2,1,0:T(8,128)(2,1)S(1)}, u32[]{:S(2)}) copy-start(bf16[1,13,48,128]{3,2,1,0:T(8,128)(2,1)S(1)} %collective-permute-done.57.refs_24_) | copy-start | bytes 479236 | tf_op jit(solution)/shard_map/cond
  74.0 15.2 %collective-permute-start.41 = (bf16[2,13,48,128]{3,2,1,0:T(8,128)(2,1)S(1)}, bf16[2,13,48,128]{3,2,1,0:T(8,128)(2,1)S(1)}, u32[]{:S(2)}, u32[]{:S(2)}) collective-permute-start(bf16[2,13,48,128]{3,2,1,0:T(8,128)(2,1)S(1)} %collective-permute-done.40.refs_7_), channel_id=1, source_target_pairs={{0,1},{1,0},{2,3},{3,2},{4,5},{5,4},{6,7},{7,6},{8,9},{9,8},{10,11... | collective-permute-start | bytes 958472 | tf_op jit(solution)/shard_map/cond/branch_1_fun/ppermute | solution.py:314
  74.6 14.6 %copy-start.59 = (bf16[1,13,48,128]{3,2,1,0:T(8,128)(2,1)}, bf16[1,13,48,128]{3,2,1,0:T(8,128)(2,1)S(1)}, u32[]{:S(2)}) copy-start(bf16[1,13,48,128]{3,2,1,0:T(8,128)(2,1)S(1)} %collective-permute-done.47.refs_14_) | copy-start | bytes 479236 | tf_op jit(solution)/shard_map/cond
  74.6 3.0 %collective-permute-start.36 = (bf16[1,13,48,128]{3,2,1,0:T(8,128)(2,1)S(1)}, bf16[1,13,48,128]{3,2,1,0:T(8,128)(2,1)S(1)}, u32[]{:S(2)}, u32[]{:S(2)}) collective-permute-start(bf16[1,13,48,128]{3,2,1,0:T(8,128)(2,1)S(1)} %get-tuple-element.135), channel_id=1, source_target_pairs={{0,1},{1,0},{2,3},{3,2},{4,5},{5,4},{6,7},{7,6},{8,9},{9,8},{10,11... | collective-permute-start | bytes 479240 | tf_op jit(solution)/shard_map/cond/branch_1_fun/ppermute | solution.py:314
  76.9 12.3 %copy-start.61 = (bf16[1,13,48,128]{3,2,1,0:T(8,128)(2,1)}, bf16[1,13,48,128]{3,2,1,0:T(8,128)(2,1)S(1)}, u32[]{:S(2)}) copy-start(bf16[1,13,48,128]{3,2,1,0:T(8,128)(2,1)S(1)} %collective-permute-done.51.refs_17_) | copy-start | bytes 479236 | tf_op jit(solution)/shard_map/cond
  76.9 12.3 %collective-permute-start.39 = (bf16[2,13,48,128]{3,2,1,0:T(8,128)(2,1)S(1)}, bf16[2,13,48,128]{3,2,1,0:T(8,128)(2,1)S(1)}, u32[]{:S(2)}, u32[]{:S(2)}) collective-permute-start(bf16[2,13,48,128]{3,2,1,0:T(8,128)(2,1)S(1)} %collective-permute-done.38.refs_5_), channel_id=1, source_target_pairs={{0,1},{1,0},{2,3},{3,2},{4,5},{5,4},{6,7},{7,6},{8,9},{9,8},{10,11... | collective-permute-start | bytes 958472 | tf_op jit(solution)/shard_map/cond/branch_1_fun/ppermute | solution.py:314
  76.9 12.3 %copy-start.12 = (bf16[2,13,48,128]{3,2,1,0:T(8,128)(2,1)}, bf16[2,13,48,128]{3,2,1,0:T(8,128)(2,1)S(1)}, u32[]{:S(2)}) copy-start(bf16[2,13,48,128]{3,2,1,0:T(8,128)(2,1)S(1)} %collective-permute-done.42.refs_9_) | copy-start | bytes 958468 | tf_op jit(solution)/shard_map/cond
  77.0 12.3 %collective-permute-start.43 = (bf16[2,13,48,128]{3,2,1,0:T(8,128)(2,1)S(1)}, bf16[2,13,48,128]{3,2,1,0:T(8,128)(2,1)S(1)}, u32[]{:S(2)}, u32[]{:S(2)}) collective-permute-start(bf16[2,13,48,128]{3,2,1,0:T(8,128)(2,1)S(1)} %collective-permute-done.42.refs_9_), channel_id=1, source_target_pairs={{0,1},{1,0},{2,3},{3,2},{4,5},{5,4},{6,7},{7,6},{8,9},{9,8},{10,11... | collective-permute-start | bytes 958472 | tf_op jit(solution)/shard_map/cond/branch_1_fun/ppermute | solution.py:314
  77.5 11.7 %copy-start.63 = (bf16[1,13,48,128]{3,2,1,0:T(8,128)(2,1)}, bf16[1,13,48,128]{3,2,1,0:T(8,128)(2,1)S(1)}, u32[]{:S(2)}) copy-start(bf16[1,13,48,128]{3,2,1,0:T(8,128)(2,1)S(1)} %collective-permute-done.50.refs_16_) | copy-start | bytes 479236 | tf_op jit(solution)/shard_map/cond
  77.5 11.8 %collective-permute-start.59 = (bf16[1,13,48,128]{3,2,1,0:T(8,128)(2,1)S(1)}, bf16[1,13,48,128]{3,2,1,0:T(8,128)(2,1)S(1)}, u32[]{:S(2)}, u32[]{:S(2)}) collective-permute-start(bf16[1,13,48,128]{3,2,1,0:T(8,128)(2,1)S(1)} %collective-permute-done.58.refs_25_), channel_id=1, source_target_pairs={{0,1},{1,0},{2,3},{3,2},{4,5},{5,4},{6,7},{7,6},{8,9},{9,8},{10,11... | collective-permute-start | bytes 479240 | tf_op jit(solution)/shard_map/cond/branch_1_fun/ppermute | solution.py:314
  77.5 0.7 copy-start.35
  77.6 11.7 %collective-permute-start.52 = (bf16[1,13,48,128]{3,2,1,0:T(8,128)(2,1)S(1)}, bf16[1,13,48,128]{3,2,1,0:T(8,128)(2,1)S(1)}, u32[]{:S(2)}, u32[]{:S(2)}) collective-permute-start(bf16[1,13,48,128]{3,2,1,0:T(8,128)(2,1)S(1)} %collective-permute-done.51.refs_17_), channel_id=1, source_target_pairs={{0,1},{1,0},{2,3},{3,2},{4,5},{5,4},{6,7},{7,6},{8,9},{9,8},{10,11... | collective-permute-start | bytes 479240 | tf_op jit(solution)/shard_map/cond/branch_1_fun/ppermute | solution.py:314
  89.2 0.7 copy-start.65
  89.2 0.7 copy-start.67
  89.3 0.8 copy-start.20
  89.3 0.9 copy-start.22
  90.2 0.7 copy-start.25
  113.7 1.2 %copy-start = (bf16[2,32,101,128]{3,1,2,0:T(8,128)(2,1)}, bf16[2,32,101,128]{3,1,2,0:T(8,128)(2,1)S(1)}, u32[]{:S(2)}) copy-start(bf16[2,32,101,128]{3,1,2,0:T(8,128)(2,1)S(1)} %get-tuple-element.150) | copy-start | bytes 4964356
where the time goes:
time: 115 us
  waiting for transfers between devices  36.8 us (32%)
  Pallas kernels  34.5 us (30%)
  starting transfers between devices  30 us (26%)
  local copies, waits for them, and re-layouts  8.34 us (7%)
  other arithmetic  3.06 us (3%)
  between operations  1.24 us (1%)
    ppermute x30, waiting for transfers between devices, swap(): lax.ppermute(value, axis, [(i, i ^ mask) for i in range(lax.axis_size(axi...  36.8 us
    pallas_call x3, Pallas kernels, call(): pl.pallas_call(kernel, out_shape=outs, in_specs=specs, scratch_shapes=scr...  34.5 us
    ppermute x30, starting transfers between devices, swap(): lax.ppermute(value, axis, [(i, i ^ mask) for i in range(lax.axis_size(axi...  30 us
    cond x51, local copies, waits for them, and re-layouts  3.65 us
    another operation x1, local copies, waits for them, and re-layouts  3.01 us
  transfers between devices with their start and end apart: 30, of which 10 were waited for; matrix products, arithmetic and copies ran while one was open for 2% of the time, Pallas kernels for 9%

commit v1 on v0

--- a/solution.py
+++ b/solution.py
@@ -146,21 +146,19 @@
     return -(-nbins // K16)
 
 
-def lag_matrix(nbins, windows):
+def lag_matrix(nbins):
     samples = 2 * (nbins - 1)
     groups = 2 * bins_of(nbins)
     rows = -(-L // K8) * K8
     freq = np.arange(nbins)
     lags = np.arange(L) - (L - 1) // 2
     angle = 2.0 * np.pi / samples * (freq[:, None] * lags[None, :] % samples)
-    weight = np.where((freq == 0) | (freq == nbins - 1), 1.0, 2.0)[:, None] / math.sqrt(windows * samples)
+    weight = np.where((freq == 0) | (freq == nbins - 1), 1.0, 2.0)[:, None]
     full = np.zeros((rows, 2, groups * K8))
     full[:L, 0, :nbins] = (weight * np.cos(angle)).T
     full[:L, 1, :nbins] = -(weight * np.sin(angle)).T
     full = full.reshape(rows, 2, groups, K8).transpose(0, 2, 1, 3).reshape(rows, groups * 2 * K8)
-    high = full.astype(jnp.bfloat16)
-    low = (full - high.astype(np.float64)).astype(jnp.bfloat16)
-    return np.concatenate([high, low], axis=0)
+    return full.astype(jnp.bfloat16)
 
 
 def pack_kernel(layout, nbins, here_ref, part_ref, slot_ref, x_ref, *rest):
@@ -168,22 +166,27 @@
     n_blk, n_grp, n_row, lanes = blocks_ref.shape
     per_peer = lanes // 4
     chans = slot_ref.shape[1]
-    pairs = n_row // K16
     here = here_ref[0]
     slot = slot_ref[...]
     target = slot // chans * per_peer + slot % chans - here * per_peer
-    target = jnp.concatenate([target] * 4, axis=1)
-    wide_ref[...] = jnp.zeros(wide_ref.shape, jnp.float32)
-    shape = (lanes, 4 * chans)
-    row, col = iota(shape, 0), iota(shape, 1)
-    same = row // per_peer == col // chans
+    shape = (n_blk * lanes, chans)
+    row = iota(shape, 0)
+    pick = jnp.where(target == row // lanes * per_peer + row % per_peer, 1.0, 0.0).astype(jnp.bfloat16)
+    rows = math.prod(x_ref.shape[:-1])
+    wide = lax.dot_general(x_ref[...].reshape(rows, chans), pick, (((1,), (1,)), ((), ())), preferred_element_type=jnp.float32)
     for block in range(n_blk):
-        pick = jnp.where(same & (target == block * per_peer + row % per_peer), 1.0, 0.0).astype(jnp.bfloat16)
-        for pair in range(pairs):
-            part = jnp.concatenate([x_ref[p, pl.ds(pair * 2 * chans, 2 * chans), :] for p in range(2)], axis=0)
-            wide_ref[:, pl.ds(0, nbins)] = jnp.dot(pick, part, preferred_element_type=jnp.float32)
-            turned = wide_ref[...].T[: n_grp * K16].astype(jnp.bfloat16)
-            blocks_ref[block, :, pl.ds(pair * K16, K16), :] = turned.reshape(n_grp, K16, lanes)
+        wide_ref[block, pl.ds(0, rows), :] = wide[:, block * lanes : (block + 1) * lanes]
+    bins = n_grp * K16
+    lane_group = iota((bins, lanes), 1) // per_peer
+    inside = iota((bins, lanes), 0) < nbins
+    for block in range(n_blk):
+        for pair in range(n_row // K16):
+            value = jnp.zeros((bins, lanes), jnp.float32)
+            for g in range(4):
+                start = (2 * pair + g % 2) * 2 * nbins + g // 2
+                value = jnp.where(lane_group == g, wide_ref[block, pl.ds(start, bins, stride=2), :], value)
+            value = jnp.where(inside, value, 0.0).astype(jnp.bfloat16)
+            blocks_ref[block, :, pl.ds(pair * K16, K16), :] = value.reshape(n_grp, K16, lanes)
     masks = [part_ref[r, here] ^ here for r in range(ROUNDS)]
     masks.append(masks[0] ^ masks[1])
     for out, message in zip(outs, layout):
@@ -256,67 +259,97 @@
             out_ref[half, :, pl.ds(pair * lanes, lanes)] = both.reshape(share * 2 * K8, lanes)
 
 
-def correlate_kernel(places, nbins, windows, here_ref, left_hbm, lag_ref, *rest):
-    count = 1 + max(index for by_d in places for by_e in by_d for index, _ in by_e)
-    pieces, rest = rest[:count], rest[count:]
-    out_ref, left_ref, right_ref, cross_ref, power_ref, scale_ref, sem = rest
-    copy = pltpu.make_async_copy(left_hbm, left_ref, sem)
-    copy.start()
+def take_pieces(pieces, places, phase, here, right_ref, power_ref, scale_ref, nbins, windows):
     n_grp, n_row, lanes = pieces[0].shape[1:]
     pairs = n_row // K16
     share = lanes // 4
-    here = here_ref[0]
     shape = (4 * lanes, 4 * lanes)
     row, col = iota(shape, 0), iota(shape, 1)
-    shard = (row // lanes) ^ here
-    spot = row % lanes // share * lanes + shard * share + row % share
+    kind = row // lanes
+    half = (here >> 1) ^ phase ^ (kind >> 1)
+    odd = (here ^ kind) & 1
+    spot = row % lanes // share * lanes + (2 * half + odd) * share + row % share
     order = jnp.where(col == spot, 1.0, 0.0).astype(jnp.bfloat16)
+    total = jnp.zeros((n_grp, 2, K8, lanes), jnp.float32)
+    for e in range(4):
+        parts = [pieces[operand][index].reshape(n_grp * n_row, lanes) for operand, index in places[e]]
+        moved = jnp.dot(jnp.concatenate(parts, axis=1), order, preferred_element_type=jnp.float32)
+        moved = moved.reshape(n_grp, pairs, 2, K8, 4 * lanes)
+        for pair in range(pairs):
+            for g in range(4):
+                value = moved[:, pair, :, :, g * lanes : (g + 1) * lanes]
+                right_ref[:, :, (pair * 4 + g) * 4 + e] = value
+                total = total + value * value
     power_ref[...] = jnp.zeros(power_ref.shape, jnp.float32)
-    for r in range(ROUNDS):
-        side = pl.ds(r * lanes, lanes)
-        total = jnp.zeros((n_grp, 2, K8, lanes), jnp.float32)
-        for e in range(4):
-            parts = [pieces[places[r][d][e][0]][places[r][d][e][1]].reshape(n_grp * n_row, lanes) for d in range(4)]
-            moved = jnp.dot(jnp.concatenate(parts, axis=1), order, preferred_element_type=jnp.float32)
-            moved = moved.reshape(n_grp, pairs, 2, K8, 4 * lanes)
-            for pair in range(pairs):
-                for g in range(4):
-                    value = moved[:, pair, :, :, g * lanes : (g + 1) * lanes]
-                    right_ref[:, :, (pair * 4 + g) * 4 + e, :, side] = value
-                    total = total + value * value
-        power_ref[pl.ds(K8, n_grp * K16), side] = total.reshape(n_grp * K16, lanes)
+    power_ref[pl.ds(K8, n_grp * K16), :] = total.reshape(n_grp * K16, lanes)
     scale_ref[...] = scale_of(power_ref, nbins, windows).reshape(scale_ref.shape)
-    copy.wait()
+
+
+def whitened(right_ref, scale_ref, index, half):
+    white = (right_ref[index, half] * scale_ref[index, half]).astype(jnp.bfloat16)
+    return white.reshape(-1, white.shape[-1])
+
+
+def receive_kernel(places, nbins, windows, here_ref, *rest):
+    pieces, (out_ref, right_ref, power_ref, scale_ref) = rest[:-4], rest[-4:]
+    take_pieces(pieces, places, 0, here_ref[0], right_ref, power_ref, scale_ref, nbins, windows)
 
     def one_group(index, carry):
         for half in range(2):
-            white = (right_ref[index, half] * scale_ref[index, half]).astype(jnp.bfloat16)
-            white = white.reshape(-1, white.shape[-1])
-            cross = jnp.dot(left_ref[2 * index + half], white, preferred_element_type=jnp.float32)
+            out_ref[2 * index + half] = whitened(right_ref, scale_ref, index, half)
+        return carry
+
+    lax.fori_loop(0, right_ref.shape[0], one_group, 0)
+
+
+def correlate_kernel(places, nbins, windows, here_ref, left_hbm, early_hbm, lag_ref, *rest):
+    pieces, rest = rest[:-9], rest[-9:]
+    out_ref, left_ref, early_ref, right_ref, cross_ref, lagged_ref, power_ref, scale_ref, sems = rest
+    copies = [
+        pltpu.make_async_copy(left_hbm, left_ref, sems.at[0]),
+        pltpu.make_async_copy(early_hbm, early_ref, sems.at[1]),
+    ]
+    for copy in copies:
+        copy.start()
+    here = here_ref[0]
+    take_pieces(pieces, places, 1, here, right_ref, power_ref, scale_ref, nbins, windows)
+    for copy in copies:
+        copy.wait()
+
+    def one_group(index, carry):
+        for half in range(2):
+            both = jnp.concatenate([early_ref[2 * index + half], whitened(right_ref, scale_ref, index, half)], axis=1)
+            cross = jnp.dot(left_ref[2 * index + half], both, preferred_element_type=jnp.float32)
             place = pl.multiple_of((2 * index + half) * 2 * K8, 2 * K8)
             cross_ref[:, pl.ds(place, 2 * K8), :] = cross.astype(jnp.bfloat16).reshape(-1, 2 * K8, cross.shape[-1])
         return carry
 
-    lax.fori_loop(0, n_grp, one_group, 0)
+    lax.fori_loop(0, right_ref.shape[0], one_group, 0)
+    norm = 1.0 / math.sqrt(windows * 2 * (nbins - 1))
+    share, lanes = cross_ref.shape[0], pieces[0].shape[-1]
+    first = iota((lag_ref.shape[0], lanes), 1) // (2 * share) == here >> 1
 
     def one_source(index, carry):
-        both = jnp.dot(lag_ref[...], cross_ref[index], preferred_element_type=jnp.float32)
-        rows = both.shape[0] // 2
-        lagged = (both[:rows] + both[rows:])[:L].astype(jnp.bfloat16)
+        lagged = jnp.dot(lag_ref[...], cross_ref[index], preferred_element_type=jnp.float32) * norm
+        early, late = lagged[:, :lanes], lagged[:, lanes:]
+        rounds = [jnp.where(first, early, late), pltpu.roll(jnp.where(first, late, early), lanes // 2, 1)]
         for r in range(ROUNDS):
-            out_ref[r, index] = lagged[:, r * lanes : (r + 1) * lanes]
+            lagged_ref[r, pl.ds(index, lagged.shape[0], stride=share), :] = rounds[r]
         return carry
 
-    lax.fori_loop(0, share, one_source, 0)
+    lax.fori_loop(0, share, one_source, 0, unroll=4)
+    for r in range(ROUNDS):
+        out_ref[r] = lagged_ref[r, pl.ds(0, L * share), :].astype(jnp.bfloat16).reshape(L, share, lanes)
 
 
 def swap(value, axis, mask):
     return lax.ppermute(value, axis, [(i, i ^ mask) for i in range(lax.axis_size(axis))])
 
 
-def call(kernel, outs, operands, scratch, name, specs=None, **grid):
+def call(kernel, outs, operands, scratch, name, specs=None, traffic=1000, **grid):
     return pl.pallas_call(
         kernel,
+        cost_estimate=pl.CostEstimate(flops=0, bytes_accessed=traffic, transcendentals=0),
         out_shape=outs,
         in_specs=specs,
         scratch_shapes=scratch,
@@ -326,8 +359,12 @@
     )(*operands)
 
 
+def after(value, *earlier):
+    return lax.optimization_barrier((value, *earlier))[0]
+
+
 def make_branch(case):
-    near, far = (case, 1 - case) if case < 2 else (None, None)
+    one, other = (case, 1 - case) if case < 2 else (None, None)
 
     def branch(spectra, channel_slot, partners, here):
         chans, nbins = spectra.shape[2:]
@@ -338,39 +375,99 @@
         piece = (n_grp, pairs * K16, chans)
         win = lax.axis_index("win")
         if case < 2:
-            far_first = [[(2, near)], [(2, None)], [(2, 2)], [(2, far)]]
+            layout = [[(2, one), (2, None)], [(2, 2), (2, other)]]
         else:
-            far_first = [[(2, 0), (2, 1)], [(3, None)], [(2, None)]]
-        layout = far_first + [[(1, 0), (1, 1)], [(1, None)], [(0, 0), (0, 1)], [(0, None)]]
+            layout = [[(2, None), (3, None)], [(2, 0), (2, 1)]]
+        layout += [[(1, 0), (1, 1), (1, None)], [(0, 0), (0, 1)], [(0, None)]]
         vmem, smem = pl.BlockSpec(memory_space=pltpu.VMEM), pl.BlockSpec(memory_space=pltpu.SMEM)
-        messages = call(
+        far_a, far_b, near, own, own_src = call(
             lambda *refs: pack_kernel(layout, nbins, *refs),
             [jax.ShapeDtypeStruct((len(m),) + piece, jnp.bfloat16) for m in layout],
-            (here, partners, channel_slot.reshape(1, chans), spectra.reshape(2, -1, nbins)),
-            [pltpu.VMEM((chans, 2 * LANES), jnp.float32), pltpu.VMEM((4,) + piece, jnp.bfloat16)],
+            (here, partners, channel_slot.reshape(1, chans), spectra.transpose(1, 3, 0, 2)),
+            [
+                pltpu.VMEM((4, spectra.shape[1] * 2 * nbins + 4 * K16, chans), jnp.float32),
+                pltpu.VMEM((4,) + piece, jnp.bfloat16),
+            ],
             "pack",
             [smem, smem, vmem, vmem],
         )
-        far_sent, (near_sent, near_src, own, own_src) = messages[:-4], messages[-4:]
-        far_got = [swap(m, "blk", 2) for m in far_sent]
-        near_got = swap(near_sent, "blk", 1)
-        near_src_got = swap(near_src, "blk", 1)
-        if case < 2:
-            relayed = [swap(far_got[i], "blk", 1) for i in (1, 0, 2)]
-            src = [own_src, near_src_got, far_got[1], relayed[1]]
-            held = {(far, 2): (far_got[3], 0), (near, 2): (far_got[0], 0)}
-            held |= {(far, 3): (relayed[2], 0), (near, 3): (relayed[0], 0)}
-        else:
-            relayed = [swap(far_got[i], "blk", 1) for i in (0, 1)]
-            src = [own_src, near_src_got, far_got[2], relayed[1]]
-            held = {(r, 2): (far_got[0], r) for r in range(2)} | {(r, 3): (relayed[0], 1 - r) for r in range(2)}
-        held |= {(r, 0): (own, r) for r in range(2)} | {(r, 1): (near_got, r) for r in range(2)}
         z = here[0]
         mine = (z >> 1) == (win >> 1)
+        got_1 = swap(near, "blk", 1)
+        got_a = swap(far_a, "blk", 2)
+        over_0 = swap(own, "win", 2)
+        over_1 = swap(after(got_1[:2], over_0), "win", 2)
+        got_b = swap(after(far_b, got_a), "blk", 2)
+        core_2b = swap(got_b, "win", 1)
+        if case < 2:
+            got_3a = swap(got_a, "blk", 1)
+            over_2a = swap(got_a[:1], "win", 2)
+            got_3b = swap(after(got_b[:1], core_2b), "blk", 1)
+            src = [own_src, got_1[2:], got_a[1:], after(got_3a[:1], over_1, over_2a)]
+        else:
+            got_3a = swap(got_a[1:], "blk", 1)
+            got_3b = swap(after(got_b, core_2b), "blk", 1)
+            src = [own_src, got_1[2:], got_a[:1], after(got_3a, over_1)]
+        high = [jnp.where(mine, src[d + 2], src[d]) for d in range(2)]
+        across = swap(jnp.concatenate(high, axis=0), "win", 2)
         low = [jnp.where(mine, src[d], src[d + 2]) for d in range(2)]
-        high = [jnp.where(mine, src[d + 2], src[d]) for d in range(2)]
+        if case < 2:
+            over_2b = swap(got_b[1:], "win", 2)
+            over_3a = swap(got_3a[1:], "win", 2)
+            over_3b = None
+            arrays = {
+                "2a": [got_a, over_2a],
+                "3a": [got_3a, over_3a],
+                "2b": [got_b, over_2b],
+                "3b": [got_3b, over_3b],
+            }
+            held = {(other, 2): ("2b", (1, 0)), (one, 2): ("2a", (0, 0))}
+            held |= {(other, 3): ("3b", (0, 0)), (one, 3): ("3a", (1, 0))}
+        else:
+            over_2b = swap(got_b, "win", 2)
+            over_3b = None
+            arrays = {"2b": [got_b, over_2b], "3b": [got_3b, over_3b]}
+            held = {(r, 2): ("2b", (r, r)) for r in range(2)} | {(r, 3): ("3b", (1 - r, 1 - r)) for r in range(2)}
+        arrays |= {0: [own, over_0], 1: [got_1, over_1]}
+        held |= {(r, d): (d, (r, r)) for r in range(2) for d in range(2)}
+        def doubled(name, last=()):
+            held_here, over = arrays[name]
+            core_here = core_2b if name == "2b" else swap(held_here, "win", 1)
+            arrays[name] = [held_here, core_here, over, swap(after(over, *last) if last else over, "win", 1)]
+
+        def places_of(phase):
+            names = list(dict.fromkeys(held[r, d][0] for r in range(ROUNDS) for d in (2 * phase, 2 * phase + 1)))
+            places = [[] for _ in range(4)]
+            for r in range(ROUNDS):
+                for d in (2 * phase, 2 * phase + 1):
+                    name, (whole, part) = held[r, d]
+                    for e in range(4):
+                        size = arrays[name][e].shape[0]
+                        index = whole if size == arrays[name][0].shape[0] else part
+                        places[e].append((4 * names.index(name) + e, index))
+            return places, [array for name in names for array in arrays[name]]
+
+        for name in (0, 1):
+            doubled(name)
+        lag = jnp.asarray(lag_matrix(nbins))
+        taken = [
+            pltpu.VMEM((n_grp, 2, pairs * 16, K8, chans), jnp.float32),
+            pltpu.VMEM((n_grp * K16 + 2 * K8, chans), jnp.float32),
+            pltpu.VMEM((n_grp, 2, K8, chans), jnp.float32),
+        ]
+        early_places, early_pieces = places_of(0)
+        early = call(
+            lambda *refs: receive_kernel(early_places, nbins, windows, *refs),
+            jax.ShapeDtypeStruct((2 * n_grp, pairs * 16 * K8, chans), jnp.bfloat16),
+            (here, *early_pieces),
+            taken,
+            "receivers",
+            [smem] + [vmem] * len(early_pieces),
+            traffic=12 * 2**20,
+        )
+        over_3b = swap(got_3b, "win", 2)
+        across = after(across, got_3b, early)
         odd = ((win ^ z) & 1) == 1
-        across = swap(jnp.concatenate(high, axis=0), "win", 2)
         first, second = low, [across[0:1], across[1:2]]
         sources = []
         for two in (first, second):
@@ -386,43 +483,40 @@
             ],
             "sources",
             [vmem] * 4,
+            traffic=20 * 2**20,
             grid=(n_grp,),
             out_specs=pl.BlockSpec((2, share * 2 * K8, pairs * chans), lambda i: (i, 0, 0)),
         )
-        pieces, places = [], [[[None] * 4 for _ in range(4)] for _ in range(ROUNDS)]
-        gathered = {}
-        for r in range(ROUNDS):
-            for d in range(4):
-                array, index = held[r, d]
-                if id(array) not in gathered:
-                    over = swap(array, "win", 2)
-                    gathered[id(array)] = (len(pieces), array)
-                    pieces += [array, swap(array, "win", 1), over, swap(over, "win", 1)]
-                for e in range(4):
-                    places[r][d][e] = (gathered[id(array)][0] + e, index)
-        lag = jnp.asarray(lag_matrix(nbins, windows))
-        return call(
-            lambda *refs: correlate_kernel(places, nbins, windows, *refs),
-            jax.ShapeDtypeStruct((ROUNDS, share, L, chans), jnp.bfloat16),
-            (here, left, lag, *pieces),
+        arrays["3b"] = [got_3b, over_3b]
+        for name in list(arrays):
+            if name not in (0, 1):
+                doubled(name, [left] if name == "3b" else [])
+        late_places, late_pieces = places_of(1)
+        hbm = pl.BlockSpec(memory_space=pl.ANY)
+        by_lag = call(
+            lambda *refs: correlate_kernel(late_places, nbins, windows, *refs),
+            jax.ShapeDtypeStruct((ROUNDS, L, share, chans), jnp.bfloat16),
+            (here, left, early, lag, *late_pieces),
             [
                 pltpu.VMEM(left.shape, jnp.bfloat16),
-                pltpu.VMEM((n_grp, 2, pairs * 16, K8, ROUNDS * chans), jnp.float32),
+                pltpu.VMEM(early.shape, jnp.bfloat16),
+                taken[0],
                 pltpu.VMEM((share, n_grp * 4 * K8, ROUNDS * chans), jnp.bfloat16),
-                pltpu.VMEM((n_grp * K16 + 2 * K8, ROUNDS * chans), jnp.float32),
-                pltpu.VMEM((n_grp, 2, K8, ROUNDS * chans), jnp.float32),
-                pltpu.SemaphoreType.DMA,
+                pltpu.VMEM((ROUNDS, lag.shape[0] * share, chans), jnp.float32),
+                *taken[1:],
+                pltpu.SemaphoreType.DMA((2,)),
             ],
             "correlate",
-            [smem, pl.BlockSpec(memory_space=pl.ANY)] + [vmem] * (1 + len(pieces)),
+            [smem, hbm, hbm] + [vmem] * (1 + len(late_pieces)),
         )
+        return by_lag.transpose(0, 2, 1, 3)
 
     return branch
 
 
 def gathering_body(spectra, channel_slot, partners):
     here = lax.axis_index("blk")
-    masks = partners[:, here] ^ here
+    masks = partners[:, 0]
     case = jnp.where(masks[0] == 1, 0, jnp.where(masks[1] == 1, 1, 2))
     branches = [make_branch(i) for i in range(3)]
     return lax.switch(case, branches, spectra, channel_slot, partners, here.reshape(1))

time: 115 us -> 97 us (0.84)
  starting transfers between devices: 30 us -> 21.6 us
  waiting for transfers between devices: 36.8 us -> 30 us
  local copies, waits for them, and re-layouts: 8.34 us -> 4.36 us
  Pallas kernels: 34.5 us -> 36.4 us
    ppermute x30 -> x26, starting transfers between devices: 30 us -> 21.6 us  [swap(): lax.ppermute(value, axis, [(i, i ^ mask) for i in range(lax.axis_size(axi...]
    ppermute x30 -> x26, waiting for transfers between devices: 36.8 us -> 30 us  [swap(): lax.ppermute(value, axis, [(i, i ^ mask) for i in range(lax.axis_size(axi...]
    another operation x1 -> x0, local copies, waits for them, and re-layouts: 3.01 us -> none
    pallas_call x3 -> x4, Pallas kernels: 34.5 us -> 36.4 us  [call(): pl.pallas_call(kernel, cost_estimate=pl.CostEstimate(flops=0, bytes_acces...]
    cond x51 -> x50, local copies, waits for them, and re-layouts: 3.65 us -> 1.82 us
  transfers between devices with their start and end apart: 30 -> 26, of which waited for: 10 -> 10; matrix products, arithmetic and copies ran while one was open for 2% -> 3% of each run, Pallas kernels for 9% -> 17%
where the time goes in v1:
time: 97 us; the launch traced here: 96.6 us
  Pallas kernels  36.4 us (38%)
  waiting for transfers between devices  30 us (31%)
  starting transfers between devices  21.6 us (22%)
  local copies, waits for them, and re-layouts  4.36 us (4%)
  other arithmetic  2.47 us (3%)
  between operations  1.29 us (1%)
    pallas_call x4, Pallas kernels, call(): pl.pallas_call(kernel, cost_estimate=pl.CostEstimate(flops=0, bytes_acces...  36.4 us
    ppermute x26, waiting for transfers between devices, swap(): lax.ppermute(value, axis, [(i, i ^ mask) for i in range(lax.axis_size(axi...  30 us
    ppermute x26, starting transfers between devices, swap(): lax.ppermute(value, axis, [(i, i ^ mask) for i in range(lax.axis_size(axi...  21.6 us
    select_n x2, other arithmetic, branch(): sources.append(swap(jnp.where(odd, two[0], two[1]), 'win', 1))  2.44 us
  transfers between devices with their start and end apart: 26, of which 10 were waited for; matrix products, arithmetic and copies ran while one was open for 3% of the time, Pallas kernels for 17%

profile of v1, /device:TPU:0, one launch (start us, length us, event | category | flops | bytes accessed | tf_op | source)
XLA Modules:
  0.0 96.6 jit_solution(858518064310677912)
XLA Ops:
  0.0 1.3 %fusion.4 = (s32[1,1]{1,0:T(1,128)}, s32[1,1]{1,0:T(1,128)}) fusion(s32[2,4]{1,0:T(2,128)} %param.11), kind=kLoop, calls=%fused_computation.31 | loop fusion | bytes 16 | tf_op jit(solution)/shard_map/slice | solution.py:520
  2.6 92.8 %conditional.1 = (bf16[2,32,101,128]{3,1,2,0:T(8,128)(2,1)S(1)}) conditional(s32[]{:T(128)} %bitcast.12, (s32[]{:T(128)}, s32[128]{0:T(128)}, bf16[2,6,128,201]{2,0,3,1:T(2,128)(2,1)}, s32[]{:T(128)}, s32[2,4]{1,0:T(2,128)}, /*index=5*/()) %tuple.32, (s32[]{:T(128)}, s32[128]{0:T(128)}, bf16[2,6,128,201]{2,0,3,1:T(2,128)(2,1)}, ...), branch_computations={%region_0.1_spmd, %region_1.2_spmd, %region_2.3_spmd} | conditional | flops 798728 | bytes 90746584 | solution.py:522
  2.6 3.2 %pack.3 = (bf16[2,13,48,128]{3,2,1,0:T(8,128)(2,1)}, bf16[2,13,48,128]{3,2,1,0:T(8,128)(2,1)}, bf16[3,13,48,128]{3,2,1,0:T(8,128)(2,1)}, bf16[2,13,48,128]{3,2,1,0:T(8,128)(2,1)}, bf16[1,13,48,128]{3,2,1,0:T(8,128)(2,1)}) custom-call(s32[1]{0:T(128)} %bitcast.refs_0_, s32[2,4]{1,0:T(2,128)} %get-tuple-element.47.refs_1_, s32[1,128]{1,0:T(1,128)} %bitcast.19, ...), custom_call_target="tpu_custom_call" | custom-call | bytes 1000 | tf_op jit(solution)/shard_map/cond/branch_0_fun/pack/pallas_call | solution.py:350
  5.8 4.0 %collective-permute-start.21 = (bf16[2,13,48,128]{3,2,1,0:T(8,128)(2,1)}, bf16[2,13,48,128]{3,2,1,0:T(8,128)(2,1)S(1)}, u32[]{:S(2)}, u32[]{:S(2)}) collective-permute-start(bf16[2,13,48,128]{3,2,1,0:T(8,128)(2,1)} %get-tuple-element.51), channel_id=1, source_target_pairs={{0,8},{4,12},{8,0},{12,4},{1,9},{5,13},{9,1},{13,5},{2,10},{6,14},... | collective-permute-start | bytes 958472 | tf_op jit(solution)/shard_map/cond/branch_0_fun/ppermute | solution.py:346
  9.9 1.6 %collective-permute-start.20 = (bf16[3,13,48,128]{3,2,1,0:T(8,128)(2,1)}, bf16[3,13,48,128]{3,2,1,0:T(8,128)(2,1)S(1)}, u32[]{:S(2)}, u32[]{:S(2)}) collective-permute-start(bf16[3,13,48,128]{3,2,1,0:T(8,128)(2,1)} %get-tuple-element.50), channel_id=1, source_target_pairs={{0,4},{4,0},{8,12},{12,8},{1,5},{5,1},{9,13},{13,9},{2,6},{6,2},{1... | collective-permute-start | bytes 1437704 | tf_op jit(solution)/shard_map/cond/branch_0_fun/ppermute | solution.py:346
  11.4 1.5 %collective-permute-start.23 = (bf16[2,13,48,128]{3,2,1,0:T(8,128)(2,1)}, bf16[2,13,48,128]{3,2,1,0:T(8,128)(2,1)S(1)}, u32[]{:S(2)}, u32[]{:S(2)}) collective-permute-start(bf16[2,13,48,128]{3,2,1,0:T(8,128)(2,1)} %get-tuple-element.52.refs_1_), channel_id=1, source_target_pairs={{0,2},{1,3},{2,0},{3,1},{4,6},{5,7},{6,4},{7,5},{8,10},{9,11},{10,... | collective-permute-start | bytes 958472 | tf_op jit(solution)/shard_map/cond/branch_0_fun/ppermute | solution.py:346
  12.9 11.6 %collective-permute-done.21.refs_4_ = bf16[2,13,48,128]{3,2,1,0:T(8,128)(2,1)S(1)} collective-permute-done((bf16[2,13,48,128]{3,2,1,0:T(8,128)(2,1)}, bf16[2,13,48,128]{3,2,1,0:T(8,128)(2,1)S(1)}, u32[]{:S(2)}, u32[]{:S(2)}) %collective-permute-start.21) | collective-permute-done | bytes 319520 | tf_op jit(solution)/shard_map/cond/branch_0_fun/ppermute | solution.py:346
  24.6 0.8 collective-permute-start.22
  25.3 3.3 %collective-permute-start.28 = (bf16[2,13,48,128]{3,2,1,0:T(8,128)(2,1)}, bf16[2,13,48,128]{3,2,1,0:T(8,128)(2,1)S(1)}, u32[]{:S(2)}, u32[]{:S(2)}) collective-permute-start(bf16[2,13,48,128]{3,2,1,0:T(8,128)(2,1)} %get-tuple-element.57), channel_id=1, source_target_pairs={{0,8},{4,12},{8,0},{12,4},{1,9},{5,13},{9,1},{13,5},{2,10},{6,14},... | collective-permute-start | bytes 958472 | tf_op jit(solution)/shard_map/cond/branch_0_fun/ppermute | solution.py:346
  28.7 6.9 %collective-permute-done.20.refs_5_ = bf16[3,13,48,128]{3,2,1,0:T(8,128)(2,1)S(1)} collective-permute-done((bf16[3,13,48,128]{3,2,1,0:T(8,128)(2,1)}, bf16[3,13,48,128]{3,2,1,0:T(8,128)(2,1)S(1)}, u32[]{:S(2)}, u32[]{:S(2)}) %collective-permute-start.20) | collective-permute-done | bytes 479264 | tf_op jit(solution)/shard_map/cond/branch_0_fun/ppermute | solution.py:346
  35.6 0.0 collective-permute-done.23.refs_3_
  35.6 1.7 %collective-permute-start.24 = (bf16[2,13,48,128]{3,2,1,0:T(8,128)(2,1)S(1)}, bf16[2,13,48,128]{3,2,1,0:T(8,128)(2,1)S(1)}, u32[]{:S(2)}, u32[]{:S(2)}) collective-permute-start(bf16[2,13,48,128]{3,2,1,0:T(8,128)(2,1)S(1)} %slice.93), channel_id=1, source_target_pairs={{0,2},{1,3},{2,0},{3,1},{4,6},{5,7},{6,4},{7,5},{8,10},{9,11},{10,... | collective-permute-start | bytes 958472 | tf_op jit(solution)/shard_map/cond/branch_0_fun/ppermute | solution.py:346
  37.3 0.0 collective-permute-start.31
  37.3 0.5 collective-permute-start.25
  37.8 3.7 %collective-permute-done.22.refs_8_ = bf16[2,13,48,128]{3,2,1,0:T(8,128)(2,1)S(1)} collective-permute-done((bf16[2,13,48,128]{3,2,1,0:T(8,128)(2,1)S(1)}, bf16[2,13,48,128]{3,2,1,0:T(8,128)(2,1)S(1)}, u32[]{:S(2)}, u32[]{:S(2)}) %collective-permute-start.22) | collective-permute-done | bytes 319520 | tf_op jit(solution)/shard_map/cond/branch_0_fun/ppermute | solution.py:346
  41.5 0.0 collective-permute-start.32
  41.5 4.6 %collective-permute-done.25.refs_6_ = bf16[1,13,48,128]{3,2,1,0:T(8,128)(2,1)S(1)} collective-permute-done((bf16[1,13,48,128]{3,2,1,0:T(8,128)(2,1)S(1)}, bf16[1,13,48,128]{3,2,1,0:T(8,128)(2,1)S(1)}, u32[]{:S(2)}, u32[]{:S(2)}) %collective-permute-start.25) | collective-permute-done | bytes 159776 | tf_op jit(solution)/shard_map/cond/branch_0_fun/ppermute | solution.py:346
  46.1 0.0 collective-permute-start.33
  46.1 0.0 collective-permute-done.28.refs_12_
  46.1 0.5 collective-permute-start.29
  46.6 0.0 collective-permute-done.24.refs_7_
  46.6 1.7 %broadcast_select_fusion.6 = (bf16[1,13,48,128]{3,2,1,0:T(8,128)(2,1)S(1)}, bf16[1,13,48,128]{3,2,1,0:T(8,128)(2,1)}, bf16[1,13,48,128]{3,2,1,0:T(8,128)(2,1)S(1)}, bf16[1,13,48,128]{3,2,1,0:T(8,128)(2,1)S(1)}) fusion(pred[]{:T(512)S(6)} %eq.18, bf16[1,13,48,128]{3,2,1,0:T(8,128)(2,1)S(1)} %get-tuple-element.54, ...), kind=kLoop, calls=%fused_computation.7 | loop fusion | flops 479232 | bytes 1277954 | tf_op jit(solution)/shard_map/cond/branch_0_fun/jit(_where)/select_n | solution.py:475
  48.4 1.7 %collective-permute-start.27 = (bf16[2,13,48,128]{3,2,1,0:T(8,128)(2,1)S(1)}, bf16[2,13,48,128]{3,2,1,0:T(8,128)(2,1)S(1)}, u32[]{:S(2)}, u32[]{:S(2)}) collective-permute-start(bf16[2,13,48,128]{3,2,1,0:T(8,128)(2,1)S(1)} %pad_maximum_fusion), channel_id=1, source_target_pairs={{0,2},{1,3},{2,0},{3,1},{4,6},{5,7},{6,4},{7,5},{8,10},{9,11},{10,... | collective-permute-start | bytes 958472 | tf_op jit(solution)/shard_map/cond/branch_0_fun/ppermute | solution.py:346
  50.1 0.0 collective-permute-done.29.refs_13_
  50.1 0.0 collective-permute-start.34
  50.1 0.0 collective-permute-done.31.refs_2_
  50.2 0.1 collective-permute-start.30
  50.3 0.5 collective-permute-start.41
  50.7 0.0 collective-permute-done.33.refs_6_
  50.8 0.2 collective-permute-start.26
  51.0 0.7 collective-permute-done.34.refs_8_
  51.8 0.7 copy-done.25
  52.5 5.3 %receivers.3.refs_2_ = bf16[26,384,128]{2,1,0:T(8,128)(2,1)} custom-call(s32[1]{0:T(128)} %bitcast.refs_0_, bf16[2,13,48,128]{3,2,1,0:T(8,128)(2,1)} %get-tuple-element.52.refs_1_, bf16[2,13,48,128]{3,2,1,0:T(8,128)(2,1)} %copy-done.18, bf16[2,13,48,128]{3,2,1,0:T(8,128)(2,1)} %copy-done.13, bf16[2,13,48,128]{3,2,1,0:T(8,128)(2,1)} %copy-done.22, ...), custom_call_target="tpu_custom_call" | custom-call | bytes 12582912 | tf_op jit(solution)/shard_map/cond/branch_0_fun/receivers/pallas_call | solution.py:350
  57.8 0.0 collective-permute-done.30.refs_16_
  57.8 1.1 %collective-permute-done.27 = bf16[2,13,48,128]{3,2,1,0:T(8,128)(2,1)S(1)} collective-permute-done((bf16[2,13,48,128]{3,2,1,0:T(8,128)(2,1)S(1)}, bf16[2,13,48,128]{3,2,1,0:T(8,128)(2,1)S(1)}, u32[]{:S(2)}, u32[]{:S(2)}) %collective-permute-start.27) | collective-permute-done | bytes 319520 | tf_op jit(solution)/shard_map/cond/branch_0_fun/ppermute | solution.py:346
  58.9 0.7 broadcast_select_fusion.4
  59.6 0.5 collective-permute-start.36
  60.1 1.6 %collective-permute-start.39 = (bf16[1,13,48,128]{3,2,1,0:T(8,128)(2,1)S(1)}, bf16[1,13,48,128]{3,2,1,0:T(8,128)(2,1)S(1)}, u32[]{:S(2)}, u32[]{:S(2)}) collective-permute-start(bf16[1,13,48,128]{3,2,1,0:T(8,128)(2,1)S(1)} %get-tuple-element.124), channel_id=1, source_target_pairs={{0,2},{1,3},{2,0},{3,1},{4,6},{5,7},{6,4},{7,5},{8,10},{9,11},{10,... | collective-permute-start | bytes 479240 | tf_op jit(solution)/shard_map/cond/branch_0_fun/ppermute | solution.py:346
  61.7 0.0 collective-permute-done.41.refs_14_
  61.7 1.4 %collective-permute-start.44 = (bf16[1,13,48,128]{3,2,1,0:T(8,128)(2,1)S(1)}, bf16[1,13,48,128]{3,2,1,0:T(8,128)(2,1)S(1)}, u32[]{:S(2)}, u32[]{:S(2)}) collective-permute-start(bf16[1,13,48,128]{3,2,1,0:T(8,128)(2,1)S(1)} %collective-permute-done.30.refs_16_), channel_id=1, source_target_pairs={{0,2},{1,3},{2,0},{3,1},{4,6},{5,7},{6,4},{7,5},{8,10},{9,11},{10,... | collective-permute-start | bytes 479240 | tf_op jit(solution)/shard_map/cond/branch_0_fun/ppermute | solution.py:346
  63.1 0.1 collective-permute-start.37
  63.2 0.0 collective-permute-done.35.refs_3_
  63.2 0.5 collective-permute-start.38
  63.7 0.0 copy-done.42
  63.8 0.1 copy-done.45
  63.8 10.9 %sources.3.refs_1_ = bf16[26,512,384]{2,1,0:T(8,128)(2,1)} custom-call(bf16[1,13,48,128]{3,2,1,0:T(8,128)(2,1)} %get-tuple-element.119.refs_0_, bf16[1,13,48,128]{3,2,1,0:T(8,128)(2,1)} %copy-done.42, bf16[1,13,48,128]{3,2,1,0:T(8,128)(2,1)} %get-tuple-element.127.refs_2_, bf16[1,13,48,128]{3,2,1,0:T(8,128)(2,1)} %copy-done.45), custom_call_target="tpu_custom_call" | custom-call | bytes 20971520 | tf_op jit(solution)/shard_map/cond/branch_0_fun/sources/pallas_call | solution.py:350
  74.7 0.0 collective-permute-done.39.refs_10_
  74.7 0.5 collective-permute-start.42
  75.2 0.1 collective-permute-start.40
  75.3 0.0 collective-permute-done.37.refs_7_
  75.3 0.5 collective-permute-start.43
  75.8 0.0 collective-permute-done.36.refs_5_
  75.8 0.1 collective-permute-start.45
  75.9 0.0 collective-permute-done.38.refs_9_
  75.9 0.3 collective-permute-done.42.refs_15_
  76.2 0.4 collective-permute-done.40.refs_11_
  76.6 0.2 collective-permute-done.43.refs_17_
  76.9 0.4 collective-permute-done.45.refs_19_
  77.3 0.0 copy-done.62
  77.3 0.2 copy-done.64
  77.5 0.7 copy-done.66
  78.2 16.9 %correlate.3 = bf16[2,101,32,128]{3,2,1,0:T(8,128)(2,1)S(1)} custom-call(s32[1]{0:T(128)} %bitcast.refs_0_, bf16[26,512,384]{2,1,0:T(8,128)(2,1)} %sources.3.refs_1_, bf16[26,384,128]{2,1,0:T(8,128)(2,1)} %receivers.3.refs_2_, bf16[104,416]{1,0:T(8,128)(2,1)} %constant.38.clone.1.refs_3_, bf16[2,13,48,128]{3,2,1,0:T(8,128)(2,1)} %copy-done.8, ...), custom_call_target="tpu_custom_call" | custom-call | bytes 1000 | tf_op jit(solution)/shard_map/cond/branch_0_fun/correlate/pallas_call | solution.py:350
  95.4 0.0 copy-start.3
  95.4 1.2 %copy-done.3 = bf16[2,32,101,128]{3,1,2,0:T(8,128)(2,1)} copy-done((bf16[2,32,101,128]{3,1,2,0:T(8,128)(2,1)}, bf16[2,32,101,128]{3,1,2,0:T(8,128)(2,1)S(1)}, u32[]{:S(2)}) %copy-start.3) | copy-done | bytes 1654808
  (53 shorter events, 0.2 us)
Async XLA Ops:
  5.8 18.7 %collective-permute-start.21 = (bf16[2,13,48,128]{3,2,1,0:T(8,128)(2,1)}, bf16[2,13,48,128]{3,2,1,0:T(8,128)(2,1)S(1)}, u32[]{:S(2)}, u32[]{:S(2)}) collective-permute-start(bf16[2,13,48,128]{3,2,1,0:T(8,128)(2,1)} %get-tuple-element.51), channel_id=1, source_target_pairs={{0,8},{4,12},{8,0},{12,4},{1,9},{5,13},{9,1},{13,5},{2,10},{6,14},... | collective-permute-start | bytes 958472 | tf_op jit(solution)/shard_map/cond/branch_0_fun/ppermute | solution.py:346
  9.9 25.7 %collective-permute-start.20 = (bf16[3,13,48,128]{3,2,1,0:T(8,128)(2,1)}, bf16[3,13,48,128]{3,2,1,0:T(8,128)(2,1)S(1)}, u32[]{:S(2)}, u32[]{:S(2)}) collective-permute-start(bf16[3,13,48,128]{3,2,1,0:T(8,128)(2,1)} %get-tuple-element.50), channel_id=1, source_target_pairs={{0,4},{4,0},{8,12},{12,8},{1,5},{5,1},{9,13},{13,9},{2,6},{6,2},{1... | collective-permute-start | bytes 1437704 | tf_op jit(solution)/shard_map/cond/branch_0_fun/ppermute | solution.py:346
  11.4 24.2 %collective-permute-start.23 = (bf16[2,13,48,128]{3,2,1,0:T(8,128)(2,1)}, bf16[2,13,48,128]{3,2,1,0:T(8,128)(2,1)S(1)}, u32[]{:S(2)}, u32[]{:S(2)}) collective-permute-start(bf16[2,13,48,128]{3,2,1,0:T(8,128)(2,1)} %get-tuple-element.52.refs_1_), channel_id=1, source_target_pairs={{0,2},{1,3},{2,0},{3,1},{4,6},{5,7},{6,4},{7,5},{8,10},{9,11},{10,... | collective-permute-start | bytes 958472 | tf_op jit(solution)/shard_map/cond/branch_0_fun/ppermute | solution.py:346
  24.6 35.0 %copy-start.8 = (bf16[2,13,48,128]{3,2,1,0:T(8,128)(2,1)}, bf16[2,13,48,128]{3,2,1,0:T(8,128)(2,1)S(1)}, u32[]{:S(2)}) copy-start(bf16[2,13,48,128]{3,2,1,0:T(8,128)(2,1)S(1)} %collective-permute-done.21.refs_4_) | copy-start | bytes 958468 | tf_op jit(solution)/shard_map/cond
  24.6 16.9 %collective-permute-start.22 = (bf16[2,13,48,128]{3,2,1,0:T(8,128)(2,1)S(1)}, bf16[2,13,48,128]{3,2,1,0:T(8,128)(2,1)S(1)}, u32[]{:S(2)}, u32[]{:S(2)}) collective-permute-start(bf16[2,13,48,128]{3,2,1,0:T(8,128)(2,1)S(1)} %collective-permute-done.21.refs_4_), channel_id=1, source_target_pairs={{0,4},{4,0},{8,12},{12,8},{1,5},{5,1},{9,13},{13,9},{2,6},{6,2},{1... | collective-permute-start | bytes 958472 | tf_op jit(solution)/shard_map/cond/branch_0_fun/ppermute | solution.py:346
  25.3 20.8 %collective-permute-start.28 = (bf16[2,13,48,128]{3,2,1,0:T(8,128)(2,1)}, bf16[2,13,48,128]{3,2,1,0:T(8,128)(2,1)S(1)}, u32[]{:S(2)}, u32[]{:S(2)}) collective-permute-start(bf16[2,13,48,128]{3,2,1,0:T(8,128)(2,1)} %get-tuple-element.57), channel_id=1, source_target_pairs={{0,8},{4,12},{8,0},{12,4},{1,9},{5,13},{9,1},{13,5},{2,10},{6,14},... | collective-permute-start | bytes 958472 | tf_op jit(solution)/shard_map/cond/branch_0_fun/ppermute | solution.py:346
  35.6 16.1 %copy-start = (bf16[3,13,48,128]{3,2,1,0:T(8,128)(2,1)}, bf16[3,13,48,128]{3,2,1,0:T(8,128)(2,1)S(1)}, u32[]{:S(2)}) copy-start(bf16[3,13,48,128]{3,2,1,0:T(8,128)(2,1)S(1)} %collective-permute-done.20.refs_5_) | copy-start | bytes 1437700 | tf_op jit(solution)/shard_map/cond
  35.6 16.1 %copy-start.13 = (bf16[2,13,48,128]{3,2,1,0:T(8,128)(2,1)}, bf16[2,13,48,128]{3,2,1,0:T(8,128)(2,1)S(1)}, u32[]{:S(2)}) copy-start(bf16[2,13,48,128]{3,2,1,0:T(8,128)(2,1)S(1)} %collective-permute-done.23.refs_3_) | copy-start | bytes 958468 | tf_op jit(solution)/shard_map/cond
  35.6 11.0 %collective-permute-start.24 = (bf16[2,13,48,128]{3,2,1,0:T(8,128)(2,1)S(1)}, bf16[2,13,48,128]{3,2,1,0:T(8,128)(2,1)S(1)}, u32[]{:S(2)}, u32[]{:S(2)}) collective-permute-start(bf16[2,13,48,128]{3,2,1,0:T(8,128)(2,1)S(1)} %slice.93), channel_id=1, source_target_pairs={{0,2},{1,3},{2,0},{3,1},{4,6},{5,7},{6,4},{7,5},{8,10},{9,11},{10,... | collective-permute-start | bytes 958472 | tf_op jit(solution)/shard_map/cond/branch_0_fun/ppermute | solution.py:346
  37.3 12.8 %collective-permute-start.31 = (bf16[2,13,48,128]{3,2,1,0:T(8,128)(2,1)}, bf16[2,13,48,128]{3,2,1,0:T(8,128)(2,1)S(1)}, u32[]{:S(2)}, u32[]{:S(2)}) collective-permute-start(bf16[2,13,48,128]{3,2,1,0:T(8,128)(2,1)} %get-tuple-element.52.refs_1_), channel_id=1, source_target_pairs={{0,1},{1,0},{2,3},{3,2},{4,5},{5,4},{6,7},{7,6},{8,9},{9,8},{10,11... | collective-permute-start | bytes 958472 | tf_op jit(solution)/shard_map/cond/branch_0_fun/ppermute | solution.py:346
  37.3 8.8 %collective-permute-start.25 = (bf16[1,13,48,128]{3,2,1,0:T(8,128)(2,1)S(1)}, bf16[1,13,48,128]{3,2,1,0:T(8,128)(2,1)S(1)}, u32[]{:S(2)}, u32[]{:S(2)}) collective-permute-start(bf16[1,13,48,128]{3,2,1,0:T(8,128)(2,1)S(1)} %slice.94), channel_id=1, source_target_pairs={{0,2},{1,3},{2,0},{3,1},{4,6},{5,7},{6,4},{7,5},{8,10},{9,11},{10,... | collective-permute-start | bytes 479240 | tf_op jit(solution)/shard_map/cond/branch_0_fun/ppermute | solution.py:346
  41.5 21.7 %copy-start.4 = (bf16[2,13,48,128]{3,2,1,0:T(8,128)(2,1)}, bf16[2,13,48,128]{3,2,1,0:T(8,128)(2,1)S(1)}, u32[]{:S(2)}) copy-start(bf16[2,13,48,128]{3,2,1,0:T(8,128)(2,1)S(1)} %collective-permute-done.22.refs_8_) | copy-start | bytes 958468 | tf_op jit(solution)/shard_map/cond
  41.5 8.7 %collective-permute-start.32 = (bf16[2,13,48,128]{3,2,1,0:T(8,128)(2,1)S(1)}, bf16[2,13,48,128]{3,2,1,0:T(8,128)(2,1)S(1)}, u32[]{:S(2)}, u32[]{:S(2)}) collective-permute-start(bf16[2,13,48,128]{3,2,1,0:T(8,128)(2,1)S(1)} %collective-permute-done.23.refs_3_), channel_id=1, source_target_pairs={{0,1},{1,0},{2,3},{3,2},{4,5},{5,4},{6,7},{7,6},{8,9},{9,8},{10,11... | collective-permute-start | bytes 958472 | tf_op jit(solution)/shard_map/cond/branch_0_fun/ppermute | solution.py:346
  46.1 17.0 %copy-start.48 = (bf16[1,13,48,128]{3,2,1,0:T(8,128)(2,1)}, bf16[1,13,48,128]{3,2,1,0:T(8,128)(2,1)S(1)}, u32[]{:S(2)}) copy-start(bf16[1,13,48,128]{3,2,1,0:T(8,128)(2,1)S(1)} %collective-permute-done.25.refs_6_) | copy-start | bytes 479236 | tf_op jit(solution)/shard_map/cond
  46.1 4.6 %collective-permute-start.33 = (bf16[3,13,48,128]{3,2,1,0:T(8,128)(2,1)S(1)}, bf16[3,13,48,128]{3,2,1,0:T(8,128)(2,1)S(1)}, u32[]{:S(2)}, u32[]{:S(2)}) collective-permute-start(bf16[3,13,48,128]{3,2,1,0:T(8,128)(2,1)S(1)} %collective-permute-done.20.refs_5_), channel_id=1, source_target_pairs={{0,1},{1,0},{2,3},{3,2},{4,5},{5,4},{6,7},{7,6},{8,9},{9,8},{10,11... | collective-permute-start | bytes 1437704 | tf_op jit(solution)/shard_map/cond/branch_0_fun/ppermute | solution.py:346
  46.1 11.7 %copy-start.6 = (bf16[2,13,48,128]{3,2,1,0:T(8,128)(2,1)}, bf16[2,13,48,128]{3,2,1,0:T(8,128)(2,1)S(1)}, u32[]{:S(2)}) copy-start(bf16[2,13,48,128]{3,2,1,0:T(8,128)(2,1)S(1)} %collective-permute-done.28.refs_12_) | copy-start | bytes 958468 | tf_op jit(solution)/shard_map/cond
  46.1 4.0 %collective-permute-start.29 = (bf16[2,13,48,128]{3,2,1,0:T(8,128)(2,1)S(1)}, bf16[2,13,48,128]{3,2,1,0:T(8,128)(2,1)S(1)}, u32[]{:S(2)}, u32[]{:S(2)}) collective-permute-start(bf16[2,13,48,128]{3,2,1,0:T(8,128)(2,1)S(1)} %collective-permute-done.28.refs_12_), channel_id=1, source_target_pairs={{0,1},{1,0},{2,3},{3,2},{4,5},{5,4},{6,7},{7,6},{8,9},{9,8},{10,11... | collective-permute-start | bytes 958472 | tf_op jit(solution)/shard_map/cond/branch_0_fun/ppermute | solution.py:346
  46.6 5.1 %copy-start.16 = (bf16[2,13,48,128]{3,2,1,0:T(8,128)(2,1)}, bf16[2,13,48,128]{3,2,1,0:T(8,128)(2,1)S(1)}, u32[]{:S(2)}) copy-start(bf16[2,13,48,128]{3,2,1,0:T(8,128)(2,1)S(1)} %collective-permute-done.24.refs_7_) | copy-start | bytes 958468 | tf_op jit(solution)/shard_map/cond
  48.4 10.5 %collective-permute-start.27 = (bf16[2,13,48,128]{3,2,1,0:T(8,128)(2,1)S(1)}, bf16[2,13,48,128]{3,2,1,0:T(8,128)(2,1)S(1)}, u32[]{:S(2)}, u32[]{:S(2)}) collective-permute-start(bf16[2,13,48,128]{3,2,1,0:T(8,128)(2,1)S(1)} %pad_maximum_fusion), channel_id=1, source_target_pairs={{0,2},{1,3},{2,0},{3,1},{4,6},{5,7},{6,4},{7,5},{8,10},{9,11},{10,... | collective-permute-start | bytes 958472 | tf_op jit(solution)/shard_map/cond/branch_0_fun/ppermute | solution.py:346
  50.1 7.7 %copy-start.29 = (bf16[2,13,48,128]{3,2,1,0:T(8,128)(2,1)}, bf16[2,13,48,128]{3,2,1,0:T(8,128)(2,1)S(1)}, u32[]{:S(2)}) copy-start(bf16[2,13,48,128]{3,2,1,0:T(8,128)(2,1)S(1)} %collective-permute-done.29.refs_13_) | copy-start | bytes 958468 | tf_op jit(solution)/shard_map/cond
  50.1 1.6 %collective-permute-start.34 = (bf16[2,13,48,128]{3,2,1,0:T(8,128)(2,1)S(1)}, bf16[2,13,48,128]{3,2,1,0:T(8,128)(2,1)S(1)}, u32[]{:S(2)}, u32[]{:S(2)}) collective-permute-start(bf16[2,13,48,128]{3,2,1,0:T(8,128)(2,1)S(1)} %collective-permute-done.24.refs_7_), channel_id=1, source_target_pairs={{0,1},{1,0},{2,3},{3,2},{4,5},{5,4},{6,7},{7,6},{8,9},{9,8},{10,11... | collective-permute-start | bytes 958472 | tf_op jit(solution)/shard_map/cond/branch_0_fun/ppermute | solution.py:346
  50.2 1.6 %copy-start.18 = (bf16[2,13,48,128]{3,2,1,0:T(8,128)(2,1)}, bf16[2,13,48,128]{3,2,1,0:T(8,128)(2,1)S(1)}, u32[]{:S(2)}) copy-start(bf16[2,13,48,128]{3,2,1,0:T(8,128)(2,1)S(1)} %collective-permute-done.31.refs_2_) | copy-start | bytes 958468 | tf_op jit(solution)/shard_map/cond
  50.2 7.7 %collective-permute-start.30 = (bf16[1,13,48,128]{3,2,1,0:T(8,128)(2,1)S(1)}, bf16[1,13,48,128]{3,2,1,0:T(8,128)(2,1)S(1)}, u32[]{:S(2)}, u32[]{:S(2)}) collective-permute-start(bf16[1,13,48,128]{3,2,1,0:T(8,128)(2,1)S(1)} %get-tuple-element.58), channel_id=1, source_target_pairs={{0,4},{4,0},{8,12},{12,8},{1,5},{5,1},{9,13},{13,9},{2,6},{6,2},{1... | collective-permute-start | bytes 479240 | tf_op jit(solution)/shard_map/cond/branch_0_fun/ppermute | solution.py:346
  50.3 1.5 %copy-start.22 = (bf16[2,13,48,128]{3,2,1,0:T(8,128)(2,1)}, bf16[2,13,48,128]{3,2,1,0:T(8,128)(2,1)S(1)}, u32[]{:S(2)}) copy-start(bf16[2,13,48,128]{3,2,1,0:T(8,128)(2,1)S(1)} %collective-permute-done.32.refs_4_) | copy-start | bytes 958468 | tf_op jit(solution)/shard_map/cond
  50.3 11.4 %collective-permute-start.41 = (bf16[1,13,48,128]{3,2,1,0:T(8,128)(2,1)S(1)}, bf16[1,13,48,128]{3,2,1,0:T(8,128)(2,1)S(1)}, u32[]{:S(2)}, u32[]{:S(2)}) collective-permute-start(bf16[1,13,48,128]{3,2,1,0:T(8,128)(2,1)S(1)} %get-tuple-element.122), channel_id=1, source_target_pairs={{0,2},{1,3},{2,0},{3,1},{4,6},{5,7},{6,4},{7,5},{8,10},{9,11},{10,... | collective-permute-start | bytes 479240 | tf_op jit(solution)/shard_map/cond/branch_0_fun/ppermute | solution.py:346
  50.8 1.0 %copy-start.10 = (bf16[3,13,48,128]{3,2,1,0:T(8,128)(2,1)}, bf16[3,13,48,128]{3,2,1,0:T(8,128)(2,1)S(1)}, u32[]{:S(2)}) copy-start(bf16[3,13,48,128]{3,2,1,0:T(8,128)(2,1)S(1)} %collective-permute-done.33.refs_6_) | copy-start | bytes 1437700 | tf_op jit(solution)/shard_map/cond
  50.8 12.3 %collective-permute-start.26 = (bf16[1,13,48,128]{3,2,1,0:T(8,128)(2,1)S(1)}, bf16[1,13,48,128]{3,2,1,0:T(8,128)(2,1)S(1)}, u32[]{:S(2)}, u32[]{:S(2)}) collective-permute-start(bf16[1,13,48,128]{3,2,1,0:T(8,128)(2,1)S(1)} %get-tuple-element.118), channel_id=1, source_target_pairs={{0,1},{1,0},{2,3},{3,2},{4,5},{5,4},{6,7},{7,6},{8,9},{9,8},{10,11... | collective-permute-start | bytes 479240 | tf_op jit(solution)/shard_map/cond/branch_0_fun/ppermute | solution.py:346
  51.8 0.7 copy-start.25
  57.8 17.5 %copy-start.50 = (bf16[1,13,48,128]{3,2,1,0:T(8,128)(2,1)}, bf16[1,13,48,128]{3,2,1,0:T(8,128)(2,1)S(1)}, u32[]{:S(2)}) copy-start(bf16[1,13,48,128]{3,2,1,0:T(8,128)(2,1)S(1)} %collective-permute-done.30.refs_16_) | copy-start | bytes 479236 | tf_op jit(solution)/shard_map/cond
  59.6 3.6 %collective-permute-start.35 = (bf16[1,13,48,128]{3,2,1,0:T(8,128)(2,1)S(1)}, bf16[1,13,48,128]{3,2,1,0:T(8,128)(2,1)S(1)}, u32[]{:S(2)}, u32[]{:S(2)}) collective-permute-start(bf16[1,13,48,128]{3,2,1,0:T(8,128)(2,1)S(1)} %get-tuple-element.126), channel_id=1, source_target_pairs={{0,1},{1,0},{2,3},{3,2},{4,5},{5,4},{6,7},{7,6},{8,9},{9,8},{10,11... | collective-permute-start | bytes 479240 | tf_op jit(solution)/shard_map/cond/branch_0_fun/ppermute | solution.py:346
  59.6 16.2 %collective-permute-start.36 = (bf16[2,13,48,128]{3,2,1,0:T(8,128)(2,1)S(1)}, bf16[2,13,48,128]{3,2,1,0:T(8,128)(2,1)S(1)}, u32[]{:S(2)}, u32[]{:S(2)}) collective-permute-start(bf16[2,13,48,128]{3,2,1,0:T(8,128)(2,1)S(1)} %collective-permute-done.21.refs_4_), channel_id=1, source_target_pairs={{0,1},{1,0},{2,3},{3,2},{4,5},{5,4},{6,7},{7,6},{8,9},{9,8},{10,11... | collective-permute-start | bytes 958472 | tf_op jit(solution)/shard_map/cond/branch_0_fun/ppermute | solution.py:346
  60.1 14.7 %collective-permute-start.39 = (bf16[1,13,48,128]{3,2,1,0:T(8,128)(2,1)S(1)}, bf16[1,13,48,128]{3,2,1,0:T(8,128)(2,1)S(1)}, u32[]{:S(2)}, u32[]{:S(2)}) collective-permute-start(bf16[1,13,48,128]{3,2,1,0:T(8,128)(2,1)S(1)} %get-tuple-element.124), channel_id=1, source_target_pairs={{0,2},{1,3},{2,0},{3,1},{4,6},{5,7},{6,4},{7,5},{8,10},{9,11},{10,... | collective-permute-start | bytes 479240 | tf_op jit(solution)/shard_map/cond/branch_0_fun/ppermute | solution.py:346
  61.7 15.5 %copy-start.52 = (bf16[1,13,48,128]{3,2,1,0:T(8,128)(2,1)}, bf16[1,13,48,128]{3,2,1,0:T(8,128)(2,1)S(1)}, u32[]{:S(2)}) copy-start(bf16[1,13,48,128]{3,2,1,0:T(8,128)(2,1)S(1)} %collective-permute-done.41.refs_14_) | copy-start | bytes 479236 | tf_op jit(solution)/shard_map/cond
  61.7 13.5 %collective-permute-start.44 = (bf16[1,13,48,128]{3,2,1,0:T(8,128)(2,1)S(1)}, bf16[1,13,48,128]{3,2,1,0:T(8,128)(2,1)S(1)}, u32[]{:S(2)}, u32[]{:S(2)}) collective-permute-start(bf16[1,13,48,128]{3,2,1,0:T(8,128)(2,1)S(1)} %collective-permute-done.30.refs_16_), channel_id=1, source_target_pairs={{0,2},{1,3},{2,0},{3,1},{4,6},{5,7},{6,4},{7,5},{8,10},{9,11},{10,... | collective-permute-start | bytes 479240 | tf_op jit(solution)/shard_map/cond/branch_0_fun/ppermute | solution.py:346
  63.1 0.7 copy-start.42
  63.1 12.2 %collective-permute-start.37 = (bf16[1,13,48,128]{3,2,1,0:T(8,128)(2,1)S(1)}, bf16[1,13,48,128]{3,2,1,0:T(8,128)(2,1)S(1)}, u32[]{:S(2)}, u32[]{:S(2)}) collective-permute-start(bf16[1,13,48,128]{3,2,1,0:T(8,128)(2,1)S(1)} %collective-permute-done.25.refs_6_), channel_id=1, source_target_pairs={{0,1},{1,0},{2,3},{3,2},{4,5},{5,4},{6,7},{7,6},{8,9},{9,8},{10,11... | collective-permute-start | bytes 479240 | tf_op jit(solution)/shard_map/cond/branch_0_fun/ppermute | solution.py:346
  63.2 0.6 copy-start.45
  63.2 12.7 %collective-permute-start.38 = (bf16[2,13,48,128]{3,2,1,0:T(8,128)(2,1)S(1)}, bf16[2,13,48,128]{3,2,1,0:T(8,128)(2,1)S(1)}, u32[]{:S(2)}, u32[]{:S(2)}) collective-permute-start(bf16[2,13,48,128]{3,2,1,0:T(8,128)(2,1)S(1)} %collective-permute-done.22.refs_8_), channel_id=1, source_target_pairs={{0,1},{1,0},{2,3},{3,2},{4,5},{5,4},{6,7},{7,6},{8,9},{9,8},{10,11... | collective-permute-start | bytes 958472 | tf_op jit(solution)/shard_map/cond/branch_0_fun/ppermute | solution.py:346
  74.7 2.5 %copy-start.54 = (bf16[1,13,48,128]{3,2,1,0:T(8,128)(2,1)}, bf16[1,13,48,128]{3,2,1,0:T(8,128)(2,1)S(1)}, u32[]{:S(2)}) copy-start(bf16[1,13,48,128]{3,2,1,0:T(8,128)(2,1)S(1)} %collective-permute-done.39.refs_10_) | copy-start | bytes 479236 | tf_op jit(solution)/shard_map/cond
  74.7 1.5 %collective-permute-start.42 = (bf16[1,13,48,128]{3,2,1,0:T(8,128)(2,1)S(1)}, bf16[1,13,48,128]{3,2,1,0:T(8,128)(2,1)S(1)}, u32[]{:S(2)}, u32[]{:S(2)}) collective-permute-start(bf16[1,13,48,128]{3,2,1,0:T(8,128)(2,1)S(1)} %collective-permute-done.41.refs_14_), channel_id=1, source_target_pairs={{0,1},{1,0},{2,3},{3,2},{4,5},{5,4},{6,7},{7,6},{8,9},{9,8},{10,11... | collective-permute-start | bytes 479240 | tf_op jit(solution)/shard_map/cond/branch_0_fun/ppermute | solution.py:346
  75.2 2.0 %copy-start.56 = (bf16[1,13,48,128]{3,2,1,0:T(8,128)(2,1)}, bf16[1,13,48,128]{3,2,1,0:T(8,128)(2,1)S(1)}, u32[]{:S(2)}) copy-start(bf16[1,13,48,128]{3,2,1,0:T(8,128)(2,1)S(1)} %collective-permute-done.44.refs_18_) | copy-start | bytes 479236 | tf_op jit(solution)/shard_map/cond
  75.2 1.4 %collective-permute-start.40 = (bf16[1,13,48,128]{3,2,1,0:T(8,128)(2,1)S(1)}, bf16[1,13,48,128]{3,2,1,0:T(8,128)(2,1)S(1)}, u32[]{:S(2)}, u32[]{:S(2)}) collective-permute-start(bf16[1,13,48,128]{3,2,1,0:T(8,128)(2,1)S(1)} %collective-permute-done.39.refs_10_), channel_id=1, source_target_pairs={{0,1},{1,0},{2,3},{3,2},{4,5},{5,4},{6,7},{7,6},{8,9},{9,8},{10,11... | collective-permute-start | bytes 479240 | tf_op jit(solution)/shard_map/cond/branch_0_fun/ppermute | solution.py:346
  75.3 1.9 %copy-start.58 = (bf16[1,13,48,128]{3,2,1,0:T(8,128)(2,1)}, bf16[1,13,48,128]{3,2,1,0:T(8,128)(2,1)S(1)}, u32[]{:S(2)}) copy-start(bf16[1,13,48,128]{3,2,1,0:T(8,128)(2,1)S(1)} %collective-permute-done.37.refs_7_) | copy-start | bytes 479236 | tf_op jit(solution)/shard_map/cond
  75.3 1.5 %collective-permute-start.43 = (bf16[1,13,48,128]{3,2,1,0:T(8,128)(2,1)S(1)}, bf16[1,13,48,128]{3,2,1,0:T(8,128)(2,1)S(1)}, u32[]{:S(2)}, u32[]{:S(2)}) collective-permute-start(bf16[1,13,48,128]{3,2,1,0:T(8,128)(2,1)S(1)} %collective-permute-done.30.refs_16_), channel_id=1, source_target_pairs={{0,1},{1,0},{2,3},{3,2},{4,5},{5,4},{6,7},{7,6},{8,9},{9,8},{10,11... | collective-permute-start | bytes 479240 | tf_op jit(solution)/shard_map/cond/branch_0_fun/ppermute | solution.py:346
  75.8 1.4 %copy-start.33 = (bf16[2,13,48,128]{3,2,1,0:T(8,128)(2,1)}, bf16[2,13,48,128]{3,2,1,0:T(8,128)(2,1)S(1)}, u32[]{:S(2)}) copy-start(bf16[2,13,48,128]{3,2,1,0:T(8,128)(2,1)S(1)} %collective-permute-done.36.refs_5_) | copy-start | bytes 958468 | tf_op jit(solution)/shard_map/cond
  75.8 1.4 %collective-permute-start.45 = (bf16[1,13,48,128]{3,2,1,0:T(8,128)(2,1)S(1)}, bf16[1,13,48,128]{3,2,1,0:T(8,128)(2,1)S(1)}, u32[]{:S(2)}, u32[]{:S(2)}) collective-permute-start(bf16[1,13,48,128]{3,2,1,0:T(8,128)(2,1)S(1)} %collective-permute-done.44.refs_18_), channel_id=1, source_target_pairs={{0,1},{1,0},{2,3},{3,2},{4,5},{5,4},{6,7},{7,6},{8,9},{9,8},{10,11... | collective-permute-start | bytes 479240 | tf_op jit(solution)/shard_map/cond/branch_0_fun/ppermute | solution.py:346
  75.9 1.3 %copy-start.36 = (bf16[2,13,48,128]{3,2,1,0:T(8,128)(2,1)}, bf16[2,13,48,128]{3,2,1,0:T(8,128)(2,1)S(1)}, u32[]{:S(2)}) copy-start(bf16[2,13,48,128]{3,2,1,0:T(8,128)(2,1)S(1)} %collective-permute-done.38.refs_9_) | copy-start | bytes 958468 | tf_op jit(solution)/shard_map/cond
  76.2 1.0 %copy-start.60 = (bf16[1,13,48,128]{3,2,1,0:T(8,128)(2,1)}, bf16[1,13,48,128]{3,2,1,0:T(8,128)(2,1)S(1)}, u32[]{:S(2)}) copy-start(bf16[1,13,48,128]{3,2,1,0:T(8,128)(2,1)S(1)} %collective-permute-done.42.refs_15_) | copy-start | bytes 479236 | tf_op jit(solution)/shard_map/cond
  76.6 0.7 copy-start.62
  76.8 0.7 copy-start.64
  77.5 0.7 copy-start.66
  95.4 1.2 %copy-start.3 = (bf16[2,32,101,128]{3,1,2,0:T(8,128)(2,1)}, bf16[2,32,101,128]{3,1,2,0:T(8,128)(2,1)S(1)}, u32[]{:S(2)}) copy-start(bf16[2,32,101,128]{3,1,2,0:T(8,128)(2,1)S(1)} %get-tuple-element.155) | copy-start | bytes 4964356

commit v2 on v1

--- a/solution.py
+++ b/solution.py
@@ -17,7 +17,8 @@
 LANES = 128
 K8 = 8
 K16 = 16
-VMEM_BYTES = 56 * 1024 * 1024
+K4 = 4
+MIB = 2**20
 
 
 def shortened(value):
@@ -157,8 +158,34 @@
     full = np.zeros((rows, 2, groups * K8))
     full[:L, 0, :nbins] = (weight * np.cos(angle)).T
     full[:L, 1, :nbins] = -(weight * np.sin(angle)).T
-    full = full.reshape(rows, 2, groups, K8).transpose(0, 2, 1, 3).reshape(rows, groups * 2 * K8)
+    full = full.reshape(rows, 2, 2 * groups, K4).transpose(0, 2, 1, 3).reshape(rows, groups * 2 * K8)
     return full.astype(jnp.bfloat16)
+
+
+def top(shape):
+    return iota(shape, 0) % K8 < K4
+
+
+def moved_by(value, rows):
+    return pltpu.roll(value, rows % value.shape[0], 0)
+
+
+def low_rows(first, second):
+    return jnp.where(top(first.shape), first, moved_by(second, K4))
+
+
+def high_rows(first, second):
+    return jnp.where(top(first.shape), moved_by(first, -K4), second)
+
+
+def tiles_of(first, second, third):
+    return low_rows(first, second), third, high_rows(first, second)
+
+
+def bins_from(tiles):
+    low, both, high = tiles
+    rest = jnp.where(top(low.shape), low + moved_by(low, -K4), high + moved_by(high, K4))
+    return both + rest
 
 
 def pack_kernel(layout, nbins, here_ref, part_ref, slot_ref, x_ref, *rest):
@@ -180,13 +207,15 @@
     lane_group = iota((bins, lanes), 1) // per_peer
     inside = iota((bins, lanes), 0) < nbins
     for block in range(n_blk):
-        for pair in range(n_row // K16):
+        values = []
+        for pair in range(3):
             value = jnp.zeros((bins, lanes), jnp.float32)
             for g in range(4):
                 start = (2 * pair + g % 2) * 2 * nbins + g // 2
                 value = jnp.where(lane_group == g, wide_ref[block, pl.ds(start, bins, stride=2), :], value)
-            value = jnp.where(inside, value, 0.0).astype(jnp.bfloat16)
-            blocks_ref[block, :, pl.ds(pair * K16, K16), :] = value.reshape(n_grp, K16, lanes)
+            values.append(jnp.where(inside, value, 0.0))
+        tiles = [tile.reshape(n_grp, 2, 1, K8, lanes) for tile in tiles_of(*values)]
+        blocks_ref[block] = jnp.concatenate(tiles, axis=2).reshape(n_grp, n_row, lanes).astype(jnp.bfloat16)
     masks = [part_ref[r, here] ^ here for r in range(ROUNDS)]
     masks.append(masks[0] ^ masks[1])
     for out, message in zip(outs, layout):
@@ -207,61 +236,65 @@
 
 
 def source_kernel(nbins, windows, *refs):
-    src, (out_ref, power_ref, scale_ref) = refs[:4], refs[4:]
+    src, (out_ref, power_ref, scale_ref, copies_ref) = refs[:4], refs[4:]
     n_grp, n_row, lanes = src[0].shape[1:]
-    pairs = n_row // K16
     share = lanes // 4
     step = pl.program_id(0)
 
     @pl.when(step == 0)
     def _():
-        total = jnp.zeros((n_grp, K16, lanes), jnp.float32)
+        totals = [jnp.zeros((n_grp, 2, K8, lanes), jnp.float32) for _ in range(3)]
         for ref in src:
-            for pair in range(pairs):
-                value = ref[0, :, pl.ds(pair * K16, K16), :].astype(jnp.float32)
-                total = total + value * value
-        total = total.reshape(n_grp * K16, lanes)
+            value = ref[0].astype(jnp.float32).reshape(n_grp, 2, 3, K8, lanes)
+            totals = [total + value[:, :, i] * value[:, :, i] for i, total in enumerate(totals)]
+        total = bins_from([total.reshape(n_grp * K16, lanes) for total in totals])
         total = total + pltpu.roll(total, 2 * share, 1)
         total = total + pltpu.roll(total, share, 1)
         power_ref[...] = jnp.zeros(power_ref.shape, jnp.float32)
         power_ref[pl.ds(K8, n_grp * K16), :] = total
-        scale_ref[...] = scale_of(power_ref, nbins, windows).reshape(scale_ref.shape)
+        scale = scale_of(power_ref, nbins, windows)
+        scales = [low_rows(scale, scale), scale, high_rows(scale, scale)]
+        scales = [value.reshape(n_grp, 2, 1, K8, lanes) for value in scales]
+        scale_ref[...] = jnp.concatenate(scales, axis=2).reshape(scale_ref.shape)
+        row, col = iota(copies_ref.shape, 0), iota(copies_ref.shape, 1)
+        same = (col % share == row // K8) & (col // share == row // K4 % 2)
+        copies_ref[...] = jnp.where(same, 1.0, 0.0).astype(jnp.bfloat16)
 
     scale = scale_ref[step]
-    white = [
-        [
-            (ref[0, step, pl.ds(pair * K16, K16), :].astype(jnp.float32) * scale).astype(jnp.bfloat16).astype(jnp.float32)
-            for ref in src
-        ]
-        for pair in range(pairs)
-    ]
-    lane_group = iota((share, lanes), 1) // (4 * K8)
-    keep = iota((share, K8, lanes), 1) == iota((share, K8, lanes), 2) % K8
+    white = [(ref[0, step].astype(jnp.float32) * scale).astype(jnp.bfloat16).astype(jnp.float32) for ref in src]
+    lane = iota((share, lanes), 1)
+    shape = (copies_ref.shape[0], 2 * lanes)
+    keep = iota(shape, 0) % K4 == iota(shape, 1) % K4
     for half in range(2):
-        rows = [white[pair][e][half * K8 : (half + 1) * K8] for pair in range(pairs) for e in range(4)]
+        tiles = [[value[(3 * half + i) * K8 : (3 * half + i + 1) * K8] for value in white] for i in range(3)]
+        third = tiles[1]
+        rows = tiles[0] + [low_rows(third[0], third[1]), low_rows(third[2], third[3])]
+        rows = rows + tiles[2] + [high_rows(third[0], third[1]), high_rows(third[2], third[3])]
+        width = len(rows) * K4
         rows = rows + [jnp.zeros((lanes - len(rows) * K8, lanes), jnp.float32)]
         turned = jnp.concatenate(rows, axis=0).T
         by_group = [turned[g * share : (g + 1) * share] for g in range(4)]
         crossed = [by_group[2], by_group[3], -by_group[0], -by_group[1]]
-        for pair in range(pairs):
-            spread = []
+        for group in range(2):
+            lines = []
             for values in (by_group, crossed):
-                line = jnp.zeros((share, lanes), jnp.float32)
-                for g in range(4):
-                    moved = values[g]
-                    shift = (g - pair) * 4 * K8 % lanes
-                    if shift:
-                        moved = pltpu.roll(moved, shift, 1)
-                    line = jnp.where(lane_group == g, moved, line)
-                line = jnp.broadcast_to(line.reshape(share, 1, lanes), (share, K8, lanes))
-                spread.append(jnp.where(keep, line, 0.0))
-            both = jnp.concatenate(spread, axis=1).astype(jnp.bfloat16)
-            out_ref[half, :, pl.ds(pair * lanes, lanes)] = both.reshape(share * 2 * K8, lanes)
+                for start, size in ((0, 8 * K4), (8 * K4, 4 * K4)):
+                    line = jnp.zeros((share, lanes), jnp.float32)
+                    for g in range(4):
+                        shift = (g * size - group * width - start) % lanes
+                        moved = pltpu.roll(values[g], shift, 1) if shift else values[g]
+                        line = jnp.where(lane // size == g, moved, line)
+                    lines.append(line)
+            lines = jnp.concatenate(
+                [jnp.concatenate(lines[:2], axis=1), jnp.concatenate(lines[2:], axis=1)], axis=0
+            ).astype(jnp.bfloat16)
+            spread = jnp.dot(copies_ref[...], lines, preferred_element_type=jnp.float32)
+            spread = jnp.where(keep, spread, 0.0).astype(jnp.bfloat16)
+            out_ref[2 * half + group] = spread[:, : out_ref.shape[2]]
 
 
 def take_pieces(pieces, places, phase, here, right_ref, power_ref, scale_ref, nbins, windows):
     n_grp, n_row, lanes = pieces[0].shape[1:]
-    pairs = n_row // K16
     share = lanes // 4
     shape = (4 * lanes, 4 * lanes)
     row, col = iota(shape, 0), iota(shape, 1)
@@ -270,23 +303,33 @@
     odd = (here ^ kind) & 1
     spot = row % lanes // share * lanes + (2 * half + odd) * share + row % share
     order = jnp.where(col == spot, 1.0, 0.0).astype(jnp.bfloat16)
-    total = jnp.zeros((n_grp, 2, K8, lanes), jnp.float32)
+    flat, tall = (n_grp * K16, lanes), (n_grp, 2, K8, lanes)
+    totals = [jnp.zeros(tall, jnp.float32) for _ in range(3)]
+    before = [None] * 4
     for e in range(4):
         parts = [pieces[operand][index].reshape(n_grp * n_row, lanes) for operand, index in places[e]]
         moved = jnp.dot(jnp.concatenate(parts, axis=1), order, preferred_element_type=jnp.float32)
-        moved = moved.reshape(n_grp, pairs, 2, K8, 4 * lanes)
-        for pair in range(pairs):
-            for g in range(4):
-                value = moved[:, pair, :, :, g * lanes : (g + 1) * lanes]
-                right_ref[:, :, (pair * 4 + g) * 4 + e] = value
-                total = total + value * value
+        moved = moved.reshape(n_grp, 2, 3, K8, 4 * lanes)
+        for g in range(4):
+            low, both, high = values = [moved[:, :, i, :, g * lanes : (g + 1) * lanes] for i in range(3)]
+            totals = [total + value * value for total, value in zip(totals, values)]
+            right_ref[:, :, 0, g * 4 + e] = low
+            right_ref[:, :, 1, g * 4 + e] = high
+            both = both.reshape(flat)
+            if e % 2:
+                spot = 16 + g * 2 + e // 2
+                right_ref[:, :, 0, spot] = low_rows(before[g], both).reshape(tall)
+                right_ref[:, :, 1, spot] = high_rows(before[g], both).reshape(tall)
+            before[g] = both
     power_ref[...] = jnp.zeros(power_ref.shape, jnp.float32)
-    power_ref[pl.ds(K8, n_grp * K16), :] = total.reshape(n_grp * K16, lanes)
-    scale_ref[...] = scale_of(power_ref, nbins, windows).reshape(scale_ref.shape)
-
-
-def whitened(right_ref, scale_ref, index, half):
-    white = (right_ref[index, half] * scale_ref[index, half]).astype(jnp.bfloat16)
+    power_ref[pl.ds(K8, n_grp * K16), :] = bins_from([total.reshape(flat) for total in totals])
+    scale = scale_of(power_ref, nbins, windows)
+    scale_ref[:, :, 0] = low_rows(scale, scale).reshape(tall)
+    scale_ref[:, :, 1] = high_rows(scale, scale).reshape(tall)
+
+
+def whitened(right_ref, scale_ref, index, half, group):
+    white = (right_ref[index, half, group] * scale_ref[index, half, group]).astype(jnp.bfloat16)
     return white.reshape(-1, white.shape[-1])
 
 
@@ -296,7 +339,8 @@
 
     def one_group(index, carry):
         for half in range(2):
-            out_ref[2 * index + half] = whitened(right_ref, scale_ref, index, half)
+            for group in range(2):
+                out_ref[4 * index + 2 * half + group] = whitened(right_ref, scale_ref, index, half, group)
         return carry
 
     lax.fori_loop(0, right_ref.shape[0], one_group, 0)
@@ -318,10 +362,14 @@
 
     def one_group(index, carry):
         for half in range(2):
-            both = jnp.concatenate([early_ref[2 * index + half], whitened(right_ref, scale_ref, index, half)], axis=1)
-            cross = jnp.dot(left_ref[2 * index + half], both, preferred_element_type=jnp.float32)
-            place = pl.multiple_of((2 * index + half) * 2 * K8, 2 * K8)
-            cross_ref[:, pl.ds(place, 2 * K8), :] = cross.astype(jnp.bfloat16).reshape(-1, 2 * K8, cross.shape[-1])
+            crosses = []
+            for group in range(2):
+                spot = 4 * index + 2 * half + group
+                both = jnp.concatenate([early_ref[spot], whitened(right_ref, scale_ref, index, half, group)], axis=1)
+                cross = jnp.dot(left_ref[spot], both, preferred_element_type=jnp.float32)
+                crosses.append(cross.reshape(-1, K8, cross.shape[-1]))
+            place = pl.multiple_of((2 * index + half) * K16, K16)
+            cross_ref[:, pl.ds(place, K16), :] = jnp.concatenate(crosses, axis=1).astype(jnp.bfloat16)
         return carry
 
     lax.fori_loop(0, right_ref.shape[0], one_group, 0)
@@ -346,14 +394,14 @@
     return lax.ppermute(value, axis, [(i, i ^ mask) for i in range(lax.axis_size(axis))])
 
 
-def call(kernel, outs, operands, scratch, name, specs=None, traffic=1000, **grid):
+def call(kernel, outs, operands, scratch, name, specs=None, vmem_mib=40, **grid):
     return pl.pallas_call(
         kernel,
-        cost_estimate=pl.CostEstimate(flops=0, bytes_accessed=traffic, transcendentals=0),
+        cost_estimate=pl.CostEstimate(flops=0, bytes_accessed=MIB, transcendentals=0),
         out_shape=outs,
         in_specs=specs,
         scratch_shapes=scratch,
-        compiler_params=pltpu.CompilerParams(vmem_limit_bytes=VMEM_BYTES),
+        compiler_params=pltpu.CompilerParams(vmem_limit_bytes=vmem_mib * MIB),
         name=name,
         **grid,
     )(*operands)
@@ -370,9 +418,8 @@
         chans, nbins = spectra.shape[2:]
         windows = spectra.shape[1] * lax.axis_size("win")
         n_grp = bins_of(nbins)
-        pairs = spectra.shape[1] // 2
         share = chans // 4
-        piece = (n_grp, pairs * K16, chans)
+        piece = (n_grp, 3 * K16, chans)
         win = lax.axis_index("win")
         if case < 2:
             layout = [[(2, one), (2, None)], [(2, 2), (2, other)]]
@@ -451,19 +498,18 @@
             doubled(name)
         lag = jnp.asarray(lag_matrix(nbins))
         taken = [
-            pltpu.VMEM((n_grp, 2, pairs * 16, K8, chans), jnp.float32),
+            pltpu.VMEM((n_grp, 2, 2, 24, K8, chans), jnp.float32),
             pltpu.VMEM((n_grp * K16 + 2 * K8, chans), jnp.float32),
-            pltpu.VMEM((n_grp, 2, K8, chans), jnp.float32),
+            pltpu.VMEM((n_grp, 2, 2, K8, chans), jnp.float32),
         ]
         early_places, early_pieces = places_of(0)
         early = call(
             lambda *refs: receive_kernel(early_places, nbins, windows, *refs),
-            jax.ShapeDtypeStruct((2 * n_grp, pairs * 16 * K8, chans), jnp.bfloat16),
+            jax.ShapeDtypeStruct((4 * n_grp, 24 * K8, chans), jnp.bfloat16),
             (here, *early_pieces),
             taken,
             "receivers",
             [smem] + [vmem] * len(early_pieces),
-            traffic=12 * 2**20,
         )
         over_3b = swap(got_3b, "win", 2)
         across = after(across, got_3b, early)
@@ -475,17 +521,17 @@
             sources.append(swap(jnp.where(odd, two[0], two[1]), "win", 1))
         left = call(
             lambda *refs: source_kernel(nbins, windows, *refs),
-            jax.ShapeDtypeStruct((2 * n_grp, share * 2 * K8, pairs * chans), jnp.bfloat16),
+            jax.ShapeDtypeStruct((4 * n_grp, share * K8, 3 * chans // 2), jnp.bfloat16),
             sources,
             [
                 pltpu.VMEM((n_grp * K16 + 2 * K8, chans), jnp.float32),
-                pltpu.VMEM((n_grp, K16, chans), jnp.float32),
+                pltpu.VMEM((n_grp, 3 * K16, chans), jnp.float32),
+                pltpu.VMEM((share * K8, 2 * share), jnp.bfloat16),
             ],
             "sources",
             [vmem] * 4,
-            traffic=20 * 2**20,
             grid=(n_grp,),
-            out_specs=pl.BlockSpec((2, share * 2 * K8, pairs * chans), lambda i: (i, 0, 0)),
+            out_specs=pl.BlockSpec((4, share * K8, 3 * chans // 2), lambda i: (i, 0, 0)),
         )
         arrays["3b"] = [got_3b, over_3b]
         for name in list(arrays):
@@ -528,7 +574,7 @@
 
     def body(spectra, channel_slot, partners):
         small = all((mesh.shape[axis] - 1).bit_length() == 2 for axis in ("blk", "win"))
-        small = small and spectra.shape[2] == LANES and spectra.shape[1] % 2 == 0 and spectra.shape[3] <= 2 * LANES
+        small = small and spectra.shape[2] == LANES and spectra.shape[1] // 2 == 3 and spectra.shape[3] <= 2 * LANES
         return (gathering_body if small else walking_body)(spectra, channel_slot, partners)
 
     return jax.shard_map(body, mesh=mesh, in_specs=in_specs, out_specs=out_specs, check_vma=False)

time: 97 us -> 81.4 us (0.84)
  Pallas kernels: 36.4 us -> 22.3 us
  waiting for transfers between devices: 30 us -> 36 us
  starting transfers between devices: 21.6 us -> 18.2 us
  other arithmetic: 2.47 us -> 0.13 us
  local copies, waits for them, and re-layouts: 4.36 us -> 2.5 us
    pallas_call x4, Pallas kernels: 36.4 us -> 22.3 us  [call(): pl.pallas_call(kernel, cost_estimate=pl.CostEstimate(flops=0, bytes_acces...]
    ppermute x26 -> x20, waiting for transfers between devices: 30 us -> 36 us  [swap(): lax.ppermute(value, axis, [(i, i ^ mask) for i in range(lax.axis_size(axi...]
    ppermute x26 -> x20, starting transfers between devices: 21.6 us -> 18.2 us  [swap(): lax.ppermute(value, axis, [(i, i ^ mask) for i in range(lax.axis_size(axi...]
    select_n x2, other arithmetic: 2.44 us -> 0.1 us  [branch(): sources.append(swap(jnp.where(odd, two[0], two[1]), 'win', 1))]
    cond x50 -> x2, local copies, waits for them, and re-layouts: 1.82 us -> 0.01 us
  transfers between devices with their start and end apart: 26 -> 20, of which waited for: 10 -> 7; matrix products, arithmetic and copies ran while one was open for 3% -> 0% of each run, Pallas kernels for 17% -> 11%
where the time goes in v2:
time: 81.4 us; the launch traced here: 81.2 us
  waiting for transfers between devices  36 us (44%)
  Pallas kernels  22.3 us (27%)
  starting transfers between devices  18.2 us (22%)
  local copies, waits for them, and re-layouts  2.5 us (3%)
  between operations  1.32 us (2%)
    ppermute x20, waiting for transfers between devices, swap(): lax.ppermute(value, axis, [(i, i ^ mask) for i in range(lax.axis_size(axi...  36 us
    pallas_call x4, Pallas kernels, call(): pl.pallas_call(kernel, cost_estimate=pl.CostEstimate(flops=0, bytes_acces...  22.3 us
    ppermute x20, starting transfers between devices, swap(): lax.ppermute(value, axis, [(i, i ^ mask) for i in range(lax.axis_size(axi...  18.2 us
  transfers between devices with their start and end apart: 20, of which 7 were waited for; matrix products, arithmetic and copies ran while one was open for 0% of the time, Pallas kernels for 11%

profile of v2, /device:TPU:0, one launch (start us, length us, event | category | flops | bytes accessed | tf_op | source)
XLA Modules:
  0.0 81.2 jit_solution(14337607223537356610)
XLA Ops:
  0.0 1.3 %fusion.4 = (s32[1,1]{1,0:T(1,128)}, s32[1,1]{1,0:T(1,128)}) fusion(s32[2,4]{1,0:T(2,128)} %param.11), kind=kLoop, calls=%fused_computation.31 | loop fusion | bytes 16 | tf_op jit(solution)/shard_map/slice | solution.py:566
  2.6 77.5 %conditional.1 = (bf16[2,32,101,128]{3,1,2,0:T(8,128)(2,1)S(1)}) conditional(s32[]{:T(128)} %bitcast.12, (s32[]{:T(128)}, s32[128]{0:T(128)}, bf16[2,6,128,201]{2,0,3,1:T(2,128)(2,1)}, s32[]{:T(128)}, s32[2,4]{1,0:T(2,128)}, /*index=5*/()) %tuple.32, (s32[]{:T(128)}, s32[128]{0:T(128)}, bf16[2,6,128,201]{2,0,3,1:T(2,128)(2,1)}, ...), branch_computations={%region_0.1_spmd, %region_1.2_spmd, %region_2.3_spmd} | conditional | flops 798728 | bytes 36170892 | solution.py:568
  3.0 2.3 %pack.5 = (bf16[2,13,48,128]{3,2,1,0:T(8,128)(2,1)S(1)}, bf16[2,13,48,128]{3,2,1,0:T(8,128)(2,1)S(1)}, bf16[3,13,48,128]{3,2,1,0:T(8,128)(2,1)S(1)}, bf16[2,13,4...) custom-call(s32[1]{0:T(128)} %bitcast.8.refs_0_, s32[2,4]{1,0:T(2,128)} %get-tuple-element.81.refs_1_, ...), custom_call_target="tpu_custom_call" | custom-call | bytes 1048576 | tf_op jit(solution)/shard_map/cond/branch_2_fun/pack/pallas_call | solution.py:398
  5.3 3.1 %collective-permute-start = (bf16[3,13,48,128]{3,2,1,0:T(8,128)(2,1)S(1)}, bf16[3,13,48,128]{3,2,1,0:T(8,128)(2,1)S(1)}, u32[]{:S(2)}, u32[]{:S(2)}) collective-permute-start(bf16[3,13,48,128]{3,2,1,0:T(8,128)(2,1)S(1)} %get-tuple-element.84), channel_id=1, source_target_pairs={{0,4},{4,0},{8,12},{12,8},{1,5},{5,1},{9,13},{13,9},{2,6},{6,2},{1... | collective-permute-start | bytes 1437704 | tf_op jit(solution)/shard_map/cond/branch_2_fun/ppermute | solution.py:394
  8.4 2.6 %collective-permute-start.1 = (bf16[2,13,48,128]{3,2,1,0:T(8,128)(2,1)S(1)}, bf16[2,13,48,128]{3,2,1,0:T(8,128)(2,1)S(1)}, u32[]{:S(2)}, u32[]{:S(2)}) collective-permute-start(bf16[2,13,48,128]{3,2,1,0:T(8,128)(2,1)S(1)} %get-tuple-element.85), channel_id=1, source_target_pairs={{0,8},{4,12},{8,0},{12,4},{1,9},{5,13},{9,1},{13,5},{2,10},{6,14},... | collective-permute-start | bytes 958472 | tf_op jit(solution)/shard_map/cond/branch_2_fun/ppermute | solution.py:394
  11.0 1.5 %collective-permute-start.3 = (bf16[2,13,48,128]{3,2,1,0:T(8,128)(2,1)S(1)}, bf16[2,13,48,128]{3,2,1,0:T(8,128)(2,1)S(1)}, u32[]{:S(2)}, u32[]{:S(2)}) collective-permute-start(bf16[2,13,48,128]{3,2,1,0:T(8,128)(2,1)S(1)} %get-tuple-element.86.refs_1_), channel_id=1, source_target_pairs={{0,2},{1,3},{2,0},{3,1},{4,6},{5,7},{6,4},{7,5},{8,10},{9,11},{10,... | collective-permute-start | bytes 958472 | tf_op jit(solution)/shard_map/cond/branch_2_fun/ppermute | solution.py:394
  12.5 13.0 %collective-permute-done.1 = bf16[2,13,48,128]{3,2,1,0:T(8,128)(2,1)S(1)} collective-permute-done((bf16[2,13,48,128]{3,2,1,0:T(8,128)(2,1)S(1)}, bf16[2,13,48,128]{3,2,1,0:T(8,128)(2,1)S(1)}, u32[]{:S(2)}, u32[]{:S(2)}) %collective-permute-start.1) | collective-permute-done | bytes 319520 | tf_op jit(solution)/shard_map/cond/branch_2_fun/ppermute | solution.py:394
  25.5 3.4 %collective-permute-start.7 = (bf16[2,13,48,128]{3,2,1,0:T(8,128)(2,1)S(1)}, bf16[2,13,48,128]{3,2,1,0:T(8,128)(2,1)S(1)}, u32[]{:S(2)}, u32[]{:S(2)}) collective-permute-start(bf16[2,13,48,128]{3,2,1,0:T(8,128)(2,1)S(1)} %get-tuple-element.91), channel_id=1, source_target_pairs={{0,8},{4,12},{8,0},{12,4},{1,9},{5,13},{9,1},{13,5},{2,10},{6,14},... | collective-permute-start | bytes 958472 | tf_op jit(solution)/shard_map/cond/branch_2_fun/ppermute | solution.py:394
  28.9 0.0 collective-permute-done.refs_5_
  28.9 0.0 collective-permute-done.3.refs_3_
  28.9 1.6 %collective-permute-start.4 = (bf16[2,13,48,128]{3,2,1,0:T(8,128)(2,1)S(1)}, bf16[2,13,48,128]{3,2,1,0:T(8,128)(2,1)S(1)}, u32[]{:S(2)}, u32[]{:S(2)}) collective-permute-start(bf16[2,13,48,128]{3,2,1,0:T(8,128)(2,1)S(1)} %slice.109), channel_id=1, source_target_pairs={{0,2},{1,3},{2,0},{3,1},{4,6},{5,7},{6,4},{7,5},{8,10},{9,11},{10,... | collective-permute-start | bytes 958472 | tf_op jit(solution)/shard_map/cond/branch_2_fun/ppermute | solution.py:394
  30.5 0.2 collective-permute-start.2
  30.7 0.0 collective-permute-start.10
  30.7 0.5 collective-permute-start.11
  31.2 7.1 %collective-permute-done.2 = bf16[1,13,48,128]{3,2,1,0:T(8,128)(2,1)S(1)} collective-permute-done((bf16[1,13,48,128]{3,2,1,0:T(8,128)(2,1)S(1)}, bf16[1,13,48,128]{3,2,1,0:T(8,128)(2,1)S(1)}, u32[]{:S(2)}, u32[]{:S(2)}) %collective-permute-start.2) | collective-permute-done | bytes 159776 | tf_op jit(solution)/shard_map/cond/branch_2_fun/ppermute | solution.py:394
  38.3 0.0 collective-permute-start.12
  38.3 4.1 %collective-permute-done.7.refs_4_ = bf16[2,13,48,128]{3,2,1,0:T(8,128)(2,1)S(1)} collective-permute-done((bf16[2,13,48,128]{3,2,1,0:T(8,128)(2,1)S(1)}, bf16[2,13,48,128]{3,2,1,0:T(8,128)(2,1)S(1)}, u32[]{:S(2)}, u32[]{:S(2)}) %collective-permute-start.7) | collective-permute-done | bytes 319520 | tf_op jit(solution)/shard_map/cond/branch_2_fun/ppermute | solution.py:394
  42.4 0.0 collective-permute-start.8
  42.4 0.0 collective-permute-done.4.refs_7_
  42.4 0.1 broadcast_select_fusion.22
  42.5 1.5 %collective-permute-start.6 = (bf16[2,13,48,128]{3,2,1,0:T(8,128)(2,1)S(1)}, bf16[2,13,48,128]{3,2,1,0:T(8,128)(2,1)S(1)}, u32[]{:S(2)}, u32[]{:S(2)}) collective-permute-start(bf16[2,13,48,128]{3,2,1,0:T(8,128)(2,1)S(1)} %pad_maximum_fusion.2), channel_id=1, source_target_pairs={{0,2},{1,3},{2,0},{3,1},{4,6},{5,7},{6,4},{7,5},{8,10},{9,11},{10,... | collective-permute-start | bytes 958472 | tf_op jit(solution)/shard_map/cond/branch_2_fun/ppermute | solution.py:394
  44.0 0.0 collective-permute-done.8.refs_5_
  44.0 0.2 collective-permute-start.13
  44.3 0.0 collective-permute-done.10.refs_2_
  44.3 0.0 collective-permute-start.9
  44.3 0.0 collective-permute-done.11.refs_4_
  44.3 1.4 %collective-permute-start.15 = (bf16[2,13,48,128]{3,2,1,0:T(8,128)(2,1)S(1)}, bf16[2,13,48,128]{3,2,1,0:T(8,128)(2,1)S(1)}, u32[]{:S(2)}, u32[]{:S(2)}) collective-permute-start(bf16[2,13,48,128]{3,2,1,0:T(8,128)(2,1)S(1)} %collective-permute-done.7.refs_4_), channel_id=1, source_target_pairs={{0,2},{1,3},{2,0},{3,1},{4,6},{5,7},{6,4},{7,5},{8,10},{9,11},{10,... | collective-permute-start | bytes 958472 | tf_op jit(solution)/shard_map/cond/branch_2_fun/ppermute | solution.py:394
  45.7 0.0 collective-permute-done.12.refs_6_
  45.7 0.1 collective-permute-start.5
  45.8 0.0 collective-permute-done.13.refs_8_
  45.8 2.2 %receivers.5.refs_2_ = bf16[52,192,128]{2,1,0:T(8,128)(2,1)S(1)} custom-call(s32[1]{0:T(128)} %bitcast.8.refs_0_, bf16[2,13,48,128]{3,2,1,0:T(8,128)(2,1)S(1)} %get-tuple-element.86.refs_1_, bf16[2,13,48,128]{3,2,1,0:T(8,128)(2,1)S(1)} %collective-permute-done.10.refs_2_, bf16[2,13,48,128]{3,2,1,0:T(8,128)(2,1)S(1)} %collective-permute-done.3.refs_3_, ...), custom_call_target="tpu_custom_call" | custom-call | bytes 1048576 | tf_op jit(solution)/shard_map/cond/branch_2_fun/receivers/pallas_call | solution.py:398
  48.0 4.9 %collective-permute-done.6 = bf16[2,13,48,128]{3,2,1,0:T(8,128)(2,1)S(1)} collective-permute-done((bf16[2,13,48,128]{3,2,1,0:T(8,128)(2,1)S(1)}, bf16[2,13,48,128]{3,2,1,0:T(8,128)(2,1)S(1)}, u32[]{:S(2)}, u32[]{:S(2)}) %collective-permute-start.6) | collective-permute-done | bytes 319520 | tf_op jit(solution)/shard_map/cond/branch_2_fun/ppermute | solution.py:394
  52.9 1.1 %collective-permute-done.9.refs_8_ = bf16[2,13,48,128]{3,2,1,0:T(8,128)(2,1)S(1)} collective-permute-done((bf16[2,13,48,128]{3,2,1,0:T(8,128)(2,1)S(1)}, bf16[2,13,48,128]{3,2,1,0:T(8,128)(2,1)S(1)}, u32[]{:S(2)}, u32[]{:S(2)}) %collective-permute-start.9) | collective-permute-done | bytes 319520 | tf_op jit(solution)/shard_map/cond/branch_2_fun/ppermute | solution.py:394
  54.0 1.4 %collective-permute-start.18 = (bf16[2,13,48,128]{3,2,1,0:T(8,128)(2,1)S(1)}, bf16[2,13,48,128]{3,2,1,0:T(8,128)(2,1)S(1)}, u32[]{:S(2)}, u32[]{:S(2)}) collective-permute-start(bf16[2,13,48,128]{3,2,1,0:T(8,128)(2,1)S(1)} %collective-permute-done.9.refs_8_), channel_id=1, source_target_pairs={{0,2},{1,3},{2,0},{3,1},{4,6},{5,7},{6,4},{7,5},{8,10},{9,11},{10,... | collective-permute-start | bytes 958472 | tf_op jit(solution)/shard_map/cond/branch_2_fun/ppermute | solution.py:394
  55.5 0.1 collective-permute-start.14
  55.5 4.2 %collective-permute-done.15.refs_6_ = bf16[2,13,48,128]{3,2,1,0:T(8,128)(2,1)S(1)} collective-permute-done((bf16[2,13,48,128]{3,2,1,0:T(8,128)(2,1)S(1)}, bf16[2,13,48,128]{3,2,1,0:T(8,128)(2,1)S(1)}, u32[]{:S(2)}, u32[]{:S(2)}) %collective-permute-start.15) | collective-permute-done | bytes 319520 | tf_op jit(solution)/shard_map/cond/branch_2_fun/ppermute | solution.py:394
  59.7 0.0 collective-permute-start.16
  59.7 0.5 collective-permute-start.17
  60.2 0.0 collective-permute-done.5.refs_1_
  60.2 0.0 collective-permute-done.14.refs_3_
  60.3 0.0 copy-start.2
  60.3 7.0 %sources.5.refs_1_ = bf16[52,256,192]{2,1,0:T(8,128)(2,1)S(1)} custom-call(bf16[1,13,48,128]{3,2,1,0:T(8,128)(2,1)S(1)} %get-tuple-element.139.refs_0_, bf16[1,13,48,128]{3,2,1,0:T(8,128)(2,1)S(1)} %collective-permute-done.5.refs_1_, bf16[1,13,48,128]{3,2,1,0:T(8,128)(2,1)S(1)} %get-tuple-element.143.refs_2_, ...), custom_call_target="tpu_custom_call" | custom-call | bytes 1048576 | tf_op jit(solution)/shard_map/cond/branch_2_fun/sources/pallas_call | solution.py:398
  67.2 0.0 collective-permute-done.18.refs_10_
  67.2 0.1 collective-permute-start.19
  67.3 0.0 collective-permute-done.16.refs_7_
  67.3 0.0 collective-permute-done.17.refs_9_
  67.3 1.6 %collective-permute-done.19.refs_11_ = bf16[2,13,48,128]{3,2,1,0:T(8,128)(2,1)S(1)} collective-permute-done((bf16[2,13,48,128]{3,2,1,0:T(8,128)(2,1)S(1)}, bf16[2,13,48,128]{3,2,1,0:T(8,128)(2,1)S(1)}, u32[]{:S(2)}, u32[]{:S(2)}) %collective-permute-start.19) | collective-permute-done | bytes 319520 | tf_op jit(solution)/shard_map/cond/branch_2_fun/ppermute | solution.py:394
  68.9 0.0 copy-done.2
  68.9 10.9 %correlate.5 = bf16[2,101,32,128]{3,2,1,0:T(8,128)(2,1)S(1)} custom-call(s32[1]{0:T(128)} %bitcast.8.refs_0_, bf16[52,256,192]{2,1,0:T(8,128)(2,1)S(1)} %sources.5.refs_1_, bf16[52,192,128]{2,1,0:T(8,128)(2,1)S(1)} %receivers.5.refs_2_, bf16[104,416]{1,0:T(8,128)(2,1)S(1)} %copy-done.2, bf16[2,13,48,128]{3,2,1,0:T(8,128)(2,1)S(1)} %collective-permute-done.7.refs_4_, ...), custom_call_target="tpu_custom_call" | custom-call | bytes 1048576 | tf_op jit(solution)/shard_map/cond/branch_2_fun/correlate/pallas_call | solution.py:398
  80.1 0.0 copy-start.3
  80.1 1.2 %copy-done.3 = bf16[2,32,101,128]{3,1,2,0:T(8,128)(2,1)} copy-done((bf16[2,32,101,128]{3,1,2,0:T(8,128)(2,1)}, bf16[2,32,101,128]{3,1,2,0:T(8,128)(2,1)S(1)}, u32[]{:S(2)}) %copy-start.3) | copy-done | bytes 1654808
  (4 shorter events, 0.1 us)
Async XLA Ops:
  5.3 23.5 %collective-permute-start = (bf16[3,13,48,128]{3,2,1,0:T(8,128)(2,1)S(1)}, bf16[3,13,48,128]{3,2,1,0:T(8,128)(2,1)S(1)}, u32[]{:S(2)}, u32[]{:S(2)}) collective-permute-start(bf16[3,13,48,128]{3,2,1,0:T(8,128)(2,1)S(1)} %get-tuple-element.84), channel_id=1, source_target_pairs={{0,4},{4,0},{8,12},{12,8},{1,5},{5,1},{9,13},{13,9},{2,6},{6,2},{1... | collective-permute-start | bytes 1437704 | tf_op jit(solution)/shard_map/cond/branch_2_fun/ppermute | solution.py:394
  8.4 17.1 %collective-permute-start.1 = (bf16[2,13,48,128]{3,2,1,0:T(8,128)(2,1)S(1)}, bf16[2,13,48,128]{3,2,1,0:T(8,128)(2,1)S(1)}, u32[]{:S(2)}, u32[]{:S(2)}) collective-permute-start(bf16[2,13,48,128]{3,2,1,0:T(8,128)(2,1)S(1)} %get-tuple-element.85), channel_id=1, source_target_pairs={{0,8},{4,12},{8,0},{12,4},{1,9},{5,13},{9,1},{13,5},{2,10},{6,14},... | collective-permute-start | bytes 958472 | tf_op jit(solution)/shard_map/cond/branch_2_fun/ppermute | solution.py:394
  11.0 17.9 %collective-permute-start.3 = (bf16[2,13,48,128]{3,2,1,0:T(8,128)(2,1)S(1)}, bf16[2,13,48,128]{3,2,1,0:T(8,128)(2,1)S(1)}, u32[]{:S(2)}, u32[]{:S(2)}) collective-permute-start(bf16[2,13,48,128]{3,2,1,0:T(8,128)(2,1)S(1)} %get-tuple-element.86.refs_1_), channel_id=1, source_target_pairs={{0,2},{1,3},{2,0},{3,1},{4,6},{5,7},{6,4},{7,5},{8,10},{9,11},{10,... | collective-permute-start | bytes 958472 | tf_op jit(solution)/shard_map/cond/branch_2_fun/ppermute | solution.py:394
  25.5 16.9 %collective-permute-start.7 = (bf16[2,13,48,128]{3,2,1,0:T(8,128)(2,1)S(1)}, bf16[2,13,48,128]{3,2,1,0:T(8,128)(2,1)S(1)}, u32[]{:S(2)}, u32[]{:S(2)}) collective-permute-start(bf16[2,13,48,128]{3,2,1,0:T(8,128)(2,1)S(1)} %get-tuple-element.91), channel_id=1, source_target_pairs={{0,8},{4,12},{8,0},{12,4},{1,9},{5,13},{9,1},{13,5},{2,10},{6,14},... | collective-permute-start | bytes 958472 | tf_op jit(solution)/shard_map/cond/branch_2_fun/ppermute | solution.py:394
  28.9 13.5 %collective-permute-start.4 = (bf16[2,13,48,128]{3,2,1,0:T(8,128)(2,1)S(1)}, bf16[2,13,48,128]{3,2,1,0:T(8,128)(2,1)S(1)}, u32[]{:S(2)}, u32[]{:S(2)}) collective-permute-start(bf16[2,13,48,128]{3,2,1,0:T(8,128)(2,1)S(1)} %slice.109), channel_id=1, source_target_pairs={{0,2},{1,3},{2,0},{3,1},{4,6},{5,7},{6,4},{7,5},{8,10},{9,11},{10,... | collective-permute-start | bytes 958472 | tf_op jit(solution)/shard_map/cond/branch_2_fun/ppermute | solution.py:394
  30.5 7.8 %collective-permute-start.2 = (bf16[1,13,48,128]{3,2,1,0:T(8,128)(2,1)S(1)}, bf16[1,13,48,128]{3,2,1,0:T(8,128)(2,1)S(1)}, u32[]{:S(2)}, u32[]{:S(2)}) collective-permute-start(bf16[1,13,48,128]{3,2,1,0:T(8,128)(2,1)S(1)} %slice.108), channel_id=1, source_target_pairs={{0,4},{4,0},{8,12},{12,8},{1,5},{5,1},{9,13},{13,9},{2,6},{6,2},{1... | collective-permute-start | bytes 479240 | tf_op jit(solution)/shard_map/cond/branch_2_fun/ppermute | solution.py:394
  30.7 13.6 %collective-permute-start.10 = (bf16[2,13,48,128]{3,2,1,0:T(8,128)(2,1)S(1)}, bf16[2,13,48,128]{3,2,1,0:T(8,128)(2,1)S(1)}, u32[]{:S(2)}, u32[]{:S(2)}) collective-permute-start(bf16[2,13,48,128]{3,2,1,0:T(8,128)(2,1)S(1)} %get-tuple-element.86.refs_1_), channel_id=1, source_target_pairs={{0,1},{1,0},{2,3},{3,2},{4,5},{5,4},{6,7},{7,6},{8,9},{9,8},{10,11... | collective-permute-start | bytes 958472 | tf_op jit(solution)/shard_map/cond/branch_2_fun/ppermute | solution.py:394
  30.7 13.6 %collective-permute-start.11 = (bf16[2,13,48,128]{3,2,1,0:T(8,128)(2,1)S(1)}, bf16[2,13,48,128]{3,2,1,0:T(8,128)(2,1)S(1)}, u32[]{:S(2)}, u32[]{:S(2)}) collective-permute-start(bf16[2,13,48,128]{3,2,1,0:T(8,128)(2,1)S(1)} %collective-permute-done.3.refs_3_), channel_id=1, source_target_pairs={{0,1},{1,0},{2,3},{3,2},{4,5},{5,4},{6,7},{7,6},{8,9},{9,8},{10,11... | collective-permute-start | bytes 958472 | tf_op jit(solution)/shard_map/cond/branch_2_fun/ppermute | solution.py:394
  38.3 7.4 %collective-permute-start.12 = (bf16[3,13,48,128]{3,2,1,0:T(8,128)(2,1)S(1)}, bf16[3,13,48,128]{3,2,1,0:T(8,128)(2,1)S(1)}, u32[]{:S(2)}, u32[]{:S(2)}) collective-permute-start(bf16[3,13,48,128]{3,2,1,0:T(8,128)(2,1)S(1)} %collective-permute-done.refs_5_), channel_id=1, source_target_pairs={{0,1},{1,0},{2,3},{3,2},{4,5},{5,4},{6,7},{7,6},{8,9},{9,8},{10,11... | collective-permute-start | bytes 1437704 | tf_op jit(solution)/shard_map/cond/branch_2_fun/ppermute | solution.py:394
  42.4 1.7 %collective-permute-start.8 = (bf16[2,13,48,128]{3,2,1,0:T(8,128)(2,1)S(1)}, bf16[2,13,48,128]{3,2,1,0:T(8,128)(2,1)S(1)}, u32[]{:S(2)}, u32[]{:S(2)}) collective-permute-start(bf16[2,13,48,128]{3,2,1,0:T(8,128)(2,1)S(1)} %collective-permute-done.7.refs_4_), channel_id=1, source_target_pairs={{0,1},{1,0},{2,3},{3,2},{4,5},{5,4},{6,7},{7,6},{8,9},{9,8},{10,11... | collective-permute-start | bytes 958472 | tf_op jit(solution)/shard_map/cond/branch_2_fun/ppermute | solution.py:394
  42.5 10.4 %collective-permute-start.6 = (bf16[2,13,48,128]{3,2,1,0:T(8,128)(2,1)S(1)}, bf16[2,13,48,128]{3,2,1,0:T(8,128)(2,1)S(1)}, u32[]{:S(2)}, u32[]{:S(2)}) collective-permute-start(bf16[2,13,48,128]{3,2,1,0:T(8,128)(2,1)S(1)} %pad_maximum_fusion.2), channel_id=1, source_target_pairs={{0,2},{1,3},{2,0},{3,1},{4,6},{5,7},{6,4},{7,5},{8,10},{9,11},{10,... | collective-permute-start | bytes 958472 | tf_op jit(solution)/shard_map/cond/branch_2_fun/ppermute | solution.py:394
  44.0 1.7 %collective-permute-start.13 = (bf16[2,13,48,128]{3,2,1,0:T(8,128)(2,1)S(1)}, bf16[2,13,48,128]{3,2,1,0:T(8,128)(2,1)S(1)}, u32[]{:S(2)}, u32[]{:S(2)}) collective-permute-start(bf16[2,13,48,128]{3,2,1,0:T(8,128)(2,1)S(1)} %collective-permute-done.4.refs_7_), channel_id=1, source_target_pairs={{0,1},{1,0},{2,3},{3,2},{4,5},{5,4},{6,7},{7,6},{8,9},{9,8},{10,11... | collective-permute-start | bytes 958472 | tf_op jit(solution)/shard_map/cond/branch_2_fun/ppermute | solution.py:394
  44.3 9.7 %collective-permute-start.9 = (bf16[2,13,48,128]{3,2,1,0:T(8,128)(2,1)S(1)}, bf16[2,13,48,128]{3,2,1,0:T(8,128)(2,1)S(1)}, u32[]{:S(2)}, u32[]{:S(2)}) collective-permute-start(bf16[2,13,48,128]{3,2,1,0:T(8,128)(2,1)S(1)} %collective-permute-done.7.refs_4_), channel_id=1, source_target_pairs={{0,4},{4,0},{8,12},{12,8},{1,5},{5,1},{9,13},{13,9},{2,6},{6,2},{1... | collective-permute-start | bytes 958472 | tf_op jit(solution)/shard_map/cond/branch_2_fun/ppermute | solution.py:394
  44.3 15.5 %collective-permute-start.15 = (bf16[2,13,48,128]{3,2,1,0:T(8,128)(2,1)S(1)}, bf16[2,13,48,128]{3,2,1,0:T(8,128)(2,1)S(1)}, u32[]{:S(2)}, u32[]{:S(2)}) collective-permute-start(bf16[2,13,48,128]{3,2,1,0:T(8,128)(2,1)S(1)} %collective-permute-done.7.refs_4_), channel_id=1, source_target_pairs={{0,2},{1,3},{2,0},{3,1},{4,6},{5,7},{6,4},{7,5},{8,10},{9,11},{10,... | collective-permute-start | bytes 958472 | tf_op jit(solution)/shard_map/cond/branch_2_fun/ppermute | solution.py:394
  45.7 14.5 %collective-permute-start.5 = (bf16[1,13,48,128]{3,2,1,0:T(8,128)(2,1)S(1)}, bf16[1,13,48,128]{3,2,1,0:T(8,128)(2,1)S(1)}, u32[]{:S(2)}, u32[]{:S(2)}) collective-permute-start(bf16[1,13,48,128]{3,2,1,0:T(8,128)(2,1)S(1)} %get-tuple-element.138), channel_id=1, source_target_pairs={{0,1},{1,0},{2,3},{3,2},{4,5},{5,4},{6,7},{7,6},{8,9},{9,8},{10,11... | collective-permute-start | bytes 479240 | tf_op jit(solution)/shard_map/cond/branch_2_fun/ppermute | solution.py:394
  54.0 13.2 %collective-permute-start.18 = (bf16[2,13,48,128]{3,2,1,0:T(8,128)(2,1)S(1)}, bf16[2,13,48,128]{3,2,1,0:T(8,128)(2,1)S(1)}, u32[]{:S(2)}, u32[]{:S(2)}) collective-permute-start(bf16[2,13,48,128]{3,2,1,0:T(8,128)(2,1)S(1)} %collective-permute-done.9.refs_8_), channel_id=1, source_target_pairs={{0,2},{1,3},{2,0},{3,1},{4,6},{5,7},{6,4},{7,5},{8,10},{9,11},{10,... | collective-permute-start | bytes 958472 | tf_op jit(solution)/shard_map/cond/branch_2_fun/ppermute | solution.py:394
  55.5 4.8 %collective-permute-start.14 = (bf16[1,13,48,128]{3,2,1,0:T(8,128)(2,1)S(1)}, bf16[1,13,48,128]{3,2,1,0:T(8,128)(2,1)S(1)}, u32[]{:S(2)}, u32[]{:S(2)}) collective-permute-start(bf16[1,13,48,128]{3,2,1,0:T(8,128)(2,1)S(1)} %get-tuple-element.142), channel_id=1, source_target_pairs={{0,1},{1,0},{2,3},{3,2},{4,5},{5,4},{6,7},{7,6},{8,9},{9,8},{10,11... | collective-permute-start | bytes 479240 | tf_op jit(solution)/shard_map/cond/branch_2_fun/ppermute | solution.py:394
  59.7 7.6 %collective-permute-start.16 = (bf16[2,13,48,128]{3,2,1,0:T(8,128)(2,1)S(1)}, bf16[2,13,48,128]{3,2,1,0:T(8,128)(2,1)S(1)}, u32[]{:S(2)}, u32[]{:S(2)}) collective-permute-start(bf16[2,13,48,128]{3,2,1,0:T(8,128)(2,1)S(1)} %collective-permute-done.15.refs_6_), channel_id=1, source_target_pairs={{0,1},{1,0},{2,3},{3,2},{4,5},{5,4},{6,7},{7,6},{8,9},{9,8},{10,11... | collective-permute-start | bytes 958472 | tf_op jit(solution)/shard_map/cond/branch_2_fun/ppermute | solution.py:394
  59.7 7.6 %collective-permute-start.17 = (bf16[2,13,48,128]{3,2,1,0:T(8,128)(2,1)S(1)}, bf16[2,13,48,128]{3,2,1,0:T(8,128)(2,1)S(1)}, u32[]{:S(2)}, u32[]{:S(2)}) collective-permute-start(bf16[2,13,48,128]{3,2,1,0:T(8,128)(2,1)S(1)} %collective-permute-done.9.refs_8_), channel_id=1, source_target_pairs={{0,1},{1,0},{2,3},{3,2},{4,5},{5,4},{6,7},{7,6},{8,9},{9,8},{10,11... | collective-permute-start | bytes 958472 | tf_op jit(solution)/shard_map/cond/branch_2_fun/ppermute | solution.py:394
  60.3 8.7 %copy-start.2 = (bf16[104,416]{1,0:T(8,128)(2,1)S(1)}, bf16[104,416]{1,0:T(8,128)(2,1)}, u32[]{:S(2)}) copy-start(bf16[104,416]{1,0:T(8,128)(2,1)} %constant.38.clone.3.refs_3_) | copy-start | bytes 259588 | tf_op jit(solution)/shard_map/cond
  67.2 1.7 %collective-permute-start.19 = (bf16[2,13,48,128]{3,2,1,0:T(8,128)(2,1)S(1)}, bf16[2,13,48,128]{3,2,1,0:T(8,128)(2,1)S(1)}, u32[]{:S(2)}, u32[]{:S(2)}) collective-permute-start(bf16[2,13,48,128]{3,2,1,0:T(8,128)(2,1)S(1)} %collective-permute-done.18.refs_10_), channel_id=1, source_target_pairs={{0,1},{1,0},{2,3},{3,2},{4,5},{5,4},{6,7},{7,6},{8,9},{9,8},{10,11... | collective-permute-start | bytes 958472 | tf_op jit(solution)/shard_map/cond/branch_2_fun/ppermute | solution.py:394
  80.1 1.2 %copy-start.3 = (bf16[2,32,101,128]{3,1,2,0:T(8,128)(2,1)}, bf16[2,32,101,128]{3,1,2,0:T(8,128)(2,1)S(1)}, u32[]{:S(2)}) copy-start(bf16[2,32,101,128]{3,1,2,0:T(8,128)(2,1)S(1)} %get-tuple-element.267) | copy-start | bytes 4964356

commit v3 on v2

--- a/solution.py
+++ b/solution.py
@@ -421,10 +421,7 @@
         share = chans // 4
         piece = (n_grp, 3 * K16, chans)
         win = lax.axis_index("win")
-        if case < 2:
-            layout = [[(2, one), (2, None)], [(2, 2), (2, other)]]
-        else:
-            layout = [[(2, None), (3, None)], [(2, 0), (2, 1)]]
+        layout = [[(3, None), (2, None)], [(2, 2), (2, other)] if case < 2 else [(2, 0), (2, 1)]]
         layout += [[(1, 0), (1, 1), (1, None)], [(0, 0), (0, 1)], [(0, None)]]
         vmem, smem = pl.BlockSpec(memory_space=pltpu.VMEM), pl.BlockSpec(memory_space=pltpu.SMEM)
         far_a, far_b, near, own, own_src = call(
@@ -442,77 +439,20 @@
         mine = (z >> 1) == (win >> 1)
         got_1 = swap(near, "blk", 1)
         got_a = swap(far_a, "blk", 2)
+        got_b = swap(after(far_b, got_a), "blk", 2)
         over_0 = swap(own, "win", 2)
-        over_1 = swap(after(got_1[:2], over_0), "win", 2)
-        got_b = swap(after(far_b, got_a), "blk", 2)
-        core_2b = swap(got_b, "win", 1)
+        near_2, far_2, passed = got_1[:2], got_b, got_b
         if case < 2:
-            got_3a = swap(got_a, "blk", 1)
-            over_2a = swap(got_a[:1], "win", 2)
-            got_3b = swap(after(got_b[:1], core_2b), "blk", 1)
-            src = [own_src, got_1[2:], got_a[1:], after(got_3a[:1], over_1, over_2a)]
-        else:
-            got_3a = swap(got_a[1:], "blk", 1)
-            got_3b = swap(after(got_b, core_2b), "blk", 1)
-            src = [own_src, got_1[2:], got_a[:1], after(got_3a, over_1)]
+            far_2 = jnp.concatenate([got_a[:1], got_b[1:]], axis=0)
+            passed = jnp.concatenate([got_a[1:], got_b[:1]], axis=0)
+        over_1 = swap(after(near_2, over_0), "win", 2)
+        got_src = swap(got_a[:1], "blk", 1)
+        over_2 = swap(far_2, "win", 2)
+        src = [own_src, got_1[2:], got_a[1:], after(got_src, over_1)]
         high = [jnp.where(mine, src[d + 2], src[d]) for d in range(2)]
         across = swap(jnp.concatenate(high, axis=0), "win", 2)
         low = [jnp.where(mine, src[d], src[d + 2]) for d in range(2)]
-        if case < 2:
-            over_2b = swap(got_b[1:], "win", 2)
-            over_3a = swap(got_3a[1:], "win", 2)
-            over_3b = None
-            arrays = {
-                "2a": [got_a, over_2a],
-                "3a": [got_3a, over_3a],
-                "2b": [got_b, over_2b],
-                "3b": [got_3b, over_3b],
-            }
-            held = {(other, 2): ("2b", (1, 0)), (one, 2): ("2a", (0, 0))}
-            held |= {(other, 3): ("3b", (0, 0)), (one, 3): ("3a", (1, 0))}
-        else:
-            over_2b = swap(got_b, "win", 2)
-            over_3b = None
-            arrays = {"2b": [got_b, over_2b], "3b": [got_3b, over_3b]}
-            held = {(r, 2): ("2b", (r, r)) for r in range(2)} | {(r, 3): ("3b", (1 - r, 1 - r)) for r in range(2)}
-        arrays |= {0: [own, over_0], 1: [got_1, over_1]}
-        held |= {(r, d): (d, (r, r)) for r in range(2) for d in range(2)}
-        def doubled(name, last=()):
-            held_here, over = arrays[name]
-            core_here = core_2b if name == "2b" else swap(held_here, "win", 1)
-            arrays[name] = [held_here, core_here, over, swap(after(over, *last) if last else over, "win", 1)]
-
-        def places_of(phase):
-            names = list(dict.fromkeys(held[r, d][0] for r in range(ROUNDS) for d in (2 * phase, 2 * phase + 1)))
-            places = [[] for _ in range(4)]
-            for r in range(ROUNDS):
-                for d in (2 * phase, 2 * phase + 1):
-                    name, (whole, part) = held[r, d]
-                    for e in range(4):
-                        size = arrays[name][e].shape[0]
-                        index = whole if size == arrays[name][0].shape[0] else part
-                        places[e].append((4 * names.index(name) + e, index))
-            return places, [array for name in names for array in arrays[name]]
-
-        for name in (0, 1):
-            doubled(name)
-        lag = jnp.asarray(lag_matrix(nbins))
-        taken = [
-            pltpu.VMEM((n_grp, 2, 2, 24, K8, chans), jnp.float32),
-            pltpu.VMEM((n_grp * K16 + 2 * K8, chans), jnp.float32),
-            pltpu.VMEM((n_grp, 2, 2, K8, chans), jnp.float32),
-        ]
-        early_places, early_pieces = places_of(0)
-        early = call(
-            lambda *refs: receive_kernel(early_places, nbins, windows, *refs),
-            jax.ShapeDtypeStruct((4 * n_grp, 24 * K8, chans), jnp.bfloat16),
-            (here, *early_pieces),
-            taken,
-            "receivers",
-            [smem] + [vmem] * len(early_pieces),
-        )
-        over_3b = swap(got_3b, "win", 2)
-        across = after(across, got_3b, early)
+        got_3 = swap(after(passed, over_1, across), "blk", 1)
         odd = ((win ^ z) & 1) == 1
         first, second = low, [across[0:1], across[1:2]]
         sources = []
@@ -533,11 +473,41 @@
             grid=(n_grp,),
             out_specs=pl.BlockSpec((4, share * K8, 3 * chans // 2), lambda i: (i, 0, 0)),
         )
-        arrays["3b"] = [got_3b, over_3b]
-        for name in list(arrays):
-            if name not in (0, 1):
-                doubled(name, [left] if name == "3b" else [])
-        late_places, late_pieces = places_of(1)
+        core_far = swap(after(far_2, left, over_2), "win", 1)
+        over_3 = swap(after(got_3, core_far), "win", 2)
+        held = {(r, d): r for r in range(2) for d in range(2)}
+        if case < 2:
+            held |= {(one, d): 0 for d in (2, 3)} | {(other, d): 1 for d in (2, 3)}
+        else:
+            held |= {(r, 2): r for r in range(2)} | {(r, 3): 1 - r for r in range(2)}
+        spots = [[(0, 0), (4, 0), (2, 0), (4, 4)], [(1, 0), (4, 2), (3, 0), (4, 6)]]
+        spots += [[(0, 0), (4, 0), (2, 0), (5, 2)], [(1, 0), (5, 0), (3, 0), (6, 0)]]
+
+        def places_of(phase):
+            kinds = [(r, d) for r in range(ROUNDS) for d in (2 * phase, 2 * phase + 1)]
+            return [[(spots[d][e][0], spots[d][e][1] + held[r, d]) for r, d in kinds] for e in range(4)]
+
+        early_pieces = [own, near_2, over_0, over_1]
+        early_pieces.append(swap(after(jnp.concatenate(early_pieces, axis=0), got_b), "win", 1))
+        lag = jnp.asarray(lag_matrix(nbins))
+        taken = [
+            pltpu.VMEM((n_grp, 2, 2, 24, K8, chans), jnp.float32),
+            pltpu.VMEM((n_grp * K16 + 2 * K8, chans), jnp.float32),
+            pltpu.VMEM((n_grp, 2, 2, K8, chans), jnp.float32),
+        ]
+        early_places = places_of(0)
+        early = call(
+            lambda *refs: receive_kernel(early_places, nbins, windows, *refs),
+            jax.ShapeDtypeStruct((4 * n_grp, 24 * K8, chans), jnp.bfloat16),
+            (here, *early_pieces),
+            taken,
+            "receivers",
+            [smem] + [vmem] * len(early_pieces),
+        )
+        late_places = places_of(1)
+        late_pieces = [far_2, got_3, over_2, over_3, core_far]
+        late_pieces.append(swap(jnp.concatenate([got_3, over_2], axis=0), "win", 1))
+        late_pieces.append(swap(after(over_3, early), "win", 1))
         hbm = pl.BlockSpec(memory_space=pl.ANY)
         by_lag = call(
             lambda *refs: correlate_kernel(late_places, nbins, windows, *refs),

time: 81.4 us -> 80.9 us (level)
  starting transfers between devices: 18.2 us -> 17 us
    ppermute x20 -> x16, starting transfers between devices: 18.2 us -> 17 us  [swap(): lax.ppermute(value, axis, [(i, i ^ mask) for i in range(lax.axis_size(axi...]
    ppermute x20 -> x16, waiting for transfers between devices: 36 us -> 36.6 us  [swap(): lax.ppermute(value, axis, [(i, i ^ mask) for i in range(lax.axis_size(axi...]
  transfers between devices with their start and end apart: 20 -> 16, of which waited for: 7 -> 9; matrix products, arithmetic and copies ran while one was open for 0% -> 0% of each run, Pallas kernels for 11% -> 11%
where the time goes in v3:
time: 80.9 us; the launch traced here: 80.8 us
  waiting for transfers between devices  36.6 us (45%)
  Pallas kernels  22.3 us (28%)
  starting transfers between devices  17 us (21%)
  local copies, waits for them, and re-layouts  2.53 us (3%)
  between operations  1.31 us (2%)
    ppermute x16, waiting for transfers between devices, swap(): lax.ppermute(value, axis, [(i, i ^ mask) for i in range(lax.axis_size(axi...  36.6 us
    pallas_call x4, Pallas kernels, call(): pl.pallas_call(kernel, cost_estimate=pl.CostEstimate(flops=0, bytes_acces...  22.3 us
    ppermute x16, starting transfers between devices, swap(): lax.ppermute(value, axis, [(i, i ^ mask) for i in range(lax.axis_size(axi...  17 us
  transfers between devices with their start and end apart: 16, of which 9 were waited for; matrix products, arithmetic and copies ran while one was open for 0% of the time, Pallas kernels for 11%

profile of v3, /device:TPU:0, one launch (start us, length us, event | category | flops | bytes accessed | tf_op | source)
XLA Modules:
  0.0 80.8 jit_solution(15642050626194223559)
XLA Ops:
  0.0 1.3 %fusion.2 = (s32[1,1]{1,0:T(1,128)}, s32[1,1]{1,0:T(1,128)}) fusion(s32[2,4]{1,0:T(2,128)} %param.11), kind=kLoop, calls=%fused_computation.39 | loop fusion | bytes 16 | tf_op jit(solution)/shard_map/slice | solution.py:536
  2.6 77.0 %conditional.1 = (bf16[2,32,101,128]{3,1,2,0:T(8,128)(2,1)S(1)}) conditional(s32[]{:T(128)} %bitcast.12, (s32[]{:T(128)}, s32[128]{0:T(128)}, bf16[2,6,128,201]{2,0,3,1:T(2,128)(2,1)}, s32[]{:T(128)}, s32[2,4]{1,0:T(2,128)}, /*index=5*/()) %tuple.38, (s32[]{:T(128)}, s32[128]{0:T(128)}, bf16[2,6,128,201]{2,0,3,1:T(2,128)(2,1)}, ...), branch_computations={%region_0.1_spmd, %region_1.2_spmd, %region_2.3_spmd} | conditional | flops 3354632 | bytes 38247164 | solution.py:538
  3.1 2.3 %pack.5 = (bf16[2,13,48,128]{3,2,1,0:T(8,128)(2,1)S(1)}, bf16[2,13,48,128]{3,2,1,0:T(8,128)(2,1)S(1)}, bf16[3,13,48,128]{3,2,1,0:T(8,128)(2,1)S(1)}, bf16[2,13,4...) custom-call(s32[1]{0:T(128)} %bitcast.8.refs_0_, s32[2,4]{1,0:T(2,128)} %get-tuple-element.85.refs_1_, ...), custom_call_target="tpu_custom_call" | custom-call | bytes 1048576 | tf_op jit(solution)/shard_map/cond/branch_2_fun/pack/pallas_call | solution.py:398
  5.4 3.1 %collective-permute-start = (bf16[3,13,48,128]{3,2,1,0:T(8,128)(2,1)S(1)}, bf16[3,13,48,128]{3,2,1,0:T(8,128)(2,1)S(1)}, u32[]{:S(2)}, u32[]{:S(2)}) collective-permute-start(bf16[3,13,48,128]{3,2,1,0:T(8,128)(2,1)S(1)} %get-tuple-element.88), channel_id=1, source_target_pairs={{0,4},{4,0},{8,12},{12,8},{1,5},{5,1},{9,13},{13,9},{2,6},{6,2},{1... | collective-permute-start | bytes 1437704 | tf_op jit(solution)/shard_map/cond/branch_2_fun/ppermute | solution.py:394
  8.5 1.5 %collective-permute-start.3 = (bf16[2,13,48,128]{3,2,1,0:T(8,128)(2,1)S(1)}, bf16[2,13,48,128]{3,2,1,0:T(8,128)(2,1)S(1)}, u32[]{:S(2)}, u32[]{:S(2)}) collective-permute-start(bf16[2,13,48,128]{3,2,1,0:T(8,128)(2,1)S(1)} %get-tuple-element.90.refs_1_), channel_id=1, source_target_pairs={{0,2},{1,3},{2,0},{3,1},{4,6},{5,7},{6,4},{7,5},{8,10},{9,11},{10,... | collective-permute-start | bytes 958472 | tf_op jit(solution)/shard_map/cond/branch_2_fun/ppermute | solution.py:394
  9.9 2.6 %collective-permute-start.1 = (bf16[2,13,48,128]{3,2,1,0:T(8,128)(2,1)S(1)}, bf16[2,13,48,128]{3,2,1,0:T(8,128)(2,1)S(1)}, u32[]{:S(2)}, u32[]{:S(2)}) collective-permute-start(bf16[2,13,48,128]{3,2,1,0:T(8,128)(2,1)S(1)} %get-tuple-element.89), channel_id=1, source_target_pairs={{0,8},{4,12},{8,0},{12,4},{1,9},{5,13},{9,1},{13,5},{2,10},{6,14},... | collective-permute-start | bytes 958472 | tf_op jit(solution)/shard_map/cond/branch_2_fun/ppermute | solution.py:394
  12.5 13.7 %collective-permute-done = bf16[3,13,48,128]{3,2,1,0:T(8,128)(2,1)S(1)} collective-permute-done((bf16[3,13,48,128]{3,2,1,0:T(8,128)(2,1)S(1)}, bf16[3,13,48,128]{3,2,1,0:T(8,128)(2,1)S(1)}, u32[]{:S(2)}, u32[]{:S(2)}) %collective-permute-start) | collective-permute-done | bytes 479264 | tf_op jit(solution)/shard_map/cond/branch_2_fun/ppermute | solution.py:394
  26.3 0.0 collective-permute-done.3.refs_3_
  26.3 1.7 %collective-permute-start.4 = (bf16[2,13,48,128]{3,2,1,0:T(8,128)(2,1)S(1)}, bf16[2,13,48,128]{3,2,1,0:T(8,128)(2,1)S(1)}, u32[]{:S(2)}, u32[]{:S(2)}) collective-permute-start(bf16[2,13,48,128]{3,2,1,0:T(8,128)(2,1)S(1)} %slice.101.refs_2_), channel_id=1, source_target_pairs={{0,2},{1,3},{2,0},{3,1},{4,6},{5,7},{6,4},{7,5},{8,10},{9,11},{10,... | collective-permute-start | bytes 958472 | tf_op jit(solution)/shard_map/cond/branch_2_fun/ppermute | solution.py:394
  28.0 0.0 collective-permute-done.1
  28.0 1.1 %collective-permute-start.2 = (bf16[1,13,48,128]{3,2,1,0:T(8,128)(2,1)S(1)}, bf16[1,13,48,128]{3,2,1,0:T(8,128)(2,1)S(1)}, u32[]{:S(2)}, u32[]{:S(2)}) collective-permute-start(bf16[1,13,48,128]{3,2,1,0:T(8,128)(2,1)S(1)} %slice.100), channel_id=1, source_target_pairs={{0,4},{4,0},{8,12},{12,8},{1,5},{5,1},{9,13},{13,9},{2,6},{6,2},{1... | collective-permute-start | bytes 479240 | tf_op jit(solution)/shard_map/cond/branch_2_fun/ppermute | solution.py:394
  29.1 3.2 %collective-permute-start.8 = (bf16[2,13,48,128]{3,2,1,0:T(8,128)(2,1)S(1)}, bf16[2,13,48,128]{3,2,1,0:T(8,128)(2,1)S(1)}, u32[]{:S(2)}, u32[]{:S(2)}) collective-permute-start(bf16[2,13,48,128]{3,2,1,0:T(8,128)(2,1)S(1)} %get-tuple-element.95), channel_id=1, source_target_pairs={{0,8},{4,12},{8,0},{12,4},{1,9},{5,13},{9,1},{13,5},{2,10},{6,14},... | collective-permute-start | bytes 958472 | tf_op jit(solution)/shard_map/cond/branch_2_fun/ppermute | solution.py:394
  32.3 3.7 %collective-permute-done.2 = bf16[1,13,48,128]{3,2,1,0:T(8,128)(2,1)S(1)} collective-permute-done((bf16[1,13,48,128]{3,2,1,0:T(8,128)(2,1)S(1)}, bf16[1,13,48,128]{3,2,1,0:T(8,128)(2,1)S(1)}, u32[]{:S(2)}, u32[]{:S(2)}) %collective-permute-start.2) | collective-permute-done | bytes 159776 | tf_op jit(solution)/shard_map/cond/branch_2_fun/ppermute | solution.py:394
  36.0 0.0 collective-permute-done.4.refs_4_
  36.0 0.1 broadcast_select_fusion.22
  36.1 0.5 collective-permute-start.6
  36.6 0.2 pad_maximum_fusion.10
  36.8 8.4 %collective-permute-done.8.refs_4_ = bf16[2,13,48,128]{3,2,1,0:T(8,128)(2,1)S(1)} collective-permute-done((bf16[2,13,48,128]{3,2,1,0:T(8,128)(2,1)S(1)}, bf16[2,13,48,128]{3,2,1,0:T(8,128)(2,1)S(1)}, u32[]{:S(2)}, u32[]{:S(2)}) %collective-permute-start.8) | collective-permute-done | bytes 319520 | tf_op jit(solution)/shard_map/cond/branch_2_fun/ppermute | solution.py:394
  45.2 0.0 collective-permute-start.9
  45.2 1.2 %collective-permute-start.11 = (bf16[2,13,48,128]{3,2,1,0:T(8,128)(2,1)S(1)}, bf16[2,13,48,128]{3,2,1,0:T(8,128)(2,1)S(1)}, u32[]{:S(2)}, u32[]{:S(2)}) collective-permute-start(bf16[2,13,48,128]{3,2,1,0:T(8,128)(2,1)S(1)} %collective-permute-done.8.refs_4_), channel_id=1, source_target_pairs={{0,2},{1,3},{2,0},{3,1},{4,6},{5,7},{6,4},{7,5},{8,10},{9,11},{10,... | collective-permute-start | bytes 958472 | tf_op jit(solution)/shard_map/cond/branch_2_fun/ppermute | solution.py:394
  46.5 0.2 collective-permute-start.5
  46.7 0.0 collective-permute-done.6
  46.7 0.3 collective-permute-start.7
  47.1 0.0 collective-permute-start.10
  47.1 1.4 %collective-permute-done.5.refs_1_ = bf16[1,13,48,128]{3,2,1,0:T(8,128)(2,1)S(1)} collective-permute-done((bf16[1,13,48,128]{3,2,1,0:T(8,128)(2,1)S(1)}, bf16[1,13,48,128]{3,2,1,0:T(8,128)(2,1)S(1)}, u32[]{:S(2)}, u32[]{:S(2)}) %collective-permute-start.5) | collective-permute-done | bytes 159776 | tf_op jit(solution)/shard_map/cond/branch_2_fun/ppermute | solution.py:394
  48.4 0.2 collective-permute-done.7.refs_3_
  48.6 6.9 %sources.5.refs_1_ = bf16[52,256,192]{2,1,0:T(8,128)(2,1)S(1)} custom-call(bf16[1,13,48,128]{3,2,1,0:T(8,128)(2,1)S(1)} %get-tuple-element.143.refs_0_, bf16[1,13,48,128]{3,2,1,0:T(8,128)(2,1)S(1)} %collective-permute-done.5.refs_1_, bf16[1,13,48,128]{3,2,1,0:T(8,128)(2,1)S(1)} %get-tuple-element.147.refs_2_, ...), custom_call_target="tpu_custom_call" | custom-call | bytes 1048576 | tf_op jit(solution)/shard_map/cond/branch_2_fun/sources/pallas_call | solution.py:398
  55.6 0.0 collective-permute-done.11.refs_6_
  55.6 0.2 collective-permute-start.12
  55.8 0.9 %collective-permute-done.10.refs_5_ = bf16[2,13,48,128]{3,2,1,0:T(8,128)(2,1)S(1)} collective-permute-done((bf16[2,13,48,128]{3,2,1,0:T(8,128)(2,1)S(1)}, bf16[2,13,48,128]{3,2,1,0:T(8,128)(2,1)S(1)}, u32[]{:S(2)}, u32[]{:S(2)}) %collective-permute-start.10) | collective-permute-done | bytes 319520 | tf_op jit(solution)/shard_map/cond/branch_2_fun/ppermute | solution.py:394
  56.7 0.6 collective-permute-done.12.refs_8_
  57.3 1.2 %collective-permute-start.13 = (bf16[2,13,48,128]{3,2,1,0:T(8,128)(2,1)S(1)}, bf16[2,13,48,128]{3,2,1,0:T(8,128)(2,1)S(1)}, u32[]{:S(2)}, u32[]{:S(2)}) collective-permute-start(bf16[2,13,48,128]{3,2,1,0:T(8,128)(2,1)S(1)} %collective-permute-done.10.refs_5_), channel_id=1, source_target_pairs={{0,2},{1,3},{2,0},{3,1},{4,6},{5,7},{6,4},{7,5},{8,10},{9,11},{10,... | collective-permute-start | bytes 958472 | tf_op jit(solution)/shard_map/cond/branch_2_fun/ppermute | solution.py:394
  58.5 0.1 pad_maximum_fusion.11
  58.6 0.0 copy-start.2
  58.6 0.1 collective-permute-start.14
  58.7 0.0 collective-permute-done.9.refs_5_
  58.7 2.2 %receivers.5.refs_2_ = bf16[52,192,128]{2,1,0:T(8,128)(2,1)S(1)} custom-call(s32[1]{0:T(128)} %bitcast.8.refs_0_, bf16[2,13,48,128]{3,2,1,0:T(8,128)(2,1)S(1)} %get-tuple-element.90.refs_1_, bf16[2,13,48,128]{3,2,1,0:T(8,128)(2,1)S(1)} %slice.101.refs_2_, bf16[2,13,48,128]{3,2,1,0:T(8,128)(2,1)S(1)} %collective-permute-done.3.refs_3_, ...), custom_call_target="tpu_custom_call" | custom-call | bytes 1048576 | tf_op jit(solution)/shard_map/cond/branch_2_fun/receivers/pallas_call | solution.py:398
  60.9 6.0 %collective-permute-done.13.refs_7_ = bf16[2,13,48,128]{3,2,1,0:T(8,128)(2,1)S(1)} collective-permute-done((bf16[2,13,48,128]{3,2,1,0:T(8,128)(2,1)S(1)}, bf16[2,13,48,128]{3,2,1,0:T(8,128)(2,1)S(1)}, u32[]{:S(2)}, u32[]{:S(2)}) %collective-permute-start.13) | collective-permute-done | bytes 319520 | tf_op jit(solution)/shard_map/cond/branch_2_fun/ppermute | solution.py:394
  66.9 0.0 collective-permute-start.15
  66.9 0.0 collective-permute-done.14.refs_9_
  66.9 1.6 %collective-permute-done.15.refs_10_ = bf16[2,13,48,128]{3,2,1,0:T(8,128)(2,1)S(1)} collective-permute-done((bf16[2,13,48,128]{3,2,1,0:T(8,128)(2,1)S(1)}, bf16[2,13,48,128]{3,2,1,0:T(8,128)(2,1)S(1)}, u32[]{:S(2)}, u32[]{:S(2)}) %collective-permute-start.15) | collective-permute-done | bytes 319520 | tf_op jit(solution)/shard_map/cond/branch_2_fun/ppermute | solution.py:394
  68.5 0.0 copy-done.2
  68.5 10.9 %correlate.5 = bf16[2,101,32,128]{3,2,1,0:T(8,128)(2,1)S(1)} custom-call(s32[1]{0:T(128)} %bitcast.8.refs_0_, bf16[52,256,192]{2,1,0:T(8,128)(2,1)S(1)} %sources.5.refs_1_, bf16[52,192,128]{2,1,0:T(8,128)(2,1)S(1)} %receivers.5.refs_2_, bf16[104,416]{1,0:T(8,128)(2,1)S(1)} %copy-done.2, bf16[2,13,48,128]{3,2,1,0:T(8,128)(2,1)S(1)} %collective-permute-done.8.refs_4_, ...), custom_call_target="tpu_custom_call" | custom-call | bytes 1048576 | tf_op jit(solution)/shard_map/cond/branch_2_fun/correlate/pallas_call | solution.py:398
  79.6 0.0 copy-start.3
  79.6 1.2 %copy-done.3 = bf16[2,32,101,128]{3,1,2,0:T(8,128)(2,1)} copy-done((bf16[2,32,101,128]{3,1,2,0:T(8,128)(2,1)}, bf16[2,32,101,128]{3,1,2,0:T(8,128)(2,1)S(1)}, u32[]{:S(2)}) %copy-start.3) | copy-done | bytes 1654808
  (4 shorter events, 0.1 us)
Async XLA Ops:
  5.4 20.9 %collective-permute-start = (bf16[3,13,48,128]{3,2,1,0:T(8,128)(2,1)S(1)}, bf16[3,13,48,128]{3,2,1,0:T(8,128)(2,1)S(1)}, u32[]{:S(2)}, u32[]{:S(2)}) collective-permute-start(bf16[3,13,48,128]{3,2,1,0:T(8,128)(2,1)S(1)} %get-tuple-element.88), channel_id=1, source_target_pairs={{0,4},{4,0},{8,12},{12,8},{1,5},{5,1},{9,13},{13,9},{2,6},{6,2},{1... | collective-permute-start | bytes 1437704 | tf_op jit(solution)/shard_map/cond/branch_2_fun/ppermute | solution.py:394
  8.5 17.8 %collective-permute-start.3 = (bf16[2,13,48,128]{3,2,1,0:T(8,128)(2,1)S(1)}, bf16[2,13,48,128]{3,2,1,0:T(8,128)(2,1)S(1)}, u32[]{:S(2)}, u32[]{:S(2)}) collective-permute-start(bf16[2,13,48,128]{3,2,1,0:T(8,128)(2,1)S(1)} %get-tuple-element.90.refs_1_), channel_id=1, source_target_pairs={{0,2},{1,3},{2,0},{3,1},{4,6},{5,7},{6,4},{7,5},{8,10},{9,11},{10,... | collective-permute-start | bytes 958472 | tf_op jit(solution)/shard_map/cond/branch_2_fun/ppermute | solution.py:394
  9.9 18.1 %collective-permute-start.1 = (bf16[2,13,48,128]{3,2,1,0:T(8,128)(2,1)S(1)}, bf16[2,13,48,128]{3,2,1,0:T(8,128)(2,1)S(1)}, u32[]{:S(2)}, u32[]{:S(2)}) collective-permute-start(bf16[2,13,48,128]{3,2,1,0:T(8,128)(2,1)S(1)} %get-tuple-element.89), channel_id=1, source_target_pairs={{0,8},{4,12},{8,0},{12,4},{1,9},{5,13},{9,1},{13,5},{2,10},{6,14},... | collective-permute-start | bytes 958472 | tf_op jit(solution)/shard_map/cond/branch_2_fun/ppermute | solution.py:394
  26.3 9.7 %collective-permute-start.4 = (bf16[2,13,48,128]{3,2,1,0:T(8,128)(2,1)S(1)}, bf16[2,13,48,128]{3,2,1,0:T(8,128)(2,1)S(1)}, u32[]{:S(2)}, u32[]{:S(2)}) collective-permute-start(bf16[2,13,48,128]{3,2,1,0:T(8,128)(2,1)S(1)} %slice.101.refs_2_), channel_id=1, source_target_pairs={{0,2},{1,3},{2,0},{3,1},{4,6},{5,7},{6,4},{7,5},{8,10},{9,11},{10,... | collective-permute-start | bytes 958472 | tf_op jit(solution)/shard_map/cond/branch_2_fun/ppermute | solution.py:394
  28.0 8.0 %collective-permute-start.2 = (bf16[1,13,48,128]{3,2,1,0:T(8,128)(2,1)S(1)}, bf16[1,13,48,128]{3,2,1,0:T(8,128)(2,1)S(1)}, u32[]{:S(2)}, u32[]{:S(2)}) collective-permute-start(bf16[1,13,48,128]{3,2,1,0:T(8,128)(2,1)S(1)} %slice.100), channel_id=1, source_target_pairs={{0,4},{4,0},{8,12},{12,8},{1,5},{5,1},{9,13},{13,9},{2,6},{6,2},{1... | collective-permute-start | bytes 479240 | tf_op jit(solution)/shard_map/cond/branch_2_fun/ppermute | solution.py:394
  29.1 16.1 %collective-permute-start.8 = (bf16[2,13,48,128]{3,2,1,0:T(8,128)(2,1)S(1)}, bf16[2,13,48,128]{3,2,1,0:T(8,128)(2,1)S(1)}, u32[]{:S(2)}, u32[]{:S(2)}) collective-permute-start(bf16[2,13,48,128]{3,2,1,0:T(8,128)(2,1)S(1)} %get-tuple-element.95), channel_id=1, source_target_pairs={{0,8},{4,12},{8,0},{12,4},{1,9},{5,13},{9,1},{13,5},{2,10},{6,14},... | collective-permute-start | bytes 958472 | tf_op jit(solution)/shard_map/cond/branch_2_fun/ppermute | solution.py:394
  36.1 10.6 %collective-permute-start.6 = (bf16[2,13,48,128]{3,2,1,0:T(8,128)(2,1)S(1)}, bf16[2,13,48,128]{3,2,1,0:T(8,128)(2,1)S(1)}, u32[]{:S(2)}, u32[]{:S(2)}) collective-permute-start(bf16[2,13,48,128]{3,2,1,0:T(8,128)(2,1)S(1)} %pad_maximum_fusion.12), channel_id=1, source_target_pairs={{0,2},{1,3},{2,0},{3,1},{4,6},{5,7},{6,4},{7,5},{8,10},{9,11},{10,... | collective-permute-start | bytes 958472 | tf_op jit(solution)/shard_map/cond/branch_2_fun/ppermute | solution.py:394
  45.2 13.5 %collective-permute-start.9 = (bf16[8,13,48,128]{3,2,1,0:T(8,128)(2,1)S(1)}, bf16[8,13,48,128]{3,2,1,0:T(8,128)(2,1)S(1)}, u32[]{:S(2)}, u32[]{:S(2)}) collective-permute-start(bf16[8,13,48,128]{3,2,1,0:T(8,128)(2,1)S(1)} %pad_maximum_fusion.10), channel_id=1, source_target_pairs={{0,1},{1,0},{2,3},{3,2},{4,5},{5,4},{6,7},{7,6},{8,9},{9,8},{10,11... | collective-permute-start | bytes 3833864 | tf_op jit(solution)/shard_map/cond/branch_2_fun/ppermute | solution.py:394
  45.2 10.4 %collective-permute-start.11 = (bf16[2,13,48,128]{3,2,1,0:T(8,128)(2,1)S(1)}, bf16[2,13,48,128]{3,2,1,0:T(8,128)(2,1)S(1)}, u32[]{:S(2)}, u32[]{:S(2)}) collective-permute-start(bf16[2,13,48,128]{3,2,1,0:T(8,128)(2,1)S(1)} %collective-permute-done.8.refs_4_), channel_id=1, source_target_pairs={{0,2},{1,3},{2,0},{3,1},{4,6},{5,7},{6,4},{7,5},{8,10},{9,11},{10,... | collective-permute-start | bytes 958472 | tf_op jit(solution)/shard_map/cond/branch_2_fun/ppermute | solution.py:394
  46.5 2.0 %collective-permute-start.5 = (bf16[1,13,48,128]{3,2,1,0:T(8,128)(2,1)S(1)}, bf16[1,13,48,128]{3,2,1,0:T(8,128)(2,1)S(1)}, u32[]{:S(2)}, u32[]{:S(2)}) collective-permute-start(bf16[1,13,48,128]{3,2,1,0:T(8,128)(2,1)S(1)} %get-tuple-element.142), channel_id=1, source_target_pairs={{0,1},{1,0},{2,3},{3,2},{4,5},{5,4},{6,7},{7,6},{8,9},{9,8},{10,11... | collective-permute-start | bytes 479240 | tf_op jit(solution)/shard_map/cond/branch_2_fun/ppermute | solution.py:394
  46.7 1.9 %collective-permute-start.7 = (bf16[1,13,48,128]{3,2,1,0:T(8,128)(2,1)S(1)}, bf16[1,13,48,128]{3,2,1,0:T(8,128)(2,1)S(1)}, u32[]{:S(2)}, u32[]{:S(2)}) collective-permute-start(bf16[1,13,48,128]{3,2,1,0:T(8,128)(2,1)S(1)} %get-tuple-element.146), channel_id=1, source_target_pairs={{0,1},{1,0},{2,3},{3,2},{4,5},{5,4},{6,7},{7,6},{8,9},{9,8},{10,11... | collective-permute-start | bytes 479240 | tf_op jit(solution)/shard_map/cond/branch_2_fun/ppermute | solution.py:394
  47.1 9.7 %collective-permute-start.10 = (bf16[2,13,48,128]{3,2,1,0:T(8,128)(2,1)S(1)}, bf16[2,13,48,128]{3,2,1,0:T(8,128)(2,1)S(1)}, u32[]{:S(2)}, u32[]{:S(2)}) collective-permute-start(bf16[2,13,48,128]{3,2,1,0:T(8,128)(2,1)S(1)} %collective-permute-done.8.refs_4_), channel_id=1, source_target_pairs={{0,4},{4,0},{8,12},{12,8},{1,5},{5,1},{9,13},{13,9},{2,6},{6,2},{1... | collective-permute-start | bytes 958472 | tf_op jit(solution)/shard_map/cond/branch_2_fun/ppermute | solution.py:394
  55.6 1.7 %collective-permute-start.12 = (bf16[2,13,48,128]{3,2,1,0:T(8,128)(2,1)S(1)}, bf16[2,13,48,128]{3,2,1,0:T(8,128)(2,1)S(1)}, u32[]{:S(2)}, u32[]{:S(2)}) collective-permute-start(bf16[2,13,48,128]{3,2,1,0:T(8,128)(2,1)S(1)} %collective-permute-done.8.refs_4_), channel_id=1, source_target_pairs={{0,1},{1,0},{2,3},{3,2},{4,5},{5,4},{6,7},{7,6},{8,9},{9,8},{10,11... | collective-permute-start | bytes 958472 | tf_op jit(solution)/shard_map/cond/branch_2_fun/ppermute | solution.py:394
  57.3 9.6 %collective-permute-start.13 = (bf16[2,13,48,128]{3,2,1,0:T(8,128)(2,1)S(1)}, bf16[2,13,48,128]{3,2,1,0:T(8,128)(2,1)S(1)}, u32[]{:S(2)}, u32[]{:S(2)}) collective-permute-start(bf16[2,13,48,128]{3,2,1,0:T(8,128)(2,1)S(1)} %collective-permute-done.10.refs_5_), channel_id=1, source_target_pairs={{0,2},{1,3},{2,0},{3,1},{4,6},{5,7},{6,4},{7,5},{8,10},{9,11},{10,... | collective-permute-start | bytes 958472 | tf_op jit(solution)/shard_map/cond/branch_2_fun/ppermute | solution.py:394
  58.6 9.9 %copy-start.2 = (bf16[104,416]{1,0:T(8,128)(2,1)S(1)}, bf16[104,416]{1,0:T(8,128)(2,1)}, u32[]{:S(2)}) copy-start(bf16[104,416]{1,0:T(8,128)(2,1)} %constant.38.clone.3.refs_3_) | copy-start | bytes 259588 | tf_op jit(solution)/shard_map/cond
  58.6 8.3 %collective-permute-start.14 = (bf16[4,13,48,128]{3,2,1,0:T(8,128)(2,1)S(1)}, bf16[4,13,48,128]{3,2,1,0:T(8,128)(2,1)S(1)}, u32[]{:S(2)}, u32[]{:S(2)}) collective-permute-start(bf16[4,13,48,128]{3,2,1,0:T(8,128)(2,1)S(1)} %pad_maximum_fusion.11), channel_id=1, source_target_pairs={{0,1},{1,0},{2,3},{3,2},{4,5},{5,4},{6,7},{7,6},{8,9},{9,8},{10,11... | collective-permute-start | bytes 1916936 | tf_op jit(solution)/shard_map/cond/branch_2_fun/ppermute | solution.py:394
  66.9 1.6 %collective-permute-start.15 = (bf16[2,13,48,128]{3,2,1,0:T(8,128)(2,1)S(1)}, bf16[2,13,48,128]{3,2,1,0:T(8,128)(2,1)S(1)}, u32[]{:S(2)}, u32[]{:S(2)}) collective-permute-start(bf16[2,13,48,128]{3,2,1,0:T(8,128)(2,1)S(1)} %collective-permute-done.13.refs_7_), channel_id=1, source_target_pairs={{0,1},{1,0},{2,3},{3,2},{4,5},{5,4},{6,7},{7,6},{8,9},{9,8},{10,11... | collective-permute-start | bytes 958472 | tf_op jit(solution)/shard_map/cond/branch_2_fun/ppermute | solution.py:394
  79.6 1.2 %copy-start.3 = (bf16[2,32,101,128]{3,1,2,0:T(8,128)(2,1)}, bf16[2,32,101,128]{3,1,2,0:T(8,128)(2,1)S(1)}, u32[]{:S(2)}) copy-start(bf16[2,32,101,128]{3,1,2,0:T(8,128)(2,1)S(1)} %get-tuple-element.215) | copy-start | bytes 4964356

commit v4 on v3

--- a/solution.py
+++ b/solution.py
@@ -372,7 +372,7 @@
             cross_ref[:, pl.ds(place, K16), :] = jnp.concatenate(crosses, axis=1).astype(jnp.bfloat16)
         return carry
 
-    lax.fori_loop(0, right_ref.shape[0], one_group, 0)
+    lax.fori_loop(0, right_ref.shape[0], one_group, 0, unroll=True)
     norm = 1.0 / math.sqrt(windows * 2 * (nbins - 1))
     share, lanes = cross_ref.shape[0], pieces[0].shape[-1]
     first = iota((lag_ref.shape[0], lanes), 1) // (2 * share) == here >> 1
@@ -385,7 +385,7 @@
             lagged_ref[r, pl.ds(index, lagged.shape[0], stride=share), :] = rounds[r]
         return carry
 
-    lax.fori_loop(0, share, one_source, 0, unroll=4)
+    lax.fori_loop(0, share, one_source, 0, unroll=True)
     for r in range(ROUNDS):
         out_ref[r] = lagged_ref[r, pl.ds(0, L * share), :].astype(jnp.bfloat16).reshape(L, share, lanes)
 

time: 80.9 us -> 77.9 us (0.963)
  Pallas kernels: 22.3 us -> 19.2 us
    pallas_call x4, Pallas kernels: 22.3 us -> 19.2 us  [call(): pl.pallas_call(kernel, cost_estimate=pl.CostEstimate(flops=0, bytes_acces...]
  transfers between devices with their start and end apart: 16 -> 16, of which waited for: 9 -> 9; matrix products, arithmetic and copies ran while one was open for 0% -> 0% of each run, Pallas kernels for 11% -> 12%
where the time goes in v4:
time: 77.9 us; the launch traced here: 77.7 us
  waiting for transfers between devices  36.6 us (47%)
  Pallas kernels  19.2 us (25%)
  starting transfers between devices  17 us (22%)
  local copies, waits for them, and re-layouts  2.53 us (3%)
  between operations  1.31 us (2%)
  loops' own time  0.8 us (1%)
    ppermute x16, waiting for transfers between devices, swap(): lax.ppermute(value, axis, [(i, i ^ mask) for i in range(lax.axis_size(axi...  36.6 us
    pallas_call x4, Pallas kernels, call(): pl.pallas_call(kernel, cost_estimate=pl.CostEstimate(flops=0, bytes_acces...  19.2 us
    ppermute x16, starting transfers between devices, swap(): lax.ppermute(value, axis, [(i, i ^ mask) for i in range(lax.axis_size(axi...  17 us
  transfers between devices with their start and end apart: 16, of which 9 were waited for; matrix products, arithmetic and copies ran while one was open for 0% of the time, Pallas kernels for 12%

profile of v4, /device:TPU:0, one launch (start us, length us, event | category | flops | bytes accessed | tf_op | source)
XLA Modules:
  0.0 77.7 jit_solution(16239807567556394057)
XLA Ops:
  0.0 1.3 %fusion.2 = (s32[1,1]{1,0:T(1,128)}, s32[1,1]{1,0:T(1,128)}) fusion(s32[2,4]{1,0:T(2,128)} %param.11), kind=kLoop, calls=%fused_computation.39 | loop fusion | bytes 16 | tf_op jit(solution)/shard_map/slice | solution.py:536
  2.6 73.9 %conditional.1 = (bf16[2,32,101,128]{3,1,2,0:T(8,128)(2,1)S(1)}) conditional(s32[]{:T(128)} %bitcast.12, (s32[]{:T(128)}, s32[128]{0:T(128)}, bf16[2,6,128,201]{2,0,3,1:T(2,128)(2,1)}, s32[]{:T(128)}, s32[2,4]{1,0:T(2,128)}, /*index=5*/()) %tuple.38, (s32[]{:T(128)}, s32[128]{0:T(128)}, bf16[2,6,128,201]{2,0,3,1:T(2,128)(2,1)}, ...), branch_computations={%region_0.1_spmd, %region_1.2_spmd, %region_2.3_spmd} | conditional | flops 3354632 | bytes 38247164 | solution.py:538
  3.1 2.3 %pack.5 = (bf16[2,13,48,128]{3,2,1,0:T(8,128)(2,1)S(1)}, bf16[2,13,48,128]{3,2,1,0:T(8,128)(2,1)S(1)}, bf16[3,13,48,128]{3,2,1,0:T(8,128)(2,1)S(1)}, bf16[2,13,4...) custom-call(s32[1]{0:T(128)} %bitcast.8.refs_0_, s32[2,4]{1,0:T(2,128)} %get-tuple-element.85.refs_1_, ...), custom_call_target="tpu_custom_call" | custom-call | bytes 1048576 | tf_op jit(solution)/shard_map/cond/branch_2_fun/pack/pallas_call | solution.py:398
  5.4 3.1 %collective-permute-start = (bf16[3,13,48,128]{3,2,1,0:T(8,128)(2,1)S(1)}, bf16[3,13,48,128]{3,2,1,0:T(8,128)(2,1)S(1)}, u32[]{:S(2)}, u32[]{:S(2)}) collective-permute-start(bf16[3,13,48,128]{3,2,1,0:T(8,128)(2,1)S(1)} %get-tuple-element.88), channel_id=1, source_target_pairs={{0,4},{4,0},{8,12},{12,8},{1,5},{5,1},{9,13},{13,9},{2,6},{6,2},{1... | collective-permute-start | bytes 1437704 | tf_op jit(solution)/shard_map/cond/branch_2_fun/ppermute | solution.py:394
  8.5 1.5 %collective-permute-start.3 = (bf16[2,13,48,128]{3,2,1,0:T(8,128)(2,1)S(1)}, bf16[2,13,48,128]{3,2,1,0:T(8,128)(2,1)S(1)}, u32[]{:S(2)}, u32[]{:S(2)}) collective-permute-start(bf16[2,13,48,128]{3,2,1,0:T(8,128)(2,1)S(1)} %get-tuple-element.90.refs_1_), channel_id=1, source_target_pairs={{0,2},{1,3},{2,0},{3,1},{4,6},{5,7},{6,4},{7,5},{8,10},{9,11},{10,... | collective-permute-start | bytes 958472 | tf_op jit(solution)/shard_map/cond/branch_2_fun/ppermute | solution.py:394
  9.9 2.6 %collective-permute-start.1 = (bf16[2,13,48,128]{3,2,1,0:T(8,128)(2,1)S(1)}, bf16[2,13,48,128]{3,2,1,0:T(8,128)(2,1)S(1)}, u32[]{:S(2)}, u32[]{:S(2)}) collective-permute-start(bf16[2,13,48,128]{3,2,1,0:T(8,128)(2,1)S(1)} %get-tuple-element.89), channel_id=1, source_target_pairs={{0,8},{4,12},{8,0},{12,4},{1,9},{5,13},{9,1},{13,5},{2,10},{6,14},... | collective-permute-start | bytes 958472 | tf_op jit(solution)/shard_map/cond/branch_2_fun/ppermute | solution.py:394
  12.5 13.7 %collective-permute-done = bf16[3,13,48,128]{3,2,1,0:T(8,128)(2,1)S(1)} collective-permute-done((bf16[3,13,48,128]{3,2,1,0:T(8,128)(2,1)S(1)}, bf16[3,13,48,128]{3,2,1,0:T(8,128)(2,1)S(1)}, u32[]{:S(2)}, u32[]{:S(2)}) %collective-permute-start) | collective-permute-done | bytes 479264 | tf_op jit(solution)/shard_map/cond/branch_2_fun/ppermute | solution.py:394
  26.3 0.0 collective-permute-done.3.refs_3_
  26.3 1.7 %collective-permute-start.4 = (bf16[2,13,48,128]{3,2,1,0:T(8,128)(2,1)S(1)}, bf16[2,13,48,128]{3,2,1,0:T(8,128)(2,1)S(1)}, u32[]{:S(2)}, u32[]{:S(2)}) collective-permute-start(bf16[2,13,48,128]{3,2,1,0:T(8,128)(2,1)S(1)} %slice.101.refs_2_), channel_id=1, source_target_pairs={{0,2},{1,3},{2,0},{3,1},{4,6},{5,7},{6,4},{7,5},{8,10},{9,11},{10,... | collective-permute-start | bytes 958472 | tf_op jit(solution)/shard_map/cond/branch_2_fun/ppermute | solution.py:394
  28.0 0.0 collective-permute-done.1
  28.0 1.1 %collective-permute-start.2 = (bf16[1,13,48,128]{3,2,1,0:T(8,128)(2,1)S(1)}, bf16[1,13,48,128]{3,2,1,0:T(8,128)(2,1)S(1)}, u32[]{:S(2)}, u32[]{:S(2)}) collective-permute-start(bf16[1,13,48,128]{3,2,1,0:T(8,128)(2,1)S(1)} %slice.100), channel_id=1, source_target_pairs={{0,4},{4,0},{8,12},{12,8},{1,5},{5,1},{9,13},{13,9},{2,6},{6,2},{1... | collective-permute-start | bytes 479240 | tf_op jit(solution)/shard_map/cond/branch_2_fun/ppermute | solution.py:394
  29.1 3.2 %collective-permute-start.8 = (bf16[2,13,48,128]{3,2,1,0:T(8,128)(2,1)S(1)}, bf16[2,13,48,128]{3,2,1,0:T(8,128)(2,1)S(1)}, u32[]{:S(2)}, u32[]{:S(2)}) collective-permute-start(bf16[2,13,48,128]{3,2,1,0:T(8,128)(2,1)S(1)} %get-tuple-element.95), channel_id=1, source_target_pairs={{0,8},{4,12},{8,0},{12,4},{1,9},{5,13},{9,1},{13,5},{2,10},{6,14},... | collective-permute-start | bytes 958472 | tf_op jit(solution)/shard_map/cond/branch_2_fun/ppermute | solution.py:394
  32.3 3.7 %collective-permute-done.2 = bf16[1,13,48,128]{3,2,1,0:T(8,128)(2,1)S(1)} collective-permute-done((bf16[1,13,48,128]{3,2,1,0:T(8,128)(2,1)S(1)}, bf16[1,13,48,128]{3,2,1,0:T(8,128)(2,1)S(1)}, u32[]{:S(2)}, u32[]{:S(2)}) %collective-permute-start.2) | collective-permute-done | bytes 159776 | tf_op jit(solution)/shard_map/cond/branch_2_fun/ppermute | solution.py:394
  36.0 0.0 collective-permute-done.4.refs_4_
  36.0 0.1 broadcast_select_fusion.22
  36.1 0.5 collective-permute-start.6
  36.6 0.2 pad_maximum_fusion.10
  36.8 8.4 %collective-permute-done.8.refs_4_ = bf16[2,13,48,128]{3,2,1,0:T(8,128)(2,1)S(1)} collective-permute-done((bf16[2,13,48,128]{3,2,1,0:T(8,128)(2,1)S(1)}, bf16[2,13,48,128]{3,2,1,0:T(8,128)(2,1)S(1)}, u32[]{:S(2)}, u32[]{:S(2)}) %collective-permute-start.8) | collective-permute-done | bytes 319520 | tf_op jit(solution)/shard_map/cond/branch_2_fun/ppermute | solution.py:394
  45.2 0.0 collective-permute-start.9
  45.2 1.2 %collective-permute-start.11 = (bf16[2,13,48,128]{3,2,1,0:T(8,128)(2,1)S(1)}, bf16[2,13,48,128]{3,2,1,0:T(8,128)(2,1)S(1)}, u32[]{:S(2)}, u32[]{:S(2)}) collective-permute-start(bf16[2,13,48,128]{3,2,1,0:T(8,128)(2,1)S(1)} %collective-permute-done.8.refs_4_), channel_id=1, source_target_pairs={{0,2},{1,3},{2,0},{3,1},{4,6},{5,7},{6,4},{7,5},{8,10},{9,11},{10,... | collective-permute-start | bytes 958472 | tf_op jit(solution)/shard_map/cond/branch_2_fun/ppermute | solution.py:394
  46.5 0.2 collective-permute-start.5
  46.7 0.0 collective-permute-done.6
  46.7 0.3 collective-permute-start.7
  47.1 0.0 collective-permute-start.10
  47.1 1.4 %collective-permute-done.5.refs_1_ = bf16[1,13,48,128]{3,2,1,0:T(8,128)(2,1)S(1)} collective-permute-done((bf16[1,13,48,128]{3,2,1,0:T(8,128)(2,1)S(1)}, bf16[1,13,48,128]{3,2,1,0:T(8,128)(2,1)S(1)}, u32[]{:S(2)}, u32[]{:S(2)}) %collective-permute-start.5) | collective-permute-done | bytes 159776 | tf_op jit(solution)/shard_map/cond/branch_2_fun/ppermute | solution.py:394
  48.4 0.2 collective-permute-done.7.refs_3_
  48.6 6.9 %sources.5.refs_1_ = bf16[52,256,192]{2,1,0:T(8,128)(2,1)S(1)} custom-call(bf16[1,13,48,128]{3,2,1,0:T(8,128)(2,1)S(1)} %get-tuple-element.143.refs_0_, bf16[1,13,48,128]{3,2,1,0:T(8,128)(2,1)S(1)} %collective-permute-done.5.refs_1_, bf16[1,13,48,128]{3,2,1,0:T(8,128)(2,1)S(1)} %get-tuple-element.147.refs_2_, ...), custom_call_target="tpu_custom_call" | custom-call | bytes 1048576 | tf_op jit(solution)/shard_map/cond/branch_2_fun/sources/pallas_call | solution.py:398
  55.6 0.0 collective-permute-done.11.refs_6_
  55.6 0.2 collective-permute-start.12
  55.8 0.9 %collective-permute-done.10.refs_5_ = bf16[2,13,48,128]{3,2,1,0:T(8,128)(2,1)S(1)} collective-permute-done((bf16[2,13,48,128]{3,2,1,0:T(8,128)(2,1)S(1)}, bf16[2,13,48,128]{3,2,1,0:T(8,128)(2,1)S(1)}, u32[]{:S(2)}, u32[]{:S(2)}) %collective-permute-start.10) | collective-permute-done | bytes 319520 | tf_op jit(solution)/shard_map/cond/branch_2_fun/ppermute | solution.py:394
  56.7 0.6 collective-permute-done.12.refs_8_
  57.3 1.2 %collective-permute-start.13 = (bf16[2,13,48,128]{3,2,1,0:T(8,128)(2,1)S(1)}, bf16[2,13,48,128]{3,2,1,0:T(8,128)(2,1)S(1)}, u32[]{:S(2)}, u32[]{:S(2)}) collective-permute-start(bf16[2,13,48,128]{3,2,1,0:T(8,128)(2,1)S(1)} %collective-permute-done.10.refs_5_), channel_id=1, source_target_pairs={{0,2},{1,3},{2,0},{3,1},{4,6},{5,7},{6,4},{7,5},{8,10},{9,11},{10,... | collective-permute-start | bytes 958472 | tf_op jit(solution)/shard_map/cond/branch_2_fun/ppermute | solution.py:394
  58.5 0.1 pad_maximum_fusion.11
  58.6 0.0 copy-start.2
  58.6 0.1 collective-permute-start.14
  58.7 0.0 collective-permute-done.9.refs_5_
  58.7 2.2 %receivers.5.refs_2_ = bf16[52,192,128]{2,1,0:T(8,128)(2,1)S(1)} custom-call(s32[1]{0:T(128)} %bitcast.8.refs_0_, bf16[2,13,48,128]{3,2,1,0:T(8,128)(2,1)S(1)} %get-tuple-element.90.refs_1_, bf16[2,13,48,128]{3,2,1,0:T(8,128)(2,1)S(1)} %slice.101.refs_2_, bf16[2,13,48,128]{3,2,1,0:T(8,128)(2,1)S(1)} %collective-permute-done.3.refs_3_, ...), custom_call_target="tpu_custom_call" | custom-call | bytes 1048576 | tf_op jit(solution)/shard_map/cond/branch_2_fun/receivers/pallas_call | solution.py:398
  60.9 6.0 %collective-permute-done.13.refs_7_ = bf16[2,13,48,128]{3,2,1,0:T(8,128)(2,1)S(1)} collective-permute-done((bf16[2,13,48,128]{3,2,1,0:T(8,128)(2,1)S(1)}, bf16[2,13,48,128]{3,2,1,0:T(8,128)(2,1)S(1)}, u32[]{:S(2)}, u32[]{:S(2)}) %collective-permute-start.13) | collective-permute-done | bytes 319520 | tf_op jit(solution)/shard_map/cond/branch_2_fun/ppermute | solution.py:394
  66.9 0.0 collective-permute-start.15
  66.9 0.0 collective-permute-done.14.refs_9_
  66.9 1.6 %collective-permute-done.15.refs_10_ = bf16[2,13,48,128]{3,2,1,0:T(8,128)(2,1)S(1)} collective-permute-done((bf16[2,13,48,128]{3,2,1,0:T(8,128)(2,1)S(1)}, bf16[2,13,48,128]{3,2,1,0:T(8,128)(2,1)S(1)}, u32[]{:S(2)}, u32[]{:S(2)}) %collective-permute-start.15) | collective-permute-done | bytes 319520 | tf_op jit(solution)/shard_map/cond/branch_2_fun/ppermute | solution.py:394
  68.5 0.0 copy-done.2
  68.5 7.8 %correlate.5 = bf16[2,101,32,128]{3,2,1,0:T(8,128)(2,1)S(1)} custom-call(s32[1]{0:T(128)} %bitcast.8.refs_0_, bf16[52,256,192]{2,1,0:T(8,128)(2,1)S(1)} %sources.5.refs_1_, bf16[52,192,128]{2,1,0:T(8,128)(2,1)S(1)} %receivers.5.refs_2_, bf16[104,416]{1,0:T(8,128)(2,1)S(1)} %copy-done.2, bf16[2,13,48,128]{3,2,1,0:T(8,128)(2,1)S(1)} %collective-permute-done.8.refs_4_, ...), custom_call_target="tpu_custom_call" | custom-call | bytes 1048576 | tf_op jit(solution)/shard_map/cond/branch_2_fun/correlate/pallas_call | solution.py:398
  76.6 0.0 copy-start.3
  76.6 1.2 %copy-done.3 = bf16[2,32,101,128]{3,1,2,0:T(8,128)(2,1)} copy-done((bf16[2,32,101,128]{3,1,2,0:T(8,128)(2,1)}, bf16[2,32,101,128]{3,1,2,0:T(8,128)(2,1)S(1)}, u32[]{:S(2)}) %copy-start.3) | copy-done | bytes 1654808
  (4 shorter events, 0.1 us)
Async XLA Ops:
  5.4 20.9 %collective-permute-start = (bf16[3,13,48,128]{3,2,1,0:T(8,128)(2,1)S(1)}, bf16[3,13,48,128]{3,2,1,0:T(8,128)(2,1)S(1)}, u32[]{:S(2)}, u32[]{:S(2)}) collective-permute-start(bf16[3,13,48,128]{3,2,1,0:T(8,128)(2,1)S(1)} %get-tuple-element.88), channel_id=1, source_target_pairs={{0,4},{4,0},{8,12},{12,8},{1,5},{5,1},{9,13},{13,9},{2,6},{6,2},{1... | collective-permute-start | bytes 1437704 | tf_op jit(solution)/shard_map/cond/branch_2_fun/ppermute | solution.py:394
  8.5 17.8 %collective-permute-start.3 = (bf16[2,13,48,128]{3,2,1,0:T(8,128)(2,1)S(1)}, bf16[2,13,48,128]{3,2,1,0:T(8,128)(2,1)S(1)}, u32[]{:S(2)}, u32[]{:S(2)}) collective-permute-start(bf16[2,13,48,128]{3,2,1,0:T(8,128)(2,1)S(1)} %get-tuple-element.90.refs_1_), channel_id=1, source_target_pairs={{0,2},{1,3},{2,0},{3,1},{4,6},{5,7},{6,4},{7,5},{8,10},{9,11},{10,... | collective-permute-start | bytes 958472 | tf_op jit(solution)/shard_map/cond/branch_2_fun/ppermute | solution.py:394
  9.9 18.1 %collective-permute-start.1 = (bf16[2,13,48,128]{3,2,1,0:T(8,128)(2,1)S(1)}, bf16[2,13,48,128]{3,2,1,0:T(8,128)(2,1)S(1)}, u32[]{:S(2)}, u32[]{:S(2)}) collective-permute-start(bf16[2,13,48,128]{3,2,1,0:T(8,128)(2,1)S(1)} %get-tuple-element.89), channel_id=1, source_target_pairs={{0,8},{4,12},{8,0},{12,4},{1,9},{5,13},{9,1},{13,5},{2,10},{6,14},... | collective-permute-start | bytes 958472 | tf_op jit(solution)/shard_map/cond/branch_2_fun/ppermute | solution.py:394
  26.3 9.7 %collective-permute-start.4 = (bf16[2,13,48,128]{3,2,1,0:T(8,128)(2,1)S(1)}, bf16[2,13,48,128]{3,2,1,0:T(8,128)(2,1)S(1)}, u32[]{:S(2)}, u32[]{:S(2)}) collective-permute-start(bf16[2,13,48,128]{3,2,1,0:T(8,128)(2,1)S(1)} %slice.101.refs_2_), channel_id=1, source_target_pairs={{0,2},{1,3},{2,0},{3,1},{4,6},{5,7},{6,4},{7,5},{8,10},{9,11},{10,... | collective-permute-start | bytes 958472 | tf_op jit(solution)/shard_map/cond/branch_2_fun/ppermute | solution.py:394
  28.0 8.0 %collective-permute-start.2 = (bf16[1,13,48,128]{3,2,1,0:T(8,128)(2,1)S(1)}, bf16[1,13,48,128]{3,2,1,0:T(8,128)(2,1)S(1)}, u32[]{:S(2)}, u32[]{:S(2)}) collective-permute-start(bf16[1,13,48,128]{3,2,1,0:T(8,128)(2,1)S(1)} %slice.100), channel_id=1, source_target_pairs={{0,4},{4,0},{8,12},{12,8},{1,5},{5,1},{9,13},{13,9},{2,6},{6,2},{1... | collective-permute-start | bytes 479240 | tf_op jit(solution)/shard_map/cond/branch_2_fun/ppermute | solution.py:394
  29.1 16.1 %collective-permute-start.8 = (bf16[2,13,48,128]{3,2,1,0:T(8,128)(2,1)S(1)}, bf16[2,13,48,128]{3,2,1,0:T(8,128)(2,1)S(1)}, u32[]{:S(2)}, u32[]{:S(2)}) collective-permute-start(bf16[2,13,48,128]{3,2,1,0:T(8,128)(2,1)S(1)} %get-tuple-element.95), channel_id=1, source_target_pairs={{0,8},{4,12},{8,0},{12,4},{1,9},{5,13},{9,1},{13,5},{2,10},{6,14},... | collective-permute-start | bytes 958472 | tf_op jit(solution)/shard_map/cond/branch_2_fun/ppermute | solution.py:394
  36.1 10.6 %collective-permute-start.6 = (bf16[2,13,48,128]{3,2,1,0:T(8,128)(2,1)S(1)}, bf16[2,13,48,128]{3,2,1,0:T(8,128)(2,1)S(1)}, u32[]{:S(2)}, u32[]{:S(2)}) collective-permute-start(bf16[2,13,48,128]{3,2,1,0:T(8,128)(2,1)S(1)} %pad_maximum_fusion.12), channel_id=1, source_target_pairs={{0,2},{1,3},{2,0},{3,1},{4,6},{5,7},{6,4},{7,5},{8,10},{9,11},{10,... | collective-permute-start | bytes 958472 | tf_op jit(solution)/shard_map/cond/branch_2_fun/ppermute | solution.py:394
  45.2 13.5 %collective-permute-start.9 = (bf16[8,13,48,128]{3,2,1,0:T(8,128)(2,1)S(1)}, bf16[8,13,48,128]{3,2,1,0:T(8,128)(2,1)S(1)}, u32[]{:S(2)}, u32[]{:S(2)}) collective-permute-start(bf16[8,13,48,128]{3,2,1,0:T(8,128)(2,1)S(1)} %pad_maximum_fusion.10), channel_id=1, source_target_pairs={{0,1},{1,0},{2,3},{3,2},{4,5},{5,4},{6,7},{7,6},{8,9},{9,8},{10,11... | collective-permute-start | bytes 3833864 | tf_op jit(solution)/shard_map/cond/branch_2_fun/ppermute | solution.py:394
  45.2 10.4 %collective-permute-start.11 = (bf16[2,13,48,128]{3,2,1,0:T(8,128)(2,1)S(1)}, bf16[2,13,48,128]{3,2,1,0:T(8,128)(2,1)S(1)}, u32[]{:S(2)}, u32[]{:S(2)}) collective-permute-start(bf16[2,13,48,128]{3,2,1,0:T(8,128)(2,1)S(1)} %collective-permute-done.8.refs_4_), channel_id=1, source_target_pairs={{0,2},{1,3},{2,0},{3,1},{4,6},{5,7},{6,4},{7,5},{8,10},{9,11},{10,... | collective-permute-start | bytes 958472 | tf_op jit(solution)/shard_map/cond/branch_2_fun/ppermute | solution.py:394
  46.5 2.0 %collective-permute-start.5 = (bf16[1,13,48,128]{3,2,1,0:T(8,128)(2,1)S(1)}, bf16[1,13,48,128]{3,2,1,0:T(8,128)(2,1)S(1)}, u32[]{:S(2)}, u32[]{:S(2)}) collective-permute-start(bf16[1,13,48,128]{3,2,1,0:T(8,128)(2,1)S(1)} %get-tuple-element.142), channel_id=1, source_target_pairs={{0,1},{1,0},{2,3},{3,2},{4,5},{5,4},{6,7},{7,6},{8,9},{9,8},{10,11... | collective-permute-start | bytes 479240 | tf_op jit(solution)/shard_map/cond/branch_2_fun/ppermute | solution.py:394
  46.7 1.9 %collective-permute-start.7 = (bf16[1,13,48,128]{3,2,1,0:T(8,128)(2,1)S(1)}, bf16[1,13,48,128]{3,2,1,0:T(8,128)(2,1)S(1)}, u32[]{:S(2)}, u32[]{:S(2)}) collective-permute-start(bf16[1,13,48,128]{3,2,1,0:T(8,128)(2,1)S(1)} %get-tuple-element.146), channel_id=1, source_target_pairs={{0,1},{1,0},{2,3},{3,2},{4,5},{5,4},{6,7},{7,6},{8,9},{9,8},{10,11... | collective-permute-start | bytes 479240 | tf_op jit(solution)/shard_map/cond/branch_2_fun/ppermute | solution.py:394
  47.1 9.7 %collective-permute-start.10 = (bf16[2,13,48,128]{3,2,1,0:T(8,128)(2,1)S(1)}, bf16[2,13,48,128]{3,2,1,0:T(8,128)(2,1)S(1)}, u32[]{:S(2)}, u32[]{:S(2)}) collective-permute-start(bf16[2,13,48,128]{3,2,1,0:T(8,128)(2,1)S(1)} %collective-permute-done.8.refs_4_), channel_id=1, source_target_pairs={{0,4},{4,0},{8,12},{12,8},{1,5},{5,1},{9,13},{13,9},{2,6},{6,2},{1... | collective-permute-start | bytes 958472 | tf_op jit(solution)/shard_map/cond/branch_2_fun/ppermute | solution.py:394
  55.6 1.7 %collective-permute-start.12 = (bf16[2,13,48,128]{3,2,1,0:T(8,128)(2,1)S(1)}, bf16[2,13,48,128]{3,2,1,0:T(8,128)(2,1)S(1)}, u32[]{:S(2)}, u32[]{:S(2)}) collective-permute-start(bf16[2,13,48,128]{3,2,1,0:T(8,128)(2,1)S(1)} %collective-permute-done.8.refs_4_), channel_id=1, source_target_pairs={{0,1},{1,0},{2,3},{3,2},{4,5},{5,4},{6,7},{7,6},{8,9},{9,8},{10,11... | collective-permute-start | bytes 958472 | tf_op jit(solution)/shard_map/cond/branch_2_fun/ppermute | solution.py:394
  57.3 9.6 %collective-permute-start.13 = (bf16[2,13,48,128]{3,2,1,0:T(8,128)(2,1)S(1)}, bf16[2,13,48,128]{3,2,1,0:T(8,128)(2,1)S(1)}, u32[]{:S(2)}, u32[]{:S(2)}) collective-permute-start(bf16[2,13,48,128]{3,2,1,0:T(8,128)(2,1)S(1)} %collective-permute-done.10.refs_5_), channel_id=1, source_target_pairs={{0,2},{1,3},{2,0},{3,1},{4,6},{5,7},{6,4},{7,5},{8,10},{9,11},{10,... | collective-permute-start | bytes 958472 | tf_op jit(solution)/shard_map/cond/branch_2_fun/ppermute | solution.py:394
  58.6 9.9 %copy-start.2 = (bf16[104,416]{1,0:T(8,128)(2,1)S(1)}, bf16[104,416]{1,0:T(8,128)(2,1)}, u32[]{:S(2)}) copy-start(bf16[104,416]{1,0:T(8,128)(2,1)} %constant.38.clone.3.refs_3_) | copy-start | bytes 259588 | tf_op jit(solution)/shard_map/cond
  58.6 8.3 %collective-permute-start.14 = (bf16[4,13,48,128]{3,2,1,0:T(8,128)(2,1)S(1)}, bf16[4,13,48,128]{3,2,1,0:T(8,128)(2,1)S(1)}, u32[]{:S(2)}, u32[]{:S(2)}) collective-permute-start(bf16[4,13,48,128]{3,2,1,0:T(8,128)(2,1)S(1)} %pad_maximum_fusion.11), channel_id=1, source_target_pairs={{0,1},{1,0},{2,3},{3,2},{4,5},{5,4},{6,7},{7,6},{8,9},{9,8},{10,11... | collective-permute-start | bytes 1916936 | tf_op jit(solution)/shard_map/cond/branch_2_fun/ppermute | solution.py:394
  66.9 1.6 %collective-permute-start.15 = (bf16[2,13,48,128]{3,2,1,0:T(8,128)(2,1)S(1)}, bf16[2,13,48,128]{3,2,1,0:T(8,128)(2,1)S(1)}, u32[]{:S(2)}, u32[]{:S(2)}) collective-permute-start(bf16[2,13,48,128]{3,2,1,0:T(8,128)(2,1)S(1)} %collective-permute-done.13.refs_7_), channel_id=1, source_target_pairs={{0,1},{1,0},{2,3},{3,2},{4,5},{5,4},{6,7},{7,6},{8,9},{9,8},{10,11... | collective-permute-start | bytes 958472 | tf_op jit(solution)/shard_map/cond/branch_2_fun/ppermute | solution.py:394
  76.6 1.2 %copy-start.3 = (bf16[2,32,101,128]{3,1,2,0:T(8,128)(2,1)}, bf16[2,32,101,128]{3,1,2,0:T(8,128)(2,1)S(1)}, u32[]{:S(2)}) copy-start(bf16[2,32,101,128]{3,1,2,0:T(8,128)(2,1)S(1)} %get-tuple-element.215) | copy-start | bytes 4964356
